TPU v7x, 256 devices: a whole 4x4x8 slice. The times are simulated.
256 devices in a mesh: gy: 16 (over y_lo, z), gx: 8 (over x, core), gz: 2 (over y_hi).
Axes of the slice: x: 4, y: 4 (y_hi: 2, y_lo: 2; y = y_hi * 2 + y_lo), z: 8, core: 2. Of those that a mesh axis runs over, the one named last changes fastest.
Arguments:
- fields: float32 [4, 128, 256, 256], P(None, 'gx', 'gy', 'gz'), may hold values from -0.3 to 0.3
- previous: float32 [3, 128, 256, 256], P(None, 'gx', 'gy', 'gz'), may hold values from -0.3 to 0.3
- cotangent: float32 [4, 128, 256, 256], P(None, 'gx', 'gy', 'gz'), may hold values from -0.3 to 0.3
Outputs:
- residual: float32 [4, 128, 256, 256], P(None, 'gx', 'gy', 'gz')
- adjoint: float32 [4, 128, 256, 256], P(None, 'gx', 'gy', 'gz')
All inputs are finite; a program needn't handle non-finite values.
Results may differ from a plain program's by a relative error of at most 0.000096.
Values sent between devices are 32-bit elements; how exact they have to be, the bound alone decides.
No kernel may reach another device: no remote copies, remote signals or barrier semaphores. Data moves between devices by JAX's collectives and lax.ppermute only.
A program may use at most 128 MiB of HBM per device.

v0:
```python
import math

import jax
import jax.numpy as jnp
from jax import lax
from jax.sharding import PartitionSpec as P

NU_VALUE = 0.001
STEP_DT = 0.1
SPACE_X = 8.0 * math.pi / 512.0
SPACE_Z = 3.0 * math.pi / 512.0
first_coeffs = (0.8, -0.2, 4.0 / 105.0, -1.0 / 280.0)
second_coeffs = (1.6, -0.2, 8.0 / 315.0, -1.0 / 560.0)
center_coeff = -205.0 / 72.0


def extended(shard, sides, width):
    for axis, dim in sides:
        peers, length = (lax.axis_size(axis), shard.shape[dim])
        up = [(i, (i + 1) % peers) for i in range(peers)]
        down = [(j, i) for i, j in up]
        last = lax.slice_in_dim(shard, length - width, length, axis=dim)
        leading = lax.slice_in_dim(shard, 0, width, axis=dim)
        before = lax.ppermute(last, axis, up)
        after = lax.ppermute(leading, axis, down)
        shard = jnp.concatenate([before, shard, after], axis=dim)
    return shard


def chebyshev_pair(points):
    final_row = points - 1
    positions = jnp.arange(points, dtype=jnp.int32)
    row_ids = positions[:, None].astype(jnp.float32)
    col_ids = positions[None, :].astype(jnp.float32)
    half_step = math.pi / (2.0 * final_row)
    spacing = (
        -2.0 * jnp.sin(half_step * (row_ids + col_ids)) * jnp.sin(half_step * (row_ids - col_ids))
    )
    ends = jnp.where((positions == 0) | (positions == final_row), 2.0, 1.0)
    signs = jnp.where(positions % 2 == 0, 1.0, -1.0)
    scaled = (ends * signs).astype(jnp.float32)
    diagonal = positions[:, None] == positions[None, :]
    entries = scaled[:, None] / scaled[None, :] / jnp.where(diagonal, 1.0, spacing)
    entries = jnp.where(diagonal, 0.0, entries)
    first_mat = entries - jnp.diag(jnp.sum(entries, axis=1))
    second_mat = jnp.dot(first_mat, first_mat, precision=lax.Precision.HIGHEST)
    return (first_mat, second_mat)


def wall_profile(positions, points):
    final_row = points - 1
    angles = positions.astype(jnp.float32) * (math.pi / final_row)
    weight = jnp.sin(angles) ** 4
    wall_rows = jnp.where((positions == 0) | (positions == final_row), 1.0, 0.0).astype(jnp.float32)
    return (weight, wall_rows)


def along_wall(matrix, field):
    return jnp.einsum("ij,cxjz->cxiz", matrix, field, precision=lax.Precision.HIGHEST)


def shifted(padded, axis_dim, offset, cells_x, cells_z):
    if axis_dim == 1:
        return padded[:, 4 + offset : 4 + offset + cells_x, :, 4 : 4 + cells_z]
    return padded[:, 4 : 4 + cells_x, :, 4 + offset : 4 + offset + cells_z]


def first_pad(padded, axis_dim, space, cells_x, cells_z):
    summed = 0.0
    for distance, factor in enumerate(first_coeffs):
        ahead = shifted(padded, axis_dim, distance + 1, cells_x, cells_z)
        behind = shifted(padded, axis_dim, -(distance + 1), cells_x, cells_z)
        summed = summed + factor * (ahead - behind)
    return summed / space


def second_pad(padded, axis_dim, space, cells_x, cells_z):
    summed = center_coeff * shifted(padded, axis_dim, 0, cells_x, cells_z)
    for distance, factor in enumerate(second_coeffs):
        ahead = shifted(padded, axis_dim, distance + 1, cells_x, cells_z)
        behind = shifted(padded, axis_dim, -(distance + 1), cells_x, cells_z)
        summed = summed + factor * (ahead + behind)
    return summed / (space * space)


def per_device(fields, previous, cotangent):
    cells_x, rows_y, cells_z = (fields.shape[1], fields.shape[2], fields.shape[3])
    groups = lax.axis_size("gy")
    points = rows_y * groups
    first_mat, second_mat = chebyshev_pair(points)
    offset = lax.axis_index("gy") * rows_y
    positions = offset + jnp.arange(rows_y, dtype=jnp.int32)
    weight, wall_rows = wall_profile(positions, points)
    weight_b = weight[None, None, :, None]
    wall_b = wall_rows[None, None, :, None]
    velocity = fields[0:3]
    weighted = weight_b * cotangent[0:3]
    mass_weighted = weight_b * cotangent[3:4]
    nothing = jnp.zeros_like(mass_weighted)
    carried = fields[1:2] * weighted + jnp.concatenate([nothing, mass_weighted, nothing], axis=0)
    packed = jnp.concatenate([fields, weighted, mass_weighted], axis=0)
    padded = extended(packed, (("gx", 1), ("gz", 3)), 4)
    first_rows = lax.dynamic_slice_in_dim(first_mat, offset, rows_y, 0)
    second_rows = lax.dynamic_slice_in_dim(second_mat, offset, rows_y, 0)
    block_piece = lax.all_gather(fields, "gy", axis=2, tiled=True)
    part_one = first_rows
    part_two = second_rows
    slope_y = along_wall(part_one, block_piece)
    curve_y = along_wall(part_two, block_piece[0:3])
    lifted_source = jnp.concatenate([carried, weighted[1:2]], axis=0)
    part_one = first_rows
    part_two = second_rows
    lifted = jnp.einsum("ij,cxiz->jcxz", part_one, lifted_source, precision=lax.Precision.HIGHEST)
    bent = jnp.einsum("ij,cxiz->jcxz", part_two, weighted, precision=lax.Precision.HIGHEST)
    summed_rows = lax.psum_scatter(
        jnp.concatenate([lifted[:, 0:3] - NU_VALUE * bent, lifted[:, 3:4]], axis=1),
        "gy",
        scatter_dimension=0,
        tiled=True,
    )
    back_y = jnp.transpose(summed_rows, (1, 2, 0, 3))
    slope_x = first_pad(padded[0:4], 1, SPACE_X, cells_x, cells_z)
    slope_z = first_pad(padded[0:4], 3, SPACE_Z, cells_x, cells_z)
    curve = (
        second_pad(padded[0:3], 1, SPACE_X, cells_x, cells_z)
        + curve_y
        + second_pad(padded[0:3], 3, SPACE_Z, cells_x, cells_z)
    )
    pressure_grad = jnp.stack([slope_x[3], slope_y[3], slope_z[3]])
    transport = fields[0:1] * slope_x[0:3] + fields[1:2] * slope_y[0:3] + fields[2:3] * slope_z[0:3]
    momentum = (velocity - previous) / STEP_DT + transport + pressure_grad - NU_VALUE * curve
    balance = weight_b * momentum + wall_b * velocity
    continuity = weight_b[0] * (slope_x[0] + slope_y[1] + slope_z[2])
    residual = jnp.concatenate([balance, continuity[None]], axis=0)
    flux_x = padded[0:1] * padded[4:7]
    flux_z = padded[2:3] * padded[4:7]
    stretch = jnp.stack(
        [
            jnp.sum(weighted * slope_x[0:3], axis=0),
            jnp.sum(weighted * slope_y[0:3], axis=0),
            jnp.sum(weighted * slope_z[0:3], axis=0),
        ]
    )
    viscous = second_pad(padded[4:7], 1, SPACE_X, cells_x, cells_z) + second_pad(
        padded[4:7], 3, SPACE_Z, cells_x, cells_z
    )
    mass_x = -first_pad(padded[7:8], 1, SPACE_X, cells_x, cells_z)
    mass_z = -first_pad(padded[7:8], 3, SPACE_Z, cells_x, cells_z)
    adjoint_vel = weighted / STEP_DT + stretch
    adjoint_vel = (
        adjoint_vel
        - first_pad(flux_x, 1, SPACE_X, cells_x, cells_z)
        - first_pad(flux_z, 3, SPACE_Z, cells_x, cells_z)
    )
    adjoint_vel = adjoint_vel + back_y[0:3] - NU_VALUE * viscous
    adjoint_vel = (
        adjoint_vel
        + jnp.concatenate([mass_x, jnp.zeros_like(mass_x), mass_z], axis=0)
        + wall_b * cotangent[0:3]
    )
    adjoint_press = (
        -first_pad(padded[4:5], 1, SPACE_X, cells_x, cells_z)
        + back_y[3:4]
        - first_pad(padded[6:7], 3, SPACE_Z, cells_x, cells_z)
    )
    adjoint = jnp.concatenate([adjoint_vel, adjoint_press], axis=0)
    return (residual, adjoint)


def solution(mesh):
    return jax.shard_map(
        per_device,
        mesh=mesh,
        in_specs=(P(None, "gx", "gy", "gz"), P(None, "gx", "gy", "gz"), P(None, "gx", "gy", "gz")),
        out_specs=(P(None, "gx", "gy", "gz"), P(None, "gx", "gy", "gz")),
        check_vma=False,
    )
```

profile of v0, /device:TPU:1, one launch (start us, length us, event | category | flops | bytes accessed | tf_op | source)
XLA Modules:
  0.0 235.5 jit_solution(7663847899523146683)
XLA Ops:
  8.0 1.0 slice_multiply_fusion.1
  9.0 1.8 slice_bitcast_fusion.2
  11.0 2.1 fusion.140
  13.1 1.9 select_subtract_fusion
  15.7 6.7 %fusion.39 = f32[256,4,16,128]{3,0,2,1:T(8,128)S(1)} fusion(f32[1,16,16,128]{3,2,1,0:T(8,128)S(1)} %slice.783, f32[3,16,16,128]{3,2,1,0:T(8,128)S(1)} %get-tuple-element.7, f32[256,256]{1,0:T(8,128)S(1)} %select_subtract_fusion, s32[]{:T(128)S(6)} %select_n.78), kind=kOutput, calls=%fused_computation.45 | convolution fusion | flops 402784256 | bytes 8929284 | tf_op jit(solution)/shard_map/ij,cxiz->jcxz/dot_general | solution.py:113
  22.6 4.3 %fusion.141 = f32[256,256]{1,0:T(8,128)S(1)} fusion(f32[256]{0:T(256)S(1)} %fusion.140, f32[256]{0:T(256)S(1)} %iota_convert_fusion, f32[256]{0:T(256)S(1)} %fusion.152), kind=kOutput, calls=%fused_computation.216 | convolution fusion | flops 202178560 | bytes 265216 | tf_op jit(solution)/shard_map/dot_general | solution.py:46
  26.9 5.7 %slice_subtract_fusion = f32[256,3,16,128]{3,0,2,1:T(8,128)S(1)} fusion(f32[256,4,16,128]{3,0,2,1:T(8,128)S(1)} %fusion.39, f32[3,16,16,128]{3,2,1,0:T(8,128)S(1)} %get-tuple-element.8, f32[256,256]{1,0:T(8,128)S(1)} %fusion.141, s32[]{:T(128)S(6)} %select_n.78), kind=kOutput, calls=%fused_computation.1 | convolution fusion | flops 305135616 | bytes 12992516 | tf_op jit(solution)/shard_map/ij,cxiz->jcxz/dot_general | solution.py:114
  32.5 3.9 %pad_maximum_fusion = f32[256,4,16,128]{3,0,2,1:T(8,128)} fusion(f32[256,1,16,128]{3,0,2,1:T(8,128)S(1)} %slice.785, f32[256,3,16,128]{3,0,2,1:T(8,128)S(1)} %slice_subtract_fusion), kind=kLoop, calls=%fused_computation | loop fusion | flops 2097152 | bytes 16777216 | tf_op jit(solution)/shard_map/concatenate | solution.py:116
  36.5 1.0 copy-done
  37.6 3.3 %collective-permute-start = (f32[8,4,16,128]{3,2,1,0:T(8,128)S(1)}, f32[8,4,16,128]{3,2,1,0:T(8,128)S(1)}, u32[]{:S(2)}, u32[]{:S(2)}) collective-permute-start(f32[8,4,16,128]{3,2,1,0:T(8,128)S(1)} %get-tuple-element.18), channel_id=1, source_target_pairs={{2,0},{4,2},{6,4},{8,6},{10,8},{12,10},{14,12},{0,14},{3,1},{5,3},... | collective-permute-start | bytes 786440 | tf_op jit(solution)/shard_map/ppermute | solution.py:25
  40.8 3.8 %collective-permute-done = f32[8,4,16,128]{3,2,1,0:T(8,128)S(1)} collective-permute-done((f32[8,4,16,128]{3,2,1,0:T(8,128)S(1)}, f32[8,4,16,128]{3,2,1,0:T(8,128)S(1)}, u32[]{:S(2)}, u32[]{:S(2)}) %collective-permute-start) | collective-permute-done | bytes 262176 | tf_op jit(solution)/shard_map/ppermute | solution.py:25
  44.8 1.7 fusion.162
  46.5 3.0 %copy.5 = f32[8,24,16,4]{1,2,3,0:T(8,128)} copy(f32[8,24,16,4]{3,2,1,0:T(8,128)} %get-tuple-element.13) | data formatting | bytes 98304 | tf_op jit(solution)/shard_map/slice | solution.py:23
  49.6 2.9 %collective-permute-start.2 = (f32[8,24,16,4]{1,2,3,0:T(8,128)}, f32[8,24,16,4]{1,2,3,0:T(8,128)}, u32[]{:S(2)}, u32[]{:S(2)}) collective-permute-start(f32[8,24,16,4]{1,2,3,0:T(8,128)} %copy.5), channel_id=1, source_target_pairs={{1,0},{0,1},{3,2},{2,3},{5,4},{4,5},{7,6},{6,7},{9,8},{8,9},{11,10... | collective-permute-start | bytes 147464 | tf_op jit(solution)/shard_map/ppermute | solution.py:25
  52.5 1.6 copy.7
  54.5 1.0 copy-done.3
  56.0 65.1 %collective-permute-done.2 = f32[8,24,16,4]{1,2,3,0:T(8,128)} collective-permute-done((f32[8,24,16,4]{1,2,3,0:T(8,128)}, f32[8,24,16,4]{1,2,3,0:T(8,128)}, u32[]{:S(2)}, u32[]{:S(2)}) %collective-permute-start.2) | collective-permute-done | bytes 49184 | tf_op jit(solution)/shard_map/ppermute | solution.py:25
  121.1 1.8 copy.6
  122.9 3.8 %collective-permute-done.3 = f32[8,24,16,4]{1,2,3,0:T(8,128)} collective-permute-done((f32[8,24,16,4]{1,2,3,0:T(8,128)}, f32[8,24,16,4]{1,2,3,0:T(8,128)}, u32[]{:S(2)}, u32[]{:S(2)}) %collective-permute-start.3) | collective-permute-done | bytes 49184 | tf_op jit(solution)/shard_map/ppermute | solution.py:24
  126.7 2.9 %copy.8 = f32[8,24,16,4]{3,2,1,0:T(8,128)} copy(f32[8,24,16,4]{1,2,3,0:T(8,128)} %collective-permute-done.3) | data formatting | bytes 98304 | tf_op jit(solution)/shard_map/ppermute | solution.py:24
  129.7 2.4 %fusion.124 = f32[1,16,16,128]{3,2,1,0:T(8,128)} fusion(f32[8,24,16,4]{3,2,1,0:T(8,128)} %copy.8, f32[8,4,16,128]{3,2,1,0:T(8,128)S(1)} %collective-permute-done, f32[8,4,16,128]{3,2,1,0:T(8,128)S(1)} %collective-permute-done.1, f32[1,16,16,128]{3,2,1,0:T(8,128)S(1)} %slice_multiply_fusion.1, f32[3,16,16,128]{3,2,1,0:T(8,128)S(1)} %get-tuple-element.8, ...), kind=kLoop, calls=%fused_computation.186 | loop fusion | flops 1736704 | bytes 1802240 | tf_op jit(solution)/shard_map/neg | solution.py:148
  132.5 1.6 broadcast_multiply_fusion.1
  134.0 1.2 broadcast_multiply_fusion
  135.3 2.0 pad_maximum_fusion.1
  137.3 1.6 copy-done.8
  139.9 2.0 fusion.25
  141.9 6.6 %convolution_bitcast_fusion = f32[4,16,16,128]{3,2,1,0:T(8,128)S(1)} fusion(f32[4,16,256,128]{3,2,1,0:T(8,128)} %all-gather.2.cloned.1.call-done, f32[256,256]{1,0:T(8,128)} %copy-done.17, s32[]{:T(128)S(6)} %select_n.78), kind=kOutput, calls=%fused_computation.9 | convolution fusion | flops 402653184 | bytes 8929284 | tf_op jit(solution)/shard_map/ij,cxjz->cxiz/dot_general | solution.py:59
  148.5 1.1 fusion.163
  149.8 6.1 %fusion.20 = f32[3,16,16,128]{3,2,1,0:T(8,128)S(1)} fusion(f32[4,16,256,128]{3,2,1,0:T(8,128)S(1)} %copy-done.7, f32[8,24,16,132]{3,2,1,0:T(8,128)} %copy-done.9, f32[8,24,16,132]{3,2,1,0:T(8,128)} %copy-done.8, f32[8,20,16,128]{3,2,1,0:T(8,128)} %copy-done.5, f32[8,20,16,128]{3,2,1,0:T(8,128)} %copy-done.3, f32[1,16,16,128]{3,2,1,0:T(8,128)S(1)} %get-tuple-element.25, ...), kind=kOutput, calls=%fused_computation.16 | convolution fusion | flops 306413568 | bytes 15746052 | tf_op jit(solution)/shard_map/ij,cxjz->cxiz/dot_general | solution.py:59
  157.6 58.5 %reduce-scatter.2.cloned.1.call-done = f32[16,4,16,128]{3,0,2,1:T(8,128)} async-done(((f32[256,4,16,128]{3,0,2,1:T(8,128)}), f32[16,4,16,128]{3,0,2,1:T(8,128)}) %reduce-scatter.2.cloned.1.call-update) | async-done | bytes 524304 | tf_op jit(solution)/shard_map/reduce_scatter | solution.py:115
  216.1 9.7 %fusion.50 = f32[3,16,16,128]{3,2,1,0:T(8,128)S(1)} fusion(f32[8,24,16,132]{3,2,1,0:T(8,128)} %copy-done.9, f32[8,24,16,132]{3,2,1,0:T(8,128)} %copy-done.8, f32[8,20,16,128]{3,2,1,0:T(8,128)} %copy-done.5, f32[8,20,16,128]{3,2,1,0:T(8,128)} %copy-done.3, f32[4,16,16,128]{3,2,1,0:T(8,128)} %bitcast.49, f32[3,24,16,136]{3,2,1,0:T(8,128)} %broadcast_multiply_fusion, ...), kind=kLoop, calls=%fused_computation.58 | loop fusion | flops 6488064 | bytes 14942272 | tf_op jit(solution)/shard_map/add | solution.py:157
  225.9 1.9 fusion.106
  (59 shorter events, 7.0 us)
Async XLA Ops:
  7.2 3.6 %copy-start.12 = (f32[4,16,16,128]{3,2,1,0:T(8,128)S(1)}, f32[4,16,16,128]{3,2,1,0:T(8,128)}, u32[]{:S(2)}) copy-start(f32[4,16,16,128]{3,2,1,0:T(8,128)} %param.5) | copy-start | bytes 1572868
  7.2 134.7 %all-gather.2.cloned.1.call-start = ((), (), s32[]{:S(2)}) async-start(), calls=%async_computation.1 | async-start | bytes 8912896 | tf_op jit(solution)/shard_map/all_gather | solution.py:105
  7.9 208.2 %reduce-scatter.2.cloned.1.call-start = ((), (), s32[]{:S(2)}) async-start(), calls=%async_computation.2 | async-start | bytes 8912896 | tf_op jit(solution)/shard_map/reduce_scatter | solution.py:115
  15.0 0.7 copy-start.17
  26.8 5.7 %copy-start.18 = (f32[256,256]{1,0:T(8,128)}, f32[256,256]{1,0:T(8,128)S(1)}, u32[]{:S(2)}) copy-start(f32[256,256]{1,0:T(8,128)S(1)} %fusion.141) | copy-start | bytes 786436
  36.5 1.0 copy-start
  37.6 7.1 %collective-permute-start = (f32[8,4,16,128]{3,2,1,0:T(8,128)S(1)}, f32[8,4,16,128]{3,2,1,0:T(8,128)S(1)}, u32[]{:S(2)}, u32[]{:S(2)}) collective-permute-start(f32[8,4,16,128]{3,2,1,0:T(8,128)S(1)} %get-tuple-element.18), channel_id=1, source_target_pairs={{2,0},{4,2},{6,4},{8,6},{10,8},{12,10},{14,12},{0,14},{3,1},{5,3},... | collective-permute-start | bytes 786440 | tf_op jit(solution)/shard_map/ppermute | solution.py:25
  40.8 3.8 %collective-permute-start.1 = (f32[8,4,16,128]{3,2,1,0:T(8,128)S(1)}, f32[8,4,16,128]{3,2,1,0:T(8,128)S(1)}, u32[]{:S(2)}, u32[]{:S(2)}) collective-permute-start(f32[8,4,16,128]{3,2,1,0:T(8,128)S(1)} %get-tuple-element.17), channel_id=1, source_target_pairs={{0,2},{2,4},{4,6},{6,8},{8,10},{10,12},{12,14},{14,0},{1,3},{3,5},... | collective-permute-start | bytes 786440 | tf_op jit(solution)/shard_map/ppermute | solution.py:24
  49.6 71.6 %collective-permute-start.2 = (f32[8,24,16,4]{1,2,3,0:T(8,128)}, f32[8,24,16,4]{1,2,3,0:T(8,128)}, u32[]{:S(2)}, u32[]{:S(2)}) collective-permute-start(f32[8,24,16,4]{1,2,3,0:T(8,128)} %copy.5), channel_id=1, source_target_pairs={{1,0},{0,1},{3,2},{2,3},{5,4},{4,5},{7,6},{6,7},{9,8},{8,9},{11,10... | collective-permute-start | bytes 147464 | tf_op jit(solution)/shard_map/ppermute | solution.py:25
  54.1 72.7 %collective-permute-start.3 = (f32[8,24,16,4]{1,2,3,0:T(8,128)}, f32[8,24,16,4]{1,2,3,0:T(8,128)}, u32[]{:S(2)}, u32[]{:S(2)}) collective-permute-start(f32[8,24,16,4]{1,2,3,0:T(8,128)} %copy.7), channel_id=1, source_target_pairs={{0,1},{1,0},{2,3},{3,2},{4,5},{5,4},{6,7},{7,6},{8,9},{9,8},{10,11... | collective-permute-start | bytes 147464 | tf_op jit(solution)/shard_map/ppermute | solution.py:24
  54.4 1.1 copy-start.3
  54.4 1.6 copy-start.5
  129.7 2.4 %copy-start.1 = (f32[8,24,16,4]{3,2,1,0:T(8,128)S(1)}, f32[8,24,16,4]{3,2,1,0:T(8,128)}, u32[]{:S(2)}) copy-start(f32[8,24,16,4]{3,2,1,0:T(8,128)} %copy.8) | copy-start | bytes 147460
  135.2 4.7 %copy-start.4 = (f32[8,20,16,128]{3,2,1,0:T(8,128)S(1)}, f32[8,20,16,128]{3,2,1,0:T(8,128)}, u32[]{:S(2)}) copy-start(f32[8,20,16,128]{3,2,1,0:T(8,128)} %copy-done.3) | copy-start | bytes 3932164
  135.3 4.7 %copy-start.6 = (f32[8,20,16,128]{3,2,1,0:T(8,128)S(1)}, f32[8,20,16,128]{3,2,1,0:T(8,128)}, u32[]{:S(2)}) copy-start(f32[8,20,16,128]{3,2,1,0:T(8,128)} %copy-done.5) | copy-start | bytes 3932164
  137.3 1.7 copy-start.8
  137.3 2.6 %copy-start.9 = (f32[8,24,16,132]{3,2,1,0:T(8,128)}, f32[8,24,16,132]{3,2,1,0:T(8,128)S(1)}, u32[]{:S(2)}) copy-start(f32[8,24,16,132]{3,2,1,0:T(8,128)S(1)} %get-tuple-element.12) | copy-start | bytes 4866052
  141.9 6.6 %copy-start.10 = (f32[4,16,16,128]{3,2,1,0:T(8,128)S(1)}, f32[4,16,16,128]{3,2,1,0:T(8,128)}, u32[]{:S(2)}) copy-start(f32[4,16,16,128]{3,2,1,0:T(8,128)} %get-tuple-element.26) | copy-start | bytes 1572868
  141.9 7.8 %copy-start.7 = (f32[4,16,256,128]{3,2,1,0:T(8,128)S(1)}, f32[4,16,256,128]{3,2,1,0:T(8,128)}, u32[]{:S(2)}) copy-start(f32[4,16,256,128]{3,2,1,0:T(8,128)} %all-gather.2.cloned.1.call-done) | copy-start | bytes 25165828
  141.9 7.8 %copy-start.14 = (f32[16,16,128]{2,1,0:T(8,128)S(1)}, f32[16,16,128]{2,1,0:T(8,128)}, u32[]{:S(2)}) copy-start(f32[16,16,128]{2,1,0:T(8,128)} %get-tuple-element.19) | copy-start | bytes 393220
  141.9 7.8 %copy-start.15 = (f32[16,16,128]{2,1,0:T(8,128)S(1)}, f32[16,16,128]{2,1,0:T(8,128)}, u32[]{:S(2)}) copy-start(f32[16,16,128]{2,1,0:T(8,128)} %get-tuple-element.21) | copy-start | bytes 393220
  148.5 1.2 copy-start.11
  148.5 1.3 copy-start.16
  155.9 60.2 %copy-start.13 = (f32[1,16,16,128]{3,2,1,0:T(8,128)S(1)}, f32[1,16,16,128]{3,2,1,0:T(8,128)}, u32[]{:S(2)}) copy-start(f32[1,16,16,128]{3,2,1,0:T(8,128)} %fusion.124) | copy-start | bytes 393220
  216.1 9.8 %copy-start.2 = (f32[8,24,16,4]{3,2,1,0:T(8,128)S(1)}, f32[8,24,16,4]{3,2,1,0:T(8,128)}, u32[]{:S(2)}) copy-start(f32[8,24,16,4]{3,2,1,0:T(8,128)} %copy.8) | copy-start | bytes 147460
Sparse Core Ops, SparseCore 0:
  9.8 104.8 all-gather.1
  117.2 98.8 reduce-scatter.1
where the time goes:
time: 236 us
  waiting for transfers between devices  132 us (56%)
  other arithmetic  34.5 us (15%)
  matrix products  29.3 us (12%)
  local copies, waits for them, and re-layouts  19 us (8%)
  between operations  14.4 us (6%)
  starting transfers between devices  6.31 us (3%)
    ppermute x2, waiting for transfers between devices, extended(): after = lax.ppermute(leading, axis, down)  68.9 us
    reduce_scatter x1, waiting for transfers between devices, per_device(): lax.psum_scatter(jnp.concatenate([lifted[:, 0:3] - NU_VALUE * bent, lifte...  58.5 us
    dot_general x2, matrix products, along_wall(): jnp.einsum('ij,cxjz->cxiz', matrix, field, precision=lax.Precision.HIGHEST)  12.7 us
    add x1, other arithmetic, per_device(): adjoint_vel + jnp.concatenate([mass_x, jnp.zeros_like(mass_x), mass_z], a...  9.74 us
    dot_general x1, matrix products, per_device(): jnp.einsum('ij,cxiz->jcxz', part_one, lifted_source, precision=lax.Precis...  6.73 us
    ppermute x2, starting transfers between devices, extended(): after = lax.ppermute(leading, axis, down)  6.18 us
    unnamed x38, local copies, waits for them, and re-layouts  6.02 us
    dot_general x1, matrix products, per_device(): jnp.einsum('ij,cxiz->jcxz', part_two, weighted, precision=lax.Precision.H...  5.67 us
  transfers between devices with their start and end apart: 6, of which 4 were waited for; matrix products, arithmetic and copies ran while one was open for 27% of the time, Pallas kernels for 0%

commit v1 on v0

v1 whole, which is shorter than its diff:
```python
import functools
import math

import jax
import jax.numpy as jnp
import numpy as np
from jax import lax
from jax.experimental import pallas as pl
from jax.experimental.pallas import tpu as pltpu
from jax.sharding import PartitionSpec as P

NU_VALUE = 0.001
STEP_DT = 0.1
SPACE_X = 8.0 * math.pi / 512.0
SPACE_Z = 3.0 * math.pi / 512.0
first_coeffs = (0.8, -0.2, 4.0 / 105.0, -1.0 / 280.0)
second_coeffs = (1.6, -0.2, 8.0 / 315.0, -1.0 / 560.0)
center_coeff = -205.0 / 72.0
VMEM_BYTES = 48 * 1024 * 1024
EXACT = lax.Precision.HIGHEST
f32 = jnp.float32


def wall_matrices(points):
    final_row = points - 1
    j = np.arange(points)
    half = math.pi / (2.0 * final_row)
    spacing = -2.0 * np.sin(half * (j[:, None] + j[None, :])) * np.sin(half * (j[:, None] - j[None, :]))
    ends = np.where((j == 0) | (j == final_row), 2.0, 1.0) * np.where(j % 2 == 0, 1.0, -1.0)
    eye = np.eye(points, dtype=bool)
    entries = np.where(eye, 0.0, ends[:, None] / ends[None, :] / np.where(eye, 1.0, spacing))
    first = entries - np.diag(entries.sum(axis=1))
    second = first @ first
    return first.astype(np.float32), second.astype(np.float32)


def wall_profile(points):
    final_row = points - 1
    j = np.arange(points)
    weight = np.sin(j * (math.pi / final_row)) ** 4
    wall = np.where((j == 0) | (j == final_row), 1.0, 0.0)
    return (
        np.repeat(weight[:, None], 128, 1).astype(np.float32),
        np.repeat(wall[:, None], 128, 1).astype(np.float32),
    )


def call(kernel, outs, args, flops, scratch=()):
    moved = sum(4 * math.prod(a.shape) for a in (*outs, *args))
    return pl.pallas_call(
        kernel,
        out_shape=outs,
        scratch_shapes=list(scratch),
        cost_estimate=pl.CostEstimate(flops=flops, bytes_accessed=moved, transcendentals=0),
        compiler_params=pltpu.CompilerParams(vmem_limit_bytes=VMEM_BYTES),
    )(*args)


def like(*shape):
    return jax.ShapeDtypeStruct(shape, f32)


def swap_kernel(a_ref, out_ref):
    for c in range(a_ref.shape[0]):
        out_ref[:, c] = a_ref[c]


def faces_kernel(fields_ref, cot_ref, cot_out, last_out, lead_out, zed_out):
    comps, cells = cot_ref.shape[0:2]
    for c in range(comps):
        cot_out[:, c] = cot_ref[c]
        last_out[c] = fields_ref[c, cells - 4 : cells]
        last_out[comps + c] = cot_ref[c, cells - 4 : cells]
        lead_out[c] = fields_ref[c, 0:4]
        lead_out[comps + c] = cot_ref[c, 0:4]

    def plane(x, _):
        lane = lax.broadcasted_iota(jnp.int32, zed_out.shape[1:], 1)
        total = jnp.zeros(zed_out.shape[1:], f32)
        for c in range(2 * comps):
            value = fields_ref[c, x] if c < comps else cot_ref[c - comps, x]
            moved = pltpu.roll(value, 4 + 8 * c, 1)
            total = jnp.where((lane >= 8 * c) & (lane < 8 * c + 8), moved, total)
        zed_out[x] = total
        return 0

    lax.fori_loop(0, cells, plane, 0)


def stencils(values, space, need_first, need_second):
    first = second = None
    if need_first:
        for k in range(4):
            term = (first_coeffs[k] / space) * (values[5 + k] - values[3 - k])
            first = term if first is None else first + term
    if need_second:
        second = (center_coeff / (space * space)) * values[4]
        for k in range(4):
            second = second + (second_coeffs[k] / (space * space)) * (values[5 + k] + values[3 - k])
    return first, second


def local_kernel(
    fields_ref, prev_ref, cot_ref, before_ref, after_ref, zed_ref, weight_ref, wall_ref, at_ref,
    res_ref, adj_ref, ext,
):
    cells, rows, lanes = fields_ref.shape[1:]
    here = pl.ds(pl.multiple_of(at_ref[0] * rows, rows), rows)
    weight = weight_ref[here]
    wall = wall_ref[here]

    for c in range(4):
        ext[c, 0:4] = before_ref[c]
        ext[c, 4 : 4 + cells] = fields_ref[c]
        ext[c, 4 + cells :] = after_ref[c]
    for c in range(4):
        for x in range(cells + 8):
            if x < 4:
                value = before_ref[4 + c, x]
            elif x < 4 + cells:
                value = cot_ref[c, x - 4]
            else:
                value = after_ref[4 + c, x - 4 - cells]
            value = weight * value
            ext[4 + c, x] = value
            if c < 3:
                ext[8 + c, x] = ext[0, x] * value

    def plane(x, _):
        lane = lax.broadcasted_iota(jnp.int32, (rows, lanes), 1)
        packed = zed_ref[x]
        own = [ext[c, 4 + x] for c in range(8)]
        far = [pltpu.roll(packed, (lanes - 4 - 8 * c) % lanes, 1) for c in range(8)]
        for c in range(4, 8):
            far[c] = weight * far[c]
        for c in range(3):
            own.append(own[2] * own[4 + c])
            far.append(far[2] * far[4 + c])

        def along_x(c, need_first, need_second):
            return stencils([ext[c, x + k] for k in range(9)], SPACE_X, need_first, need_second)

        def along_z(c, need_first, need_second):
            values = [None] * 9
            values[4] = own[c]
            for k in range(1, 5):
                values[4 + k] = pltpu.roll(jnp.where(lane < k, far[c], own[c]), lanes - k, 1)
                values[4 - k] = pltpu.roll(jnp.where(lane >= lanes - k, far[c], own[c]), k, 1)
            return stencils(values, SPACE_Z, need_first, need_second)

        u = own[0:4]
        w = own[4:8]
        dx, dz, curve = [], [], []
        for c in range(4):
            fx, sx = along_x(c, True, c < 3)
            fz, sz = along_z(c, True, c < 3)
            dx.append(fx)
            dz.append(fz)
            curve.append(sx + sz if c < 3 else None)
        for c in range(3):
            moment = (u[c] - prev_ref[c, x]) * (1.0 / STEP_DT) + u[0] * dx[c] + u[2] * dz[c] - NU_VALUE * curve[c]
            if c == 0:
                moment = moment + dx[3]
            if c == 2:
                moment = moment + dz[3]
            res_ref[c, x] = weight * moment + wall * u[c]
        res_ref[3, x] = weight * (dx[0] + dz[2])

        wx = [along_x(4 + c, c in (0, 3), c < 3) for c in range(4)]
        wz = [along_z(4 + c, c in (2, 3), c < 3) for c in range(4)]
        for c in range(3):
            flux = along_x(8 + c, True, False)[0] + along_z(8 + c, True, False)[0]
            total = w[c] * (1.0 / STEP_DT) - flux - NU_VALUE * (wx[c][1] + wz[c][1]) + wall * cot_ref[c, x]
            if c == 0:
                total = total + (w[0] * dx[0] + w[1] * dx[1] + w[2] * dx[2]) - wx[3][0]
            if c == 2:
                total = total + (w[0] * dz[0] + w[1] * dz[1] + w[2] * dz[2]) - wz[3][0]
            adj_ref[c, x] = total
        adj_ref[3, x] = -(wx[0][0] + wz[2][0])
        return 0

    lax.fori_loop(0, cells, plane, 0)


def lines(ref, c):
    groups, _, rows, lanes = ref.shape
    return ref[:, c].reshape(groups * rows, lanes)


def blocks(value, groups):
    return value.reshape(groups, value.shape[0] // groups, value.shape[1])


def res_lines_kernel(first_ref, second_ref, weight_ref, f_ref, out_ref, slope_ref):
    groups = f_ref.shape[0]
    weight = weight_ref[...]
    u = [lines(f_ref, c) for c in range(4)]
    for c in range(3):
        slope = jnp.dot(first_ref[...], u[c], precision=EXACT, preferred_element_type=f32)
        curve = jnp.dot(second_ref[...], u[c], precision=EXACT, preferred_element_type=f32)
        slope_ref[c] = slope
        total = u[1] * slope - NU_VALUE * curve
        if c == 1:
            total = total + jnp.dot(first_ref[...], u[3], precision=EXACT, preferred_element_type=f32)
            out_ref[:, 3] = blocks(weight * slope, groups)
        out_ref[:, c] = blocks(weight * total, groups)


def adj_lines_kernel(first_t_ref, second_t_ref, weight_ref, f_ref, c_ref, slope_ref, out_ref):
    groups = f_ref.shape[0]
    weight = weight_ref[...]
    u2 = lines(f_ref, 1)
    w = [weight * lines(c_ref, c) for c in range(4)]
    for c in range(3):
        carried = u2 * w[c]
        if c == 1:
            carried = carried + w[3]
        total = jnp.dot(first_t_ref[...], carried, precision=EXACT, preferred_element_type=f32)
        total = total - NU_VALUE * jnp.dot(second_t_ref[...], w[c], precision=EXACT, preferred_element_type=f32)
        if c == 1:
            total = total + w[0] * slope_ref[0] + w[1] * slope_ref[1] + w[2] * slope_ref[2]
        out_ref[:, c] = blocks(total, groups)
    press = jnp.dot(first_t_ref[...], w[1], precision=EXACT, preferred_element_type=f32)
    out_ref[:, 3] = blocks(press, groups)


def add_kernel(a_ref, b_ref, out_ref):
    for c in range(a_ref.shape[0]):
        out_ref[c] = a_ref[c] + b_ref[:, c]


def per_device(fields, previous, cotangent):
    cells, rows, lanes = fields.shape[1:]
    groups = lax.axis_size("gy")
    points = rows * groups
    first, second = wall_matrices(points)
    weight, wall = wall_profile(points)
    at = lax.axis_index("gy").astype(jnp.int32).reshape(1)
    sent = like(cells, 4, rows, lanes)
    block = like(4, cells, rows, lanes)

    exchange = functools.partial(lax.all_to_all, axis_name="gy", split_axis=0, concat_axis=0, tiled=True)

    (f_out,) = call(swap_kernel, [sent], [fields], 0)
    f_lines = exchange(f_out)
    face = like(8, 4, rows, lanes)
    c_out, last, lead, zed = call(
        faces_kernel, [sent, face, face, like(cells, rows, lanes)], [fields, cotangent], 10**6
    )
    c_lines = exchange(c_out)

    gx = lax.axis_size("gx")
    gz = lax.axis_size("gz")
    before = lax.ppermute(last, "gx", [(i, (i + 1) % gx) for i in range(gx)])
    after = lax.ppermute(lead, "gx", [((i + 1) % gx, i) for i in range(gx)])
    zed = lax.ppermute(zed, "gz", [(i, (i + 1) % gz) for i in range(gz)])

    local_res, local_adj = pl.pallas_call(
        local_kernel,
        out_shape=[block, block],
        in_specs=[pl.BlockSpec(memory_space=pltpu.VMEM)] * 8 + [pl.BlockSpec(memory_space=pltpu.SMEM)],
        scratch_shapes=[pltpu.VMEM((11, cells + 8, rows, lanes), f32)],
        cost_estimate=pl.CostEstimate(flops=2 * 10**7, bytes_accessed=6 * 10**6, transcendentals=0),
        compiler_params=pltpu.CompilerParams(vmem_limit_bytes=VMEM_BYTES),
    )(fields, previous, cotangent, before, after, zed, jnp.asarray(weight), jnp.asarray(wall), at)

    wide = 2 * points * points * lanes * 42
    r_out, slope = call(
        res_lines_kernel,
        [like(groups, 4, rows, lanes), like(3, points, lanes)],
        [jnp.asarray(first), jnp.asarray(second), jnp.asarray(weight), f_lines],
        wide,
    )
    r_back = exchange(r_out)
    (a_out,) = call(
        adj_lines_kernel,
        [like(groups, 4, rows, lanes)],
        [
            jnp.asarray(np.ascontiguousarray(first.T)),
            jnp.asarray(np.ascontiguousarray(second.T)),
            jnp.asarray(weight),
            f_lines,
            c_lines,
            slope,
        ],
        wide,
    )
    a_back = exchange(a_out)
    (residual,) = call(add_kernel, [block], [local_res, r_back], 10**6)
    (adjoint,) = call(add_kernel, [block], [local_adj, a_back], 10**6)
    return residual, adjoint


def solution(mesh):
    spec = P(None, "gx", "gy", "gz")
    return jax.shard_map(
        per_device, mesh=mesh, in_specs=(spec,) * 3, out_specs=(spec,) * 2, check_vma=False
    )
```

time: 236 us -> 94.5 us (0.40)
  the two profiles are of different devices: /device:TPU:1 before, /device:TPU:8 now
where the time goes in v1:
time: 94.5 us; the launch traced here: 93.9 us
  waiting for transfers between devices  39.8 us (42%)
  starting transfers between devices  32.9 us (35%)
  Pallas kernels  15.2 us (16%)
  local copies, waits for them, and re-layouts  5.23 us (6%)
    all_to_all x1, waiting for transfers between devices, per_device(): f_lines = exchange(f_out)  12.1 us
    all_to_all x1, waiting for transfers between devices, per_device(): c_lines = exchange(c_out)  11.3 us
    all_to_all x1, starting transfers between devices, per_device(): f_lines = exchange(f_out)  10.1 us
    all_to_all x1, waiting for transfers between devices, per_device(): r_back = exchange(r_out)  9.97 us
    pallas_call x6, Pallas kernels, call(): pl.pallas_call(kernel, out_shape=outs, scratch_shapes=list(scratch), cost...  9.74 us
    ppermute x1, waiting for transfers between devices, per_device(): zed = lax.ppermute(zed, 'gz', [(i, (i + 1) % gz) for i in range(gz)])  6.39 us
    all_to_all x1, starting transfers between devices, per_device(): r_back = exchange(r_out)  6.04 us
    all_to_all x1, starting transfers between devices, per_device(): c_lines = exchange(c_out)  5.92 us
  transfers between devices with their start and end apart: 7, of which 4 were waited for; matrix products, arithmetic and copies ran while one was open for 0% of the time, Pallas kernels for 14%

profile of v1, /device:TPU:8, one launch (start us, length us, event | category | flops | bytes accessed | tf_op | source)
XLA Modules:
  0.0 93.9 jit_solution(3638965992470571431)
XLA Ops:
  0.6 0.0 copy-start
  0.6 1.0 %copy-done = f32[4,16,16,128]{3,2,1,0:T(8,128)S(1)} copy-done((f32[4,16,16,128]{3,2,1,0:T(8,128)S(1)}, f32[4,16,16,128]{3,2,1,0:T(8,128)}, u32[]{:S(2)}) %copy-start) | copy-done | bytes 524312
  1.7 0.8 shard_map.106
  2.5 10.1 %all-to-all-start = ((f32[16,4,16,128]{3,2,1,0:T(8,128)}), f32[16,4,16,128]{3,2,1,0:T(8,128)S(1)}, u32[]{:S(2)}, u32[]{:S(2)}) async-start(f32[16,4,16,128]{3,2,1,0:T(8,128)} %shard_map.106), calls=%async_computation | async-start | bytes 1048576 | tf_op jit(solution)/shard_map/all_to_all | solution.py:245
  12.6 2.3 %shard_map.104 = (f32[16,4,16,128]{3,2,1,0:T(8,128)}, f32[8,4,16,128]{3,2,1,0:T(8,128)}, f32[8,4,16,128]{3,2,1,0:T(8,128)}, f32[16,16,128]{2,1,0:T(8,128)S(1)}) custom-call(f32[4,16,16,128]{3,2,1,0:T(8,128)S(1)} %copy-done.1, f32[4,16,16,128]{3,2,1,0:T(8,128)S(1)} %copy-done.2), custom_call_target="tpu_custom_call" | custom-call | flops 1000000 | bytes 2228224 | tf_op jit(solution)/shard_map/pallas_call | solution.py:50
  14.9 12.1 %all-to-all-done.f_ref = f32[16,4,16,128]{3,2,1,0:T(8,128)S(1)} async-done(((f32[16,4,16,128]{3,2,1,0:T(8,128)}), f32[16,4,16,128]{3,2,1,0:T(8,128)S(1)}, u32[]{:S(2)}, u32[]{:S(2)}) %all-to-all-start) | async-done | bytes 524320 | tf_op jit(solution)/shard_map/all_to_all | solution.py:245
  27.1 0.0 copy-done.12
  27.1 5.9 %all-to-all-start.2 = ((f32[16,4,16,128]{3,2,1,0:T(8,128)}), f32[16,4,16,128]{3,2,1,0:T(8,128)S(1)}, u32[]{:S(2)}, u32[]{:S(2)}) async-start(f32[16,4,16,128]{3,2,1,0:T(8,128)} %get-tuple-element.16), calls=%async_computation.2 | async-start | bytes 1048576 | tf_op jit(solution)/shard_map/all_to_all | solution.py:250
  33.0 0.0 copy-done.3
  33.0 0.0 copy-done.14
  33.0 2.4 %shard_map.107 = (f32[16,4,16,128]{3,2,1,0:T(8,128)}, f32[3,256,128]{2,1,0:T(8,128)S(1)}) custom-call(f32[256,256]{1,0:T(8,128)S(1)} %copy-done.15, f32[256,256]{1,0:T(8,128)S(1)} %copy-done.14, f32[256,128]{1,0:T(8,128)S(1)} %copy-done.3, f32[16,4,16,128]{3,2,1,0:T(8,128)S(1)} %all-to-all-done.f_ref), custom_call_target="tpu_custom_call" | custom-call | flops 704643072 | bytes 2097152 | tf_op jit(solution)/shard_map/pallas_call | solution.py:50
  35.5 11.3 %all-to-all-done.2.c_ref = f32[16,4,16,128]{3,2,1,0:T(8,128)S(1)} async-done(((f32[16,4,16,128]{3,2,1,0:T(8,128)}), f32[16,4,16,128]{3,2,1,0:T(8,128)S(1)}, u32[]{:S(2)}, u32[]{:S(2)}) %all-to-all-start.2) | async-done | bytes 524320 | tf_op jit(solution)/shard_map/all_to_all | solution.py:250
  46.8 6.0 %all-to-all-start.1 = ((f32[16,4,16,128]{3,2,1,0:T(8,128)}), f32[16,4,16,128]{3,2,1,0:T(8,128)S(1)}, u32[]{:S(2)}, u32[]{:S(2)}) async-start(f32[16,4,16,128]{3,2,1,0:T(8,128)} %get-tuple-element.14), calls=%async_computation.1 | async-start | bytes 1048576 | tf_op jit(solution)/shard_map/all_to_all | solution.py:274
  52.8 0.0 copy-start.6
  52.9 0.9 %copy-done.6 = f32[256,256]{1,0:T(8,128)S(1)} copy-done((f32[256,256]{1,0:T(8,128)S(1)}, f32[256,256]{1,0:T(8,128)}, u32[]{:S(2)}) %copy-start.6) | copy-done | bytes 262168
  53.8 2.4 %shard_map.109 = f32[16,4,16,128]{3,2,1,0:T(8,128)} custom-call(f32[256,256]{1,0:T(8,128)S(1)} %copy-done.6, f32[256,256]{1,0:T(8,128)S(1)} %copy-done.5, f32[256,128]{1,0:T(8,128)S(1)} %copy-done.3, f32[16,4,16,128]{3,2,1,0:T(8,128)S(1)} %all-to-all-done.f_ref, f32[16,4,16,128]{3,2,1,0:T(8,128)S(1)} %all-to-all-done.2.c_ref, ...), custom_call_target="tpu_custom_call" | custom-call | flops 704643072 | bytes 2621440 | tf_op jit(solution)/shard_map/pallas_call | solution.py:50
  56.2 10.0 %all-to-all-done.1.b_ref = f32[16,4,16,128]{3,2,1,0:T(8,128)S(1)} async-done(((f32[16,4,16,128]{3,2,1,0:T(8,128)}), f32[16,4,16,128]{3,2,1,0:T(8,128)S(1)}, u32[]{:S(2)}, u32[]{:S(2)}) %all-to-all-start.1) | async-done | bytes 524320 | tf_op jit(solution)/shard_map/all_to_all | solution.py:274
  66.2 5.6 %all-to-all-start.3 = ((f32[16,4,16,128]{3,2,1,0:T(8,128)}), f32[16,4,16,128]{3,2,1,0:T(8,128)S(1)}, u32[]{:S(2)}, u32[]{:S(2)}) async-start(f32[16,4,16,128]{3,2,1,0:T(8,128)} %shard_map.109), calls=%async_computation.3 | async-start | bytes 1048576 | tf_op jit(solution)/shard_map/all_to_all | solution.py:288
  71.8 0.0 collective-permute-start
  71.9 2.9 %collective-permute-start.1 = (f32[8,4,16,128]{3,2,1,0:T(8,128)}, f32[8,4,16,128]{3,2,1,0:T(8,128)S(1)}, u32[]{:S(2)}, u32[]{:S(2)}) collective-permute-start(f32[8,4,16,128]{3,2,1,0:T(8,128)} %get-tuple-element.11), channel_id=1, source_target_pairs={{2,0},{4,2},{6,4},{8,6},{10,8},{12,10},{14,12},{0,14},{3,1},{5,3},... | collective-permute-start | bytes 786440 | tf_op jit(solution)/shard_map/ppermute | solution.py:255
  74.8 2.3 %collective-permute-start.2 = (f32[16,16,128]{2,1,0:T(8,128)S(1)}, f32[16,16,128]{2,1,0:T(8,128)S(1)}, u32[]{:S(2)}, u32[]{:S(2)}) collective-permute-start(f32[16,16,128]{2,1,0:T(8,128)S(1)} %copy-done.13), channel_id=1, source_target_pairs={{0,1},{1,0},{2,3},{3,2},{4,5},{5,4},{6,7},{7,6},{8,9},{9,8},{10,11... | collective-permute-start | bytes 393224 | tf_op jit(solution)/shard_map/ppermute | solution.py:256
  77.1 6.4 %collective-permute-done.2.zed_ref = f32[16,16,128]{2,1,0:T(8,128)S(1)} collective-permute-done((f32[16,16,128]{2,1,0:T(8,128)S(1)}, f32[16,16,128]{2,1,0:T(8,128)S(1)}, u32[]{:S(2)}, u32[]{:S(2)}) %collective-permute-start.2) | collective-permute-done | bytes 131104 | tf_op jit(solution)/shard_map/ppermute | solution.py:256
  83.5 0.7 copy-done.10
  84.2 0.0 collective-permute-done.before_ref
  84.2 0.0 collective-permute-done.1.after_ref
  84.2 0.7 copy-done.7
  84.9 0.9 %copy-done.8 = f32[8,4,16,128]{3,2,1,0:T(8,128)S(1)} copy-done((f32[8,4,16,128]{3,2,1,0:T(8,128)S(1)}, f32[8,4,16,128]{3,2,1,0:T(8,128)}, u32[]{:S(2)}) %copy-start.8) | copy-done | bytes 262168
  85.8 0.9 copy-done.11
  86.7 5.5 %shard_map.105 = (f32[4,16,16,128]{3,2,1,0:T(8,128)S(1)}, f32[4,16,16,128]{3,2,1,0:T(8,128)S(1)}) custom-call(f32[4,16,16,128]{3,2,1,0:T(8,128)S(1)} %copy-done.1, f32[3,16,16,128]{3,2,1,0:T(8,128)S(1)} %copy-done.4, f32[4,16,16,128]{3,2,1,0:T(8,128)S(1)} %copy-done.2, f32[8,4,16,128]{3,2,1,0:T(8,128)S(1)} %collective-permute-done.before_ref, ...), custom_call_target="tpu_custom_call" | custom-call | flops 20000000 | bytes 6000000 | tf_op jit(solution)/shard_map/pallas_call | solution.py:258
  92.2 0.8 shard_map.108
  93.0 0.0 all-to-all-done.3.b_ref
  93.0 0.8 shard_map.110
  (21 shorter events, 0.0 us)
Async XLA Ops:
  0.6 1.0 %copy-start = (f32[4,16,16,128]{3,2,1,0:T(8,128)S(1)}, f32[4,16,16,128]{3,2,1,0:T(8,128)}, u32[]{:S(2)}) copy-start(f32[4,16,16,128]{3,2,1,0:T(8,128)} %a_ref.1) | copy-start | bytes 1572868
  2.5 10.1 %copy-start.1 = (f32[4,16,16,128]{3,2,1,0:T(8,128)S(1)}, f32[4,16,16,128]{3,2,1,0:T(8,128)}, u32[]{:S(2)}) copy-start(f32[4,16,16,128]{3,2,1,0:T(8,128)} %a_ref.1) | copy-start | bytes 1572868
  2.5 10.1 %copy-start.2 = (f32[4,16,16,128]{3,2,1,0:T(8,128)S(1)}, f32[4,16,16,128]{3,2,1,0:T(8,128)}, u32[]{:S(2)}) copy-start(f32[4,16,16,128]{3,2,1,0:T(8,128)} %cot_ref.3) | copy-start | bytes 1572868
  2.5 24.5 %all-to-all-start = ((f32[16,4,16,128]{3,2,1,0:T(8,128)}), f32[16,4,16,128]{3,2,1,0:T(8,128)S(1)}, u32[]{:S(2)}, u32[]{:S(2)}) async-start(f32[16,4,16,128]{3,2,1,0:T(8,128)} %shard_map.106), calls=%async_computation | async-start | bytes 1048576 | tf_op jit(solution)/shard_map/all_to_all | solution.py:245
  14.9 12.1 %copy-start.12 = (f32[16,16,128]{2,1,0:T(8,128)}, f32[16,16,128]{2,1,0:T(8,128)S(1)}, u32[]{:S(2)}) copy-start(f32[16,16,128]{2,1,0:T(8,128)S(1)} %get-tuple-element.12) | copy-start | bytes 393220
  27.1 5.9 %copy-start.3 = (f32[256,128]{1,0:T(8,128)S(1)}, f32[256,128]{1,0:T(8,128)}, u32[]{:S(2)}) copy-start(f32[256,128]{1,0:T(8,128)} %constant.17.clone.weight_ref) | copy-start | bytes 393220
  27.1 5.9 %copy-start.14 = (f32[256,256]{1,0:T(8,128)S(1)}, f32[256,256]{1,0:T(8,128)}, u32[]{:S(2)}) copy-start(f32[256,256]{1,0:T(8,128)} %constant.20.clone.second_ref) | copy-start | bytes 786436
  27.1 5.9 %copy-start.15 = (f32[256,256]{1,0:T(8,128)S(1)}, f32[256,256]{1,0:T(8,128)}, u32[]{:S(2)}) copy-start(f32[256,256]{1,0:T(8,128)} %constant.19.clone.first_ref) | copy-start | bytes 786436
  27.1 19.7 %all-to-all-start.2 = ((f32[16,4,16,128]{3,2,1,0:T(8,128)}), f32[16,4,16,128]{3,2,1,0:T(8,128)S(1)}, u32[]{:S(2)}, u32[]{:S(2)}) async-start(f32[16,4,16,128]{3,2,1,0:T(8,128)} %get-tuple-element.16), calls=%async_computation.2 | async-start | bytes 1048576 | tf_op jit(solution)/shard_map/all_to_all | solution.py:250
  46.8 6.0 %copy-start.5 = (f32[256,256]{1,0:T(8,128)S(1)}, f32[256,256]{1,0:T(8,128)}, u32[]{:S(2)}) copy-start(f32[256,256]{1,0:T(8,128)} %constant.22.clone.second_t_ref) | copy-start | bytes 786436
  46.8 19.4 %all-to-all-start.1 = ((f32[16,4,16,128]{3,2,1,0:T(8,128)}), f32[16,4,16,128]{3,2,1,0:T(8,128)S(1)}, u32[]{:S(2)}, u32[]{:S(2)}) async-start(f32[16,4,16,128]{3,2,1,0:T(8,128)} %get-tuple-element.14), calls=%async_computation.1 | async-start | bytes 1048576 | tf_op jit(solution)/shard_map/all_to_all | solution.py:274
  52.8 1.0 %copy-start.6 = (f32[256,256]{1,0:T(8,128)S(1)}, f32[256,256]{1,0:T(8,128)}, u32[]{:S(2)}) copy-start(f32[256,256]{1,0:T(8,128)} %constant.21.clone.first_t_ref) | copy-start | bytes 786436
  56.2 18.6 %copy-start.13 = (f32[16,16,128]{2,1,0:T(8,128)S(1)}, f32[16,16,128]{2,1,0:T(8,128)}, u32[]{:S(2)}) copy-start(f32[16,16,128]{2,1,0:T(8,128)} %copy-done.12) | copy-start | bytes 393220
  56.2 28.6 %copy-start.4 = (f32[3,16,16,128]{3,2,1,0:T(8,128)S(1)}, f32[3,16,16,128]{3,2,1,0:T(8,128)}, u32[]{:S(2)}) copy-start(f32[3,16,16,128]{3,2,1,0:T(8,128)} %prev_ref.1) | copy-start | bytes 1179652
  56.2 28.6 %copy-start.9 = (f32[256,128]{1,0:T(8,128)S(1)}, f32[256,128]{1,0:T(8,128)}, u32[]{:S(2)}) copy-start(f32[256,128]{1,0:T(8,128)} %constant.18.clone.wall_ref) | copy-start | bytes 393220
  66.2 26.8 %all-to-all-start.3 = ((f32[16,4,16,128]{3,2,1,0:T(8,128)}), f32[16,4,16,128]{3,2,1,0:T(8,128)S(1)}, u32[]{:S(2)}, u32[]{:S(2)}) async-start(f32[16,4,16,128]{3,2,1,0:T(8,128)} %shard_map.109), calls=%async_computation.3 | async-start | bytes 1048576 | tf_op jit(solution)/shard_map/all_to_all | solution.py:288
  71.8 12.3 %collective-permute-start = (f32[8,4,16,128]{3,2,1,0:T(8,128)}, f32[8,4,16,128]{3,2,1,0:T(8,128)S(1)}, u32[]{:S(2)}, u32[]{:S(2)}) collective-permute-start(f32[8,4,16,128]{3,2,1,0:T(8,128)} %get-tuple-element.10), channel_id=1, source_target_pairs={{0,2},{2,4},{4,6},{6,8},{8,10},{10,12},{12,14},{14,0},{1,3},{3,5},... | collective-permute-start | bytes 786440 | tf_op jit(solution)/shard_map/ppermute | solution.py:254
  71.9 12.3 %collective-permute-start.1 = (f32[8,4,16,128]{3,2,1,0:T(8,128)}, f32[8,4,16,128]{3,2,1,0:T(8,128)S(1)}, u32[]{:S(2)}, u32[]{:S(2)}) collective-permute-start(f32[8,4,16,128]{3,2,1,0:T(8,128)} %get-tuple-element.11), channel_id=1, source_target_pairs={{2,0},{4,2},{6,4},{8,6},{10,8},{12,10},{14,12},{0,14},{3,1},{5,3},... | collective-permute-start | bytes 786440 | tf_op jit(solution)/shard_map/ppermute | solution.py:255
  74.8 8.7 %collective-permute-start.2 = (f32[16,16,128]{2,1,0:T(8,128)S(1)}, f32[16,16,128]{2,1,0:T(8,128)S(1)}, u32[]{:S(2)}, u32[]{:S(2)}) collective-permute-start(f32[16,16,128]{2,1,0:T(8,128)S(1)} %copy-done.13), channel_id=1, source_target_pairs={{0,1},{1,0},{2,3},{3,2},{4,5},{5,4},{6,7},{7,6},{8,9},{9,8},{10,11... | collective-permute-start | bytes 393224 | tf_op jit(solution)/shard_map/ppermute | solution.py:256
  83.5 0.7 copy-start.10
  84.2 0.7 copy-start.7
  84.9 1.0 %copy-start.8 = (f32[8,4,16,128]{3,2,1,0:T(8,128)S(1)}, f32[8,4,16,128]{3,2,1,0:T(8,128)}, u32[]{:S(2)}) copy-start(f32[8,4,16,128]{3,2,1,0:T(8,128)} %copy-done.7) | copy-start | bytes 786436
  85.8 0.9 copy-start.11

commit v2 on v1

--- a/solution.py
+++ b/solution.py
@@ -60,19 +60,17 @@
     return jax.ShapeDtypeStruct(shape, f32)
 
 
-def swap_kernel(a_ref, out_ref):
-    for c in range(a_ref.shape[0]):
-        out_ref[:, c] = a_ref[c]
-
-
-def faces_kernel(fields_ref, cot_ref, cot_out, last_out, lead_out, zed_out):
+def pack_kernel(fields_ref, cot_ref, sent_out, last_out, lead_out):
     comps, cells = cot_ref.shape[0:2]
     for c in range(comps):
-        cot_out[:, c] = cot_ref[c]
-        last_out[c] = fields_ref[c, cells - 4 : cells]
-        last_out[comps + c] = cot_ref[c, cells - 4 : cells]
-        lead_out[c] = fields_ref[c, 0:4]
-        lead_out[comps + c] = cot_ref[c, 0:4]
+        for ref, slot in ((fields_ref, c), (cot_ref, comps + c)):
+            sent_out[:, slot] = ref[c]
+            last_out[slot] = ref[c, cells - 4 : cells]
+            lead_out[slot] = ref[c, 0:4]
+
+
+def zed_kernel(fields_ref, cot_ref, zed_out):
+    comps, cells = cot_ref.shape[0:2]
 
     def plane(x, _):
         lane = lax.broadcasted_iota(jnp.int32, zed_out.shape[1:], 1)
@@ -191,42 +189,43 @@
     return value.reshape(groups, value.shape[0] // groups, value.shape[1])
 
 
-def res_lines_kernel(first_ref, second_ref, weight_ref, f_ref, out_ref, slope_ref):
-    groups = f_ref.shape[0]
+def product(matrix_ref, values):
+    lanes = values[0].shape[1]
+    wide = jnp.dot(
+        matrix_ref[...], jnp.concatenate(values, axis=1), precision=EXACT, preferred_element_type=f32
+    )
+    return [wide[:, i * lanes : (i + 1) * lanes] for i in range(len(values))]
+
+
+def lines_kernel(first_ref, second_ref, first_t_ref, second_t_ref, weight_ref, in_ref, out_ref):
+    groups = in_ref.shape[0]
     weight = weight_ref[...]
-    u = [lines(f_ref, c) for c in range(4)]
+    u = [lines(in_ref, c) for c in range(4)]
+    slope = product(first_ref, u)
+    curve = product(second_ref, u[0:3])
     for c in range(3):
-        slope = jnp.dot(first_ref[...], u[c], precision=EXACT, preferred_element_type=f32)
-        curve = jnp.dot(second_ref[...], u[c], precision=EXACT, preferred_element_type=f32)
-        slope_ref[c] = slope
-        total = u[1] * slope - NU_VALUE * curve
+        total = u[1] * slope[c] - NU_VALUE * curve[c]
         if c == 1:
-            total = total + jnp.dot(first_ref[...], u[3], precision=EXACT, preferred_element_type=f32)
-            out_ref[:, 3] = blocks(weight * slope, groups)
+            total = total + slope[3]
         out_ref[:, c] = blocks(weight * total, groups)
-
-
-def adj_lines_kernel(first_t_ref, second_t_ref, weight_ref, f_ref, c_ref, slope_ref, out_ref):
-    groups = f_ref.shape[0]
-    weight = weight_ref[...]
-    u2 = lines(f_ref, 1)
-    w = [weight * lines(c_ref, c) for c in range(4)]
+    out_ref[:, 3] = blocks(weight * slope[1], groups)
+    w = [weight * lines(in_ref, 4 + c) for c in range(4)]
+    stretch = w[0] * slope[0] + w[1] * slope[1] + w[2] * slope[2]
+    carried = [u[1] * w[0], u[1] * w[1] + w[3], u[1] * w[2], w[1]]
+    lifted = product(first_t_ref, carried)
+    bent = product(second_t_ref, w[0:3])
     for c in range(3):
-        carried = u2 * w[c]
+        total = lifted[c] - NU_VALUE * bent[c]
         if c == 1:
-            carried = carried + w[3]
-        total = jnp.dot(first_t_ref[...], carried, precision=EXACT, preferred_element_type=f32)
-        total = total - NU_VALUE * jnp.dot(second_t_ref[...], w[c], precision=EXACT, preferred_element_type=f32)
-        if c == 1:
-            total = total + w[0] * slope_ref[0] + w[1] * slope_ref[1] + w[2] * slope_ref[2]
-        out_ref[:, c] = blocks(total, groups)
-    press = jnp.dot(first_t_ref[...], w[1], precision=EXACT, preferred_element_type=f32)
-    out_ref[:, 3] = blocks(press, groups)
-
-
-def add_kernel(a_ref, b_ref, out_ref):
-    for c in range(a_ref.shape[0]):
-        out_ref[c] = a_ref[c] + b_ref[:, c]
+            total = total + stretch
+        out_ref[:, 4 + c] = blocks(total, groups)
+    out_ref[:, 7] = blocks(lifted[3], groups)
+
+
+def add_kernel(res_ref, adj_ref, back_ref, res_out, adj_out):
+    for c in range(4):
+        res_out[c] = res_ref[c] + back_ref[:, c]
+        adj_out[c] = adj_ref[c] + back_ref[:, 4 + c]
 
 
 def per_device(fields, previous, cotangent):
@@ -236,21 +235,16 @@
     first, second = wall_matrices(points)
     weight, wall = wall_profile(points)
     at = lax.axis_index("gy").astype(jnp.int32).reshape(1)
-    sent = like(cells, 4, rows, lanes)
+    sent = like(cells, 8, rows, lanes)
+    face = like(8, 4, rows, lanes)
     block = like(4, cells, rows, lanes)
+    gx, gz = lax.axis_size("gx"), lax.axis_size("gz")
 
     exchange = functools.partial(lax.all_to_all, axis_name="gy", split_axis=0, concat_axis=0, tiled=True)
 
-    (f_out,) = call(swap_kernel, [sent], [fields], 0)
-    f_lines = exchange(f_out)
-    face = like(8, 4, rows, lanes)
-    c_out, last, lead, zed = call(
-        faces_kernel, [sent, face, face, like(cells, rows, lanes)], [fields, cotangent], 10**6
-    )
-    c_lines = exchange(c_out)
-
-    gx = lax.axis_size("gx")
-    gz = lax.axis_size("gz")
+    packed, last, lead = call(pack_kernel, [sent, face, face], [fields, cotangent], 0)
+    gathered = exchange(packed)
+    (zed,) = call(zed_kernel, [like(cells, rows, lanes)], [fields, cotangent], 10**6)
     before = lax.ppermute(last, "gx", [(i, (i + 1) % gx) for i in range(gx)])
     after = lax.ppermute(lead, "gx", [((i + 1) % gx, i) for i in range(gx)])
     zed = lax.ppermute(zed, "gz", [(i, (i + 1) % gz) for i in range(gz)])
@@ -264,30 +258,15 @@
         compiler_params=pltpu.CompilerParams(vmem_limit_bytes=VMEM_BYTES),
     )(fields, previous, cotangent, before, after, zed, jnp.asarray(weight), jnp.asarray(wall), at)
 
-    wide = 2 * points * points * lanes * 42
-    r_out, slope = call(
-        res_lines_kernel,
-        [like(groups, 4, rows, lanes), like(3, points, lanes)],
-        [jnp.asarray(first), jnp.asarray(second), jnp.asarray(weight), f_lines],
-        wide,
-    )
-    r_back = exchange(r_out)
-    (a_out,) = call(
-        adj_lines_kernel,
-        [like(groups, 4, rows, lanes)],
-        [
-            jnp.asarray(np.ascontiguousarray(first.T)),
-            jnp.asarray(np.ascontiguousarray(second.T)),
-            jnp.asarray(weight),
-            f_lines,
-            c_lines,
-            slope,
-        ],
-        wide,
-    )
-    a_back = exchange(a_out)
-    (residual,) = call(add_kernel, [block], [local_res, r_back], 10**6)
-    (adjoint,) = call(add_kernel, [block], [local_adj, a_back], 10**6)
+    matrices = [first, second, np.ascontiguousarray(first.T), np.ascontiguousarray(second.T), weight]
+    (lined,) = call(
+        lines_kernel,
+        [like(groups, 8, rows, lanes)],
+        [jnp.asarray(m) for m in matrices] + [gathered],
+        2 * points * points * lanes * 14 * 6,
+    )
+    back = exchange(lined)
+    residual, adjoint = call(add_kernel, [block, block], [local_res, local_adj, back], 10**6)
     return residual, adjoint
 
 

time: 94.5 us -> 75 us (0.79)
  the two profiles are of different devices: /device:TPU:8 before, /device:TPU:32 now
where the time goes in v2:
time: 75 us; the launch traced here: 74.6 us
  blocking collectives  35.7 us (48%)
  Pallas kernels  11.6 us (15%)
  starting transfers between devices  11.3 us (15%)
  local copies, waits for them, and re-layouts  8.79 us (12%)
  waiting for transfers between devices  6.36 us (8%)
    all_to_all x1, blocking collectives, per_device(): gathered = exchange(packed)  35.7 us
    unnamed x36, local copies, waits for them, and re-layouts  8.79 us
    pallas_call x4, Pallas kernels, call(): pl.pallas_call(kernel, out_shape=outs, scratch_shapes=list(scratch), cost...  6.18 us
    pallas_call x1, Pallas kernels, per_device(): pl.pallas_call(local_kernel, out_shape=[block, block], in_specs=[pl.Block...  5.45 us
    all_to_all x1, starting transfers between devices, per_device(): back = exchange(lined)  5.4 us
    ppermute x1, waiting for transfers between devices, per_device(): zed = lax.ppermute(zed, 'gz', [(i, (i + 1) % gz) for i in range(gz)])  5.06 us
    ppermute x1, starting transfers between devices, per_device(): zed = lax.ppermute(zed, 'gz', [(i, (i + 1) % gz) for i in range(gz)])  2.99 us
    ppermute x1, starting transfers between devices, per_device(): after = lax.ppermute(lead, 'gx', [((i + 1) % gx, i) for i in range(gx)])  2.94 us
  transfers between devices with their start and end apart: 4, of which 2 were waited for; matrix products, arithmetic and copies ran while one was open for 0% of the time, Pallas kernels for 9%

profile of v2, /device:TPU:32, one launch (start us, length us, event | category | flops | bytes accessed | tf_op | source)
XLA Modules:
  0.0 74.6 jit_solution(8534832219965523029)
XLA Ops:
  0.6 0.0 copy-start
  0.6 1.0 %copy-done = f32[4,16,16,128]{3,2,1,0:T(8,128)S(1)} copy-done((f32[4,16,16,128]{3,2,1,0:T(8,128)S(1)}, f32[4,16,16,128]{3,2,1,0:T(8,128)}, u32[]{:S(2)}) %copy-start) | copy-done | bytes 524312
  1.7 1.0 %copy-done.2 = f32[4,16,16,128]{3,2,1,0:T(8,128)S(1)} copy-done((f32[4,16,16,128]{3,2,1,0:T(8,128)S(1)}, f32[4,16,16,128]{3,2,1,0:T(8,128)}, u32[]{:S(2)}) %copy-start.2) | copy-done | bytes 524312
  2.7 0.8 %shard_map.104 = (f32[16,8,16,128]{3,2,1,0:T(8,128)S(1)}, f32[8,4,16,128]{3,2,1,0:T(8,128)}, f32[8,4,16,128]{3,2,1,0:T(8,128)S(1)}) custom-call(f32[4,16,16,128]{3,2,1,0:T(8,128)S(1)} %copy-done, f32[4,16,16,128]{3,2,1,0:T(8,128)S(1)} %copy-done.2), custom_call_target="tpu_custom_call" | custom-call | bytes 2621440 | tf_op jit(solution)/shard_map/pallas_call | solution.py:50
  3.5 0.0 copy-start.17
  3.5 35.7 %all_to_all.10.in_ref = f32[16,8,16,128]{3,2,1,0:T(8,128)S(1)} all-to-all(f32[16,8,16,128]{3,2,1,0:T(8,128)S(1)} %get-tuple-element.11), channel_id=1, replica_groups=mesh['gy'=16,'gx'=8,'gz'=2] {'gy'}, dimensions={0} | all-to-all | bytes 2097152 | tf_op jit(solution)/shard_map/all_to_all | solution.py:246
  39.3 0.0 copy-done.9
  39.3 0.0 copy-done.14
  39.3 0.0 copy-done.15
  39.3 0.0 copy-done.16
  39.3 3.0 %shard_map.107 = f32[16,8,16,128]{3,2,1,0:T(8,128)} custom-call(f32[256,256]{1,0:T(8,128)S(1)} %copy-done.17, f32[256,256]{1,0:T(8,128)S(1)} %copy-done.16, f32[256,256]{1,0:T(8,128)S(1)} %copy-done.15, f32[256,256]{1,0:T(8,128)S(1)} %copy-done.14, f32[256,128]{1,0:T(8,128)S(1)} %copy-done.9, f32[16,8,16,128]{3,2,1,0:T(8,128)S(1)} %all_to_all.10.in_ref), custom_call_target="tpu_custom_call" | custom-call | flops 1409286144 | bytes 3276800 | tf_op jit(solution)/shard_map/pallas_call | solution.py:50
  42.3 5.4 %all-to-all-start.1 = ((f32[16,8,16,128]{3,2,1,0:T(8,128)}), f32[16,8,16,128]{3,2,1,0:T(8,128)S(1)}, u32[]{:S(2)}, u32[]{:S(2)}) async-start(f32[16,8,16,128]{3,2,1,0:T(8,128)} %shard_map.107), calls=%async_computation.1 | async-start | bytes 2097152 | tf_op jit(solution)/shard_map/all_to_all | solution.py:268
  47.7 0.0 collective-permute-start
  47.7 0.0 copy-start.4
  47.7 2.9 %collective-permute-start.1 = (f32[8,4,16,128]{3,2,1,0:T(8,128)S(1)}, f32[8,4,16,128]{3,2,1,0:T(8,128)S(1)}, u32[]{:S(2)}, u32[]{:S(2)}) collective-permute-start(f32[8,4,16,128]{3,2,1,0:T(8,128)S(1)} %get-tuple-element.8), channel_id=1, source_target_pairs={{2,0},{4,2},{6,4},{8,6},{10,8},{12,10},{14,12},{0,14},{3,1},{5,3},... | collective-permute-start | bytes 786440 | tf_op jit(solution)/shard_map/ppermute | solution.py:249
  50.6 1.4 %shard_map.105 = f32[16,16,128]{2,1,0:T(8,128)S(1)} custom-call(f32[4,16,16,128]{3,2,1,0:T(8,128)S(1)} %copy-done.1, f32[4,16,16,128]{3,2,1,0:T(8,128)S(1)} %copy-done.3), custom_call_target="tpu_custom_call" | custom-call | flops 1000000 | bytes 1179648 | tf_op jit(solution)/shard_map/pallas_call | solution.py:50
  52.0 3.0 %collective-permute-start.2 = (f32[16,16,128]{2,1,0:T(8,128)S(1)}, f32[16,16,128]{2,1,0:T(8,128)S(1)}, u32[]{:S(2)}, u32[]{:S(2)}) collective-permute-start(f32[16,16,128]{2,1,0:T(8,128)S(1)} %shard_map.105), channel_id=1, source_target_pairs={{0,1},{1,0},{2,3},{3,2},{4,5},{5,4},{6,7},{7,6},{8,9},{9,8},{10,11... | collective-permute-start | bytes 393224 | tf_op jit(solution)/shard_map/ppermute | solution.py:250
  55.0 5.1 %collective-permute-done.2.zed_ref = f32[16,16,128]{2,1,0:T(8,128)S(1)} collective-permute-done((f32[16,16,128]{2,1,0:T(8,128)S(1)}, f32[16,16,128]{2,1,0:T(8,128)S(1)}, u32[]{:S(2)}, u32[]{:S(2)}) %collective-permute-start.2) | collective-permute-done | bytes 131104 | tf_op jit(solution)/shard_map/ppermute | solution.py:250
  60.1 0.7 copy-done.12
  60.7 0.0 collective-permute-done.before_ref
  60.7 0.7 copy-done.5
  61.4 0.0 collective-permute-done.1.after_ref
  61.4 0.7 copy-done.7
  62.1 0.0 copy-done.4
  62.1 0.9 %copy-done.6 = f32[8,4,16,128]{3,2,1,0:T(8,128)S(1)} copy-done((f32[8,4,16,128]{3,2,1,0:T(8,128)S(1)}, f32[8,4,16,128]{3,2,1,0:T(8,128)}, u32[]{:S(2)}) %copy-start.6) | copy-done | bytes 262168
  63.1 0.9 %copy-done.8 = f32[8,4,16,128]{3,2,1,0:T(8,128)S(1)} copy-done((f32[8,4,16,128]{3,2,1,0:T(8,128)S(1)}, f32[8,4,16,128]{3,2,1,0:T(8,128)}, u32[]{:S(2)}) %copy-start.8) | copy-done | bytes 262168
  64.0 0.9 %copy-done.10 = f32[256,128]{1,0:T(8,128)S(1)} copy-done((f32[256,128]{1,0:T(8,128)S(1)}, f32[256,128]{1,0:T(8,128)}, u32[]{:S(2)}) %copy-start.10) | copy-done | bytes 131096
  64.9 0.9 %copy-done.11 = f32[256,128]{1,0:T(8,128)S(1)} copy-done((f32[256,128]{1,0:T(8,128)S(1)}, f32[256,128]{1,0:T(8,128)}, u32[]{:S(2)}) %copy-start.11) | copy-done | bytes 131096
  65.9 0.9 %copy-done.13 = f32[16,16,128]{2,1,0:T(8,128)S(1)} copy-done((f32[16,16,128]{2,1,0:T(8,128)S(1)}, f32[16,16,128]{2,1,0:T(8,128)}, u32[]{:S(2)}) %copy-start.13) | copy-done | bytes 131096
  66.8 5.5 %shard_map.106 = (f32[4,16,16,128]{3,2,1,0:T(8,128)S(1)}, f32[4,16,16,128]{3,2,1,0:T(8,128)S(1)}) custom-call(f32[4,16,16,128]{3,2,1,0:T(8,128)S(1)} %copy-done.1, f32[3,16,16,128]{3,2,1,0:T(8,128)S(1)} %copy-done.4, f32[4,16,16,128]{3,2,1,0:T(8,128)S(1)} %copy-done.3, f32[8,4,16,128]{3,2,1,0:T(8,128)S(1)} %copy-done.6, f32[8,4,16,128]{3,2,1,0:T(8,128)S(1)} %copy-done.8, ...), custom_call_target="tpu_custom_call" | custom-call | flops 20000000 | bytes 6000000 | tf_op jit(solution)/shard_map/pallas_call | solution.py:252
  72.2 1.3 %all-to-all-done.1.back_ref = f32[16,8,16,128]{3,2,1,0:T(8,128)S(1)} async-done(((f32[16,8,16,128]{3,2,1,0:T(8,128)}), f32[16,8,16,128]{3,2,1,0:T(8,128)S(1)}, u32[]{:S(2)}, u32[]{:S(2)}) %all-to-all-start.1) | async-done | bytes 1048608 | tf_op jit(solution)/shard_map/all_to_all | solution.py:268
  73.5 1.1 %shard_map.108 = (f32[4,16,16,128]{3,2,1,0:T(8,128)}, f32[4,16,16,128]{3,2,1,0:T(8,128)}) custom-call(f32[4,16,16,128]{3,2,1,0:T(8,128)S(1)} %get-tuple-element.9.res_ref, f32[4,16,16,128]{3,2,1,0:T(8,128)S(1)} %get-tuple-element.10.adj_ref, f32[16,8,16,128]{3,2,1,0:T(8,128)S(1)} %all-to-all-done.1.back_ref), custom_call_target="tpu_custom_call" | custom-call | flops 1000000 | bytes 3145728 | tf_op jit(solution)/shard_map/pallas_call | solution.py:50
  (18 shorter events, 0.0 us)
Async XLA Ops:
  0.6 1.0 %copy-start = (f32[4,16,16,128]{3,2,1,0:T(8,128)S(1)}, f32[4,16,16,128]{3,2,1,0:T(8,128)}, u32[]{:S(2)}) copy-start(f32[4,16,16,128]{3,2,1,0:T(8,128)} %fields_ref.5) | copy-start | bytes 1572868
  1.7 1.0 %copy-start.2 = (f32[4,16,16,128]{3,2,1,0:T(8,128)S(1)}, f32[4,16,16,128]{3,2,1,0:T(8,128)}, u32[]{:S(2)}) copy-start(f32[4,16,16,128]{3,2,1,0:T(8,128)} %cot_ref.5) | copy-start | bytes 1572868
  3.5 35.8 %copy-start.9 = (f32[256,128]{1,0:T(8,128)S(1)}, f32[256,128]{1,0:T(8,128)}, u32[]{:S(2)}) copy-start(f32[256,128]{1,0:T(8,128)} %constant.17.clone.weight_ref) | copy-start | bytes 393220
  3.5 35.8 %copy-start.14 = (f32[256,256]{1,0:T(8,128)S(1)}, f32[256,256]{1,0:T(8,128)}, u32[]{:S(2)}) copy-start(f32[256,256]{1,0:T(8,128)} %constant.22.clone.second_t_ref) | copy-start | bytes 786436
  3.5 35.8 %copy-start.15 = (f32[256,256]{1,0:T(8,128)S(1)}, f32[256,256]{1,0:T(8,128)}, u32[]{:S(2)}) copy-start(f32[256,256]{1,0:T(8,128)} %constant.21.clone.first_t_ref) | copy-start | bytes 786436
  3.5 35.8 %copy-start.16 = (f32[256,256]{1,0:T(8,128)S(1)}, f32[256,256]{1,0:T(8,128)}, u32[]{:S(2)}) copy-start(f32[256,256]{1,0:T(8,128)} %constant.20.clone.second_ref) | copy-start | bytes 786436
  3.5 35.8 %copy-start.17 = (f32[256,256]{1,0:T(8,128)S(1)}, f32[256,256]{1,0:T(8,128)}, u32[]{:S(2)}) copy-start(f32[256,256]{1,0:T(8,128)} %constant.19.clone.first_ref) | copy-start | bytes 786436
  42.3 8.4 %copy-start.1 = (f32[4,16,16,128]{3,2,1,0:T(8,128)S(1)}, f32[4,16,16,128]{3,2,1,0:T(8,128)}, u32[]{:S(2)}) copy-start(f32[4,16,16,128]{3,2,1,0:T(8,128)} %fields_ref.5) | copy-start | bytes 1572868
  42.3 8.4 %copy-start.3 = (f32[4,16,16,128]{3,2,1,0:T(8,128)S(1)}, f32[4,16,16,128]{3,2,1,0:T(8,128)}, u32[]{:S(2)}) copy-start(f32[4,16,16,128]{3,2,1,0:T(8,128)} %cot_ref.5) | copy-start | bytes 1572868
  42.3 31.2 %all-to-all-start.1 = ((f32[16,8,16,128]{3,2,1,0:T(8,128)}), f32[16,8,16,128]{3,2,1,0:T(8,128)S(1)}, u32[]{:S(2)}, u32[]{:S(2)}) async-start(f32[16,8,16,128]{3,2,1,0:T(8,128)} %shard_map.107), calls=%async_computation.1 | async-start | bytes 2097152 | tf_op jit(solution)/shard_map/all_to_all | solution.py:268
  47.7 13.1 %collective-permute-start = (f32[8,4,16,128]{3,2,1,0:T(8,128)}, f32[8,4,16,128]{3,2,1,0:T(8,128)S(1)}, u32[]{:S(2)}, u32[]{:S(2)}) collective-permute-start(f32[8,4,16,128]{3,2,1,0:T(8,128)} %get-tuple-element.7), channel_id=1, source_target_pairs={{0,2},{2,4},{4,6},{6,8},{8,10},{10,12},{12,14},{14,0},{1,3},{3,5},... | collective-permute-start | bytes 786440 | tf_op jit(solution)/shard_map/ppermute | solution.py:248
  47.7 14.5 %copy-start.4 = (f32[3,16,16,128]{3,2,1,0:T(8,128)S(1)}, f32[3,16,16,128]{3,2,1,0:T(8,128)}, u32[]{:S(2)}) copy-start(f32[3,16,16,128]{3,2,1,0:T(8,128)} %prev_ref.1) | copy-start | bytes 1179652
  47.7 13.7 %collective-permute-start.1 = (f32[8,4,16,128]{3,2,1,0:T(8,128)S(1)}, f32[8,4,16,128]{3,2,1,0:T(8,128)S(1)}, u32[]{:S(2)}, u32[]{:S(2)}) collective-permute-start(f32[8,4,16,128]{3,2,1,0:T(8,128)S(1)} %get-tuple-element.8), channel_id=1, source_target_pairs={{2,0},{4,2},{6,4},{8,6},{10,8},{12,10},{14,12},{0,14},{3,1},{5,3},... | collective-permute-start | bytes 786440 | tf_op jit(solution)/shard_map/ppermute | solution.py:249
  52.0 8.1 %collective-permute-start.2 = (f32[16,16,128]{2,1,0:T(8,128)S(1)}, f32[16,16,128]{2,1,0:T(8,128)S(1)}, u32[]{:S(2)}, u32[]{:S(2)}) collective-permute-start(f32[16,16,128]{2,1,0:T(8,128)S(1)} %shard_map.105), channel_id=1, source_target_pairs={{0,1},{1,0},{2,3},{3,2},{4,5},{5,4},{6,7},{7,6},{8,9},{9,8},{10,11... | collective-permute-start | bytes 393224 | tf_op jit(solution)/shard_map/ppermute | solution.py:250
  60.1 0.7 copy-start.12
  60.7 0.7 copy-start.5
  61.4 0.7 copy-start.7
  62.1 1.0 %copy-start.6 = (f32[8,4,16,128]{3,2,1,0:T(8,128)S(1)}, f32[8,4,16,128]{3,2,1,0:T(8,128)}, u32[]{:S(2)}) copy-start(f32[8,4,16,128]{3,2,1,0:T(8,128)} %copy-done.5) | copy-start | bytes 786436
  63.1 0.9 %copy-start.8 = (f32[8,4,16,128]{3,2,1,0:T(8,128)S(1)}, f32[8,4,16,128]{3,2,1,0:T(8,128)}, u32[]{:S(2)}) copy-start(f32[8,4,16,128]{3,2,1,0:T(8,128)} %copy-done.7) | copy-start | bytes 786436
  64.0 0.9 %copy-start.10 = (f32[256,128]{1,0:T(8,128)S(1)}, f32[256,128]{1,0:T(8,128)}, u32[]{:S(2)}) copy-start(f32[256,128]{1,0:T(8,128)} %constant.17.clone.weight_ref) | copy-start | bytes 393220
  64.9 0.9 %copy-start.11 = (f32[256,128]{1,0:T(8,128)S(1)}, f32[256,128]{1,0:T(8,128)}, u32[]{:S(2)}) copy-start(f32[256,128]{1,0:T(8,128)} %constant.18.clone.wall_ref) | copy-start | bytes 393220
  65.9 0.9 %copy-start.13 = (f32[16,16,128]{2,1,0:T(8,128)S(1)}, f32[16,16,128]{2,1,0:T(8,128)}, u32[]{:S(2)}) copy-start(f32[16,16,128]{2,1,0:T(8,128)} %copy-done.12) | copy-start | bytes 393220

commit v3 on v2

--- a/solution.py
+++ b/solution.py
@@ -60,17 +60,26 @@
     return jax.ShapeDtypeStruct(shape, f32)
 
 
-def pack_kernel(fields_ref, cot_ref, sent_out, last_out, lead_out):
+def pack_kernel(fields_ref, cot_ref, sent_out, held, sems):
+    comps = cot_ref.shape[0]
+    copies = [
+        pltpu.make_async_copy(fields_ref, held.at[0], sems.at[0]),
+        pltpu.make_async_copy(cot_ref, held.at[1], sems.at[1]),
+    ]
+    for copy in copies:
+        copy.start()
+    for half, copy in enumerate(copies):
+        copy.wait()
+        for c in range(comps):
+            sent_out[:, half * comps + c] = held[half, c]
+
+
+def faces_kernel(fields_ref, cot_ref, last_out, lead_out, zed_out):
     comps, cells = cot_ref.shape[0:2]
     for c in range(comps):
         for ref, slot in ((fields_ref, c), (cot_ref, comps + c)):
-            sent_out[:, slot] = ref[c]
             last_out[slot] = ref[c, cells - 4 : cells]
             lead_out[slot] = ref[c, 0:4]
-
-
-def zed_kernel(fields_ref, cot_ref, zed_out):
-    comps, cells = cot_ref.shape[0:2]
 
     def plane(x, _):
         lane = lax.broadcasted_iota(jnp.int32, zed_out.shape[1:], 1)
@@ -99,27 +108,34 @@
 
 
 def local_kernel(
-    fields_ref, prev_ref, cot_ref, before_ref, after_ref, zed_ref, weight_ref, wall_ref, at_ref,
-    res_ref, adj_ref, ext,
+    fields_any, prev_any, cot_any, before_any, after_any, zed_any, weight_any, wall_any, at_ref,
+    res_ref, adj_ref, ext, cot_ref, prev_ref, zed_ref, weight_ref, wall_ref, sems,
 ):
-    cells, rows, lanes = fields_ref.shape[1:]
+    cells, rows, lanes = fields_any.shape[1:]
     here = pl.ds(pl.multiple_of(at_ref[0] * rows, rows), rows)
-    weight = weight_ref[here]
-    wall = wall_ref[here]
-
-    for c in range(4):
-        ext[c, 0:4] = before_ref[c]
-        ext[c, 4 : 4 + cells] = fields_ref[c]
-        ext[c, 4 + cells :] = after_ref[c]
+    pairs = [
+        (fields_any, ext.at[0:4, 4 : 4 + cells]),
+        (before_any.at[0:4], ext.at[0:4, 0:4]),
+        (after_any.at[0:4], ext.at[0:4, 4 + cells : 8 + cells]),
+        (cot_any, cot_ref.at[:, 4 : 4 + cells]),
+        (before_any.at[4:8], cot_ref.at[:, 0:4]),
+        (after_any.at[4:8], cot_ref.at[:, 4 + cells : 8 + cells]),
+        (prev_any, prev_ref),
+        (zed_any, zed_ref),
+        (weight_any.at[here], weight_ref),
+        (wall_any.at[here], wall_ref),
+    ]
+    copies = [pltpu.make_async_copy(src, dst, sems.at[i]) for i, (src, dst) in enumerate(pairs)]
+    for copy in copies:
+        copy.start()
+    for copy in copies:
+        copy.wait()
+    weight = weight_ref[...]
+    wall = wall_ref[...]
+
     for c in range(4):
         for x in range(cells + 8):
-            if x < 4:
-                value = before_ref[4 + c, x]
-            elif x < 4 + cells:
-                value = cot_ref[c, x - 4]
-            else:
-                value = after_ref[4 + c, x - 4 - cells]
-            value = weight * value
+            value = weight * cot_ref[c, x]
             ext[4 + c, x] = value
             if c < 3:
                 ext[8 + c, x] = ext[0, x] * value
@@ -168,7 +184,7 @@
         wz = [along_z(4 + c, c in (2, 3), c < 3) for c in range(4)]
         for c in range(3):
             flux = along_x(8 + c, True, False)[0] + along_z(8 + c, True, False)[0]
-            total = w[c] * (1.0 / STEP_DT) - flux - NU_VALUE * (wx[c][1] + wz[c][1]) + wall * cot_ref[c, x]
+            total = w[c] * (1.0 / STEP_DT) - flux - NU_VALUE * (wx[c][1] + wz[c][1]) + wall * cot_ref[c, 4 + x]
             if c == 0:
                 total = total + (w[0] * dx[0] + w[1] * dx[1] + w[2] * dx[2]) - wx[3][0]
             if c == 2:
@@ -197,29 +213,39 @@
     return [wide[:, i * lanes : (i + 1) * lanes] for i in range(len(values))]
 
 
-def lines_kernel(first_ref, second_ref, first_t_ref, second_t_ref, weight_ref, in_ref, out_ref):
+def lines_kernel(
+    first_ref, second_ref, first_t_ref, second_t_ref, weight_ref, in_ref, out_ref, held, sems
+):
     groups = in_ref.shape[0]
     weight = weight_ref[...]
+    copies = []
+
+    def send(slot, value):
+        held[slot] = blocks(value, groups)
+        copies.append(pltpu.make_async_copy(held.at[slot], out_ref.at[:, slot], sems.at[slot]))
+        copies[-1].start()
+
     u = [lines(in_ref, c) for c in range(4)]
+    w = [weight * lines(in_ref, 4 + c) for c in range(4)]
     slope = product(first_ref, u)
     curve = product(second_ref, u[0:3])
     for c in range(3):
         total = u[1] * slope[c] - NU_VALUE * curve[c]
         if c == 1:
             total = total + slope[3]
-        out_ref[:, c] = blocks(weight * total, groups)
-    out_ref[:, 3] = blocks(weight * slope[1], groups)
-    w = [weight * lines(in_ref, 4 + c) for c in range(4)]
+        send(c, weight * total)
+    send(3, weight * slope[1])
     stretch = w[0] * slope[0] + w[1] * slope[1] + w[2] * slope[2]
-    carried = [u[1] * w[0], u[1] * w[1] + w[3], u[1] * w[2], w[1]]
-    lifted = product(first_t_ref, carried)
+    lifted = product(first_t_ref, [u[1] * w[0], u[1] * w[1] + w[3], u[1] * w[2], w[1]])
+    send(7, lifted[3])
     bent = product(second_t_ref, w[0:3])
     for c in range(3):
         total = lifted[c] - NU_VALUE * bent[c]
         if c == 1:
             total = total + stretch
-        out_ref[:, 4 + c] = blocks(total, groups)
-    out_ref[:, 7] = blocks(lifted[3], groups)
+        send(4 + c, total)
+    for copy in copies:
+        copy.wait()
 
 
 def add_kernel(res_ref, adj_ref, back_ref, res_out, adj_out):
@@ -242,29 +268,51 @@
 
     exchange = functools.partial(lax.all_to_all, axis_name="gy", split_axis=0, concat_axis=0, tiled=True)
 
-    packed, last, lead = call(pack_kernel, [sent, face, face], [fields, cotangent], 0)
+    packed = pl.pallas_call(
+        pack_kernel,
+        out_shape=pltpu.VMEM(sent.shape, f32),
+        in_specs=[pl.BlockSpec(memory_space=pltpu.HBM)] * 2,
+        out_specs=pl.BlockSpec(memory_space=pltpu.VMEM),
+        scratch_shapes=[pltpu.VMEM((2,) + fields.shape, f32), pltpu.SemaphoreType.DMA((2,))],
+    )(fields, cotangent)
     gathered = exchange(packed)
-    (zed,) = call(zed_kernel, [like(cells, rows, lanes)], [fields, cotangent], 10**6)
+    last, lead, zed = call(
+        faces_kernel, [face, face, like(cells, rows, lanes)], [fields, cotangent], 10**6
+    )
     before = lax.ppermute(last, "gx", [(i, (i + 1) % gx) for i in range(gx)])
     after = lax.ppermute(lead, "gx", [((i + 1) % gx, i) for i in range(gx)])
     zed = lax.ppermute(zed, "gz", [(i, (i + 1) % gz) for i in range(gz)])
 
+    far = pl.BlockSpec(memory_space=pltpu.HBM)
     local_res, local_adj = pl.pallas_call(
         local_kernel,
-        out_shape=[block, block],
-        in_specs=[pl.BlockSpec(memory_space=pltpu.VMEM)] * 8 + [pl.BlockSpec(memory_space=pltpu.SMEM)],
-        scratch_shapes=[pltpu.VMEM((11, cells + 8, rows, lanes), f32)],
+        out_shape=[pltpu.VMEM(block.shape, f32)] * 2,
+        in_specs=[far] * 8 + [pl.BlockSpec(memory_space=pltpu.SMEM)],
+        scratch_shapes=[
+            pltpu.VMEM((11, cells + 8, rows, lanes), f32),
+            pltpu.VMEM((4, cells + 8, rows, lanes), f32),
+            pltpu.VMEM((3, cells, rows, lanes), f32),
+            pltpu.VMEM((cells, rows, lanes), f32),
+            pltpu.VMEM((rows, lanes), f32),
+            pltpu.VMEM((rows, lanes), f32),
+            pltpu.SemaphoreType.DMA((10,)),
+        ],
         cost_estimate=pl.CostEstimate(flops=2 * 10**7, bytes_accessed=6 * 10**6, transcendentals=0),
+    )(fields, previous, cotangent, before, after, zed, jnp.asarray(weight), jnp.asarray(wall), at)
+
+    matrices = [first, second, np.ascontiguousarray(first.T), np.ascontiguousarray(second.T), weight]
+    resident = pl.BlockSpec(memory_space=pltpu.VMEM)
+    lined = pl.pallas_call(
+        lines_kernel,
+        out_shape=like(groups, 8, rows, lanes),
+        in_specs=[resident] * 6,
+        out_specs=pl.BlockSpec(memory_space=pltpu.HBM),
+        scratch_shapes=[pltpu.VMEM((8, groups, rows, lanes), f32), pltpu.SemaphoreType.DMA((8,))],
+        cost_estimate=pl.CostEstimate(
+            flops=2 * points * points * lanes * 14 * 6, bytes_accessed=4 * 10**6, transcendentals=0
+        ),
         compiler_params=pltpu.CompilerParams(vmem_limit_bytes=VMEM_BYTES),
-    )(fields, previous, cotangent, before, after, zed, jnp.asarray(weight), jnp.asarray(wall), at)
-
-    matrices = [first, second, np.ascontiguousarray(first.T), np.ascontiguousarray(second.T), weight]
-    (lined,) = call(
-        lines_kernel,
-        [like(groups, 8, rows, lanes)],
-        [jnp.asarray(m) for m in matrices] + [gathered],
-        2 * points * points * lanes * 14 * 6,
-    )
+    )(*[jnp.asarray(m) for m in matrices], gathered)
     back = exchange(lined)
     residual, adjoint = call(add_kernel, [block, block], [local_res, local_adj, back], 10**6)
     return residual, adjoint

time: 75 us -> 73.2 us (0.976)
  local copies, waits for them, and re-layouts: 8.79 us -> 0.86 us
  waiting for transfers between devices: 6.36 us -> 10.7 us
  Pallas kernels: 11.6 us -> 13.5 us
    unnamed x36 -> x20, local copies, waits for them, and re-layouts: 8.79 us -> 0.86 us
    pallas_call x1 -> x3, Pallas kernels: 5.45 us -> 11.1 us  [the longest x1 6.99 us: per_device(): pl.pallas_call(local_kernel, out_shape=[pltpu.VMEM(block.shape, f32)] * 2...]
    all_to_all x1, waiting for transfers between devices: 1.3 us -> 5.7 us  [per_device(): back = exchange(lined)]
    pallas_call x4 -> x2, Pallas kernels: 6.18 us -> 2.46 us  [call(): pl.pallas_call(kernel, out_shape=outs, scratch_shapes=list(scratch), cost...]
  transfers between devices with their start and end apart: 4 -> 4, of which waited for: 2 -> 2; matrix products, arithmetic and copies ran while one was open for 0% -> 0% of each run, Pallas kernels for 9% -> 12%
where the time goes in v3:
time: 73.2 us; the launch traced here: 72.9 us
  blocking collectives  35.7 us (49%)
  Pallas kernels  13.5 us (18%)
  starting transfers between devices  11.3 us (15%)
  waiting for transfers between devices  10.7 us (15%)
  local copies, waits for them, and re-layouts  0.86 us (1%)
  between operations  0.77 us (1%)
    all_to_all x1, blocking collectives, per_device(): gathered = exchange(packed)  35.7 us
    pallas_call x1, Pallas kernels, per_device(): pl.pallas_call(local_kernel, out_shape=[pltpu.VMEM(block.shape, f32)] * 2...  6.99 us
    all_to_all x1, waiting for transfers between devices, per_device(): back = exchange(lined)  5.7 us
    all_to_all x1, starting transfers between devices, per_device(): back = exchange(lined)  5.41 us
    ppermute x1, waiting for transfers between devices, per_device(): zed = lax.ppermute(zed, 'gz', [(i, (i + 1) % gz) for i in range(gz)])  5.02 us
    ppermute x1, starting transfers between devices, per_device(): after = lax.ppermute(lead, 'gx', [((i + 1) % gx, i) for i in range(gx)])  2.94 us
    ppermute x1, starting transfers between devices, per_device(): zed = lax.ppermute(zed, 'gz', [(i, (i + 1) % gz) for i in range(gz)])  2.9 us
    pallas_call x1, Pallas kernels, per_device(): pl.pallas_call(lines_kernel, out_shape=like(groups, 8, rows, lanes), in_s...  2.82 us
  transfers between devices with their start and end apart: 4, of which 2 were waited for; matrix products, arithmetic and copies ran while one was open for 0% of the time, Pallas kernels for 12%

profile of v3, /device:TPU:32, one launch (start us, length us, event | category | flops | bytes accessed | tf_op | source)
XLA Modules:
  0.0 72.9 jit_solution(10705070651540022731)
XLA Ops:
  0.6 1.3 %shard_map.106 = f32[16,8,16,128]{3,2,1,0:T(8,128)S(1)} custom-call(f32[4,16,16,128]{3,2,1,0:T(8,128)} %fields_ref.3, f32[4,16,16,128]{3,2,1,0:T(8,128)} %cot_ref.3), custom_call_target="tpu_custom_call" | custom-call | tf_op jit(solution)/shard_map/pallas_call | solution.py:271
  1.9 0.0 copy-start.2
  1.9 0.0 copy-start.3
  1.9 0.0 copy-start.4
  1.9 0.0 copy-start.5
  1.9 0.0 copy-start.6
  2.0 35.7 %all_to_all.10.in_ref = f32[16,8,16,128]{3,2,1,0:T(8,128)S(1)} all-to-all(f32[16,8,16,128]{3,2,1,0:T(8,128)S(1)} %shard_map.106), channel_id=1, replica_groups=mesh['gy'=16,'gx'=8,'gz'=2] {'gy'}, dimensions={0} | all-to-all | bytes 2097152 | tf_op jit(solution)/shard_map/all_to_all | solution.py:278
  37.7 0.0 copy-done.2
  37.7 0.0 copy-done.3
  37.7 0.0 copy-done.4
  37.7 0.0 copy-done.5
  37.7 0.0 copy-done.6
  37.7 2.8 %shard_map.107 = f32[16,8,16,128]{3,2,1,0:T(8,128)} custom-call(f32[256,256]{1,0:T(8,128)S(1)} %copy-done.6, f32[256,256]{1,0:T(8,128)S(1)} %copy-done.5, f32[256,256]{1,0:T(8,128)S(1)} %copy-done.4, f32[256,256]{1,0:T(8,128)S(1)} %copy-done.3, f32[256,128]{1,0:T(8,128)S(1)} %copy-done.2, f32[16,8,16,128]{3,2,1,0:T(8,128)S(1)} %all_to_all.10.in_ref), custom_call_target="tpu_custom_call" | custom-call | flops 1409286144 | bytes 4000000 | tf_op jit(solution)/shard_map/pallas_call | solution.py:305
  40.6 0.0 copy-start
  40.6 0.0 copy-start.1
  40.6 5.4 %all-to-all-start.1 = ((f32[16,8,16,128]{3,2,1,0:T(8,128)}), f32[16,8,16,128]{3,2,1,0:T(8,128)S(1)}, u32[]{:S(2)}, u32[]{:S(2)}) async-start(f32[16,8,16,128]{3,2,1,0:T(8,128)} %shard_map.107), calls=%async_computation.1 | async-start | bytes 2097152 | tf_op jit(solution)/shard_map/all_to_all | solution.py:316
  46.0 0.0 copy-done
  46.0 0.0 copy-done.1
  46.0 1.4 %shard_map.104 = (f32[8,4,16,128]{3,2,1,0:T(8,128)S(1)}, f32[8,4,16,128]{3,2,1,0:T(8,128)S(1)}, f32[16,16,128]{2,1,0:T(8,128)S(1)}) custom-call(f32[4,16,16,128]{3,2,1,0:T(8,128)S(1)} %copy-done, f32[4,16,16,128]{3,2,1,0:T(8,128)S(1)} %copy-done.1), custom_call_target="tpu_custom_call" | custom-call | flops 1000000 | bytes 1703936 | tf_op jit(solution)/shard_map/pallas_call | solution.py:50
  47.4 0.0 collective-permute-start
  47.4 2.9 %collective-permute-start.1 = (f32[8,4,16,128]{3,2,1,0:T(8,128)S(1)}, f32[8,4,16,128]{3,2,1,0:T(8,128)S(1)}, u32[]{:S(2)}, u32[]{:S(2)}) collective-permute-start(f32[8,4,16,128]{3,2,1,0:T(8,128)S(1)} %get-tuple-element.8), channel_id=1, source_target_pairs={{2,0},{4,2},{6,4},{8,6},{10,8},{12,10},{14,12},{0,14},{3,1},{5,3},... | collective-permute-start | bytes 786440 | tf_op jit(solution)/shard_map/ppermute | solution.py:283
  50.4 2.9 %collective-permute-start.2 = (f32[16,16,128]{2,1,0:T(8,128)S(1)}, f32[16,16,128]{2,1,0:T(8,128)S(1)}, u32[]{:S(2)}, u32[]{:S(2)}) collective-permute-start(f32[16,16,128]{2,1,0:T(8,128)S(1)} %get-tuple-element.9), channel_id=1, source_target_pairs={{0,1},{1,0},{2,3},{3,2},{4,5},{5,4},{6,7},{7,6},{8,9},{9,8},{10,11... | collective-permute-start | bytes 393224 | tf_op jit(solution)/shard_map/ppermute | solution.py:284
  53.3 5.0 %collective-permute-done.2.zed_any = f32[16,16,128]{2,1,0:T(8,128)S(1)} collective-permute-done((f32[16,16,128]{2,1,0:T(8,128)S(1)}, f32[16,16,128]{2,1,0:T(8,128)S(1)}, u32[]{:S(2)}, u32[]{:S(2)}) %collective-permute-start.2) | collective-permute-done | bytes 131104 | tf_op jit(solution)/shard_map/ppermute | solution.py:284
  58.3 0.0 collective-permute-done.before_any
  58.3 0.0 collective-permute-done.1.after_any
  58.3 0.0 copy-start.8
  58.3 0.6 copy-done.9
  59.0 0.1 copy-done.7
  59.0 0.1 copy-done.8
  59.1 7.0 %shard_map.105 = (f32[4,16,16,128]{3,2,1,0:T(8,128)S(1)}, f32[4,16,16,128]{3,2,1,0:T(8,128)S(1)}) custom-call(f32[4,16,16,128]{3,2,1,0:T(8,128)} %fields_ref.3, f32[3,16,16,128]{3,2,1,0:T(8,128)} %prev_any.1, f32[4,16,16,128]{3,2,1,0:T(8,128)} %cot_ref.3, f32[8,4,16,128]{3,2,1,0:T(8,128)} %copy-done.7, f32[8,4,16,128]{3,2,1,0:T(8,128)} %copy-done.8, ...), custom_call_target="tpu_custom_call" | custom-call | flops 20000000 | bytes 6000000 | tf_op jit(solution)/shard_map/pallas_call | solution.py:287
  66.1 5.7 %all-to-all-done.1.back_ref = f32[16,8,16,128]{3,2,1,0:T(8,128)S(1)} async-done(((f32[16,8,16,128]{3,2,1,0:T(8,128)}), f32[16,8,16,128]{3,2,1,0:T(8,128)S(1)}, u32[]{:S(2)}, u32[]{:S(2)}) %all-to-all-start.1) | async-done | bytes 1048608 | tf_op jit(solution)/shard_map/all_to_all | solution.py:316
  71.8 1.1 %shard_map.108 = (f32[4,16,16,128]{3,2,1,0:T(8,128)}, f32[4,16,16,128]{3,2,1,0:T(8,128)}) custom-call(f32[4,16,16,128]{3,2,1,0:T(8,128)S(1)} %get-tuple-element.10.res_ref, f32[4,16,16,128]{3,2,1,0:T(8,128)S(1)} %get-tuple-element.11.adj_ref, f32[16,8,16,128]{3,2,1,0:T(8,128)S(1)} %all-to-all-done.1.back_ref), custom_call_target="tpu_custom_call" | custom-call | flops 1000000 | bytes 3145728 | tf_op jit(solution)/shard_map/pallas_call | solution.py:50
  (2 shorter events, 0.0 us)
Async XLA Ops:
  1.9 35.8 %copy-start.2 = (f32[256,128]{1,0:T(8,128)S(1)}, f32[256,128]{1,0:T(8,128)}, u32[]{:S(2)}) copy-start(f32[256,128]{1,0:T(8,128)} %constant.17.clone.weight_any.weight_ref) | copy-start | bytes 393220
  1.9 35.8 %copy-start.3 = (f32[256,256]{1,0:T(8,128)S(1)}, f32[256,256]{1,0:T(8,128)}, u32[]{:S(2)}) copy-start(f32[256,256]{1,0:T(8,128)} %constant.22.clone.second_t_ref) | copy-start | bytes 786436
  1.9 35.8 %copy-start.4 = (f32[256,256]{1,0:T(8,128)S(1)}, f32[256,256]{1,0:T(8,128)}, u32[]{:S(2)}) copy-start(f32[256,256]{1,0:T(8,128)} %constant.21.clone.first_t_ref) | copy-start | bytes 786436
  1.9 35.8 %copy-start.5 = (f32[256,256]{1,0:T(8,128)S(1)}, f32[256,256]{1,0:T(8,128)}, u32[]{:S(2)}) copy-start(f32[256,256]{1,0:T(8,128)} %constant.20.clone.second_ref) | copy-start | bytes 786436
  1.9 35.8 %copy-start.6 = (f32[256,256]{1,0:T(8,128)S(1)}, f32[256,256]{1,0:T(8,128)}, u32[]{:S(2)}) copy-start(f32[256,256]{1,0:T(8,128)} %constant.19.clone.first_ref) | copy-start | bytes 786436
  40.6 5.4 %copy-start = (f32[4,16,16,128]{3,2,1,0:T(8,128)S(1)}, f32[4,16,16,128]{3,2,1,0:T(8,128)}, u32[]{:S(2)}) copy-start(f32[4,16,16,128]{3,2,1,0:T(8,128)} %fields_ref.3) | copy-start | bytes 1572868
  40.6 5.4 %copy-start.1 = (f32[4,16,16,128]{3,2,1,0:T(8,128)S(1)}, f32[4,16,16,128]{3,2,1,0:T(8,128)}, u32[]{:S(2)}) copy-start(f32[4,16,16,128]{3,2,1,0:T(8,128)} %cot_ref.3) | copy-start | bytes 1572868
  40.6 31.3 %all-to-all-start.1 = ((f32[16,8,16,128]{3,2,1,0:T(8,128)}), f32[16,8,16,128]{3,2,1,0:T(8,128)S(1)}, u32[]{:S(2)}, u32[]{:S(2)}) async-start(f32[16,8,16,128]{3,2,1,0:T(8,128)} %shard_map.107), calls=%async_computation.1 | async-start | bytes 2097152 | tf_op jit(solution)/shard_map/all_to_all | solution.py:316
  47.4 10.9 %collective-permute-start = (f32[8,4,16,128]{3,2,1,0:T(8,128)S(1)}, f32[8,4,16,128]{3,2,1,0:T(8,128)S(1)}, u32[]{:S(2)}, u32[]{:S(2)}) collective-permute-start(f32[8,4,16,128]{3,2,1,0:T(8,128)S(1)} %get-tuple-element.7), channel_id=1, source_target_pairs={{0,2},{2,4},{4,6},{6,8},{8,10},{10,12},{12,14},{14,0},{1,3},{3,5},... | collective-permute-start | bytes 786440 | tf_op jit(solution)/shard_map/ppermute | solution.py:282
  47.4 10.9 %collective-permute-start.1 = (f32[8,4,16,128]{3,2,1,0:T(8,128)S(1)}, f32[8,4,16,128]{3,2,1,0:T(8,128)S(1)}, u32[]{:S(2)}, u32[]{:S(2)}) collective-permute-start(f32[8,4,16,128]{3,2,1,0:T(8,128)S(1)} %get-tuple-element.8), channel_id=1, source_target_pairs={{2,0},{4,2},{6,4},{8,6},{10,8},{12,10},{14,12},{0,14},{3,1},{5,3},... | collective-permute-start | bytes 786440 | tf_op jit(solution)/shard_map/ppermute | solution.py:283
  50.4 7.9 %collective-permute-start.2 = (f32[16,16,128]{2,1,0:T(8,128)S(1)}, f32[16,16,128]{2,1,0:T(8,128)S(1)}, u32[]{:S(2)}, u32[]{:S(2)}) collective-permute-start(f32[16,16,128]{2,1,0:T(8,128)S(1)} %get-tuple-element.9), channel_id=1, source_target_pairs={{0,1},{1,0},{2,3},{3,2},{4,5},{5,4},{6,7},{7,6},{8,9},{9,8},{10,11... | collective-permute-start | bytes 393224 | tf_op jit(solution)/shard_map/ppermute | solution.py:284
  58.3 0.7 copy-start.9
  58.3 0.7 %copy-start.7 = (f32[8,4,16,128]{3,2,1,0:T(8,128)}, f32[8,4,16,128]{3,2,1,0:T(8,128)S(1)}, u32[]{:S(2)}) copy-start(f32[8,4,16,128]{3,2,1,0:T(8,128)S(1)} %collective-permute-done.before_any) | copy-start | bytes 786436
  58.3 0.8 %copy-start.8 = (f32[8,4,16,128]{3,2,1,0:T(8,128)}, f32[8,4,16,128]{3,2,1,0:T(8,128)S(1)}, u32[]{:S(2)}) copy-start(f32[8,4,16,128]{3,2,1,0:T(8,128)S(1)} %collective-permute-done.1.after_any) | copy-start | bytes 786436

commit v4 on v3

v4 whole, which is shorter than its diff:
```python
import functools
import math

import jax
import jax.numpy as jnp
import numpy as np
from jax import lax
from jax.experimental import pallas as pl
from jax.experimental.pallas import tpu as pltpu
from jax.sharding import PartitionSpec as P

NU_VALUE = 0.001
STEP_DT = 0.1
SPACE_X = 8.0 * math.pi / 512.0
SPACE_Z = 3.0 * math.pi / 512.0
first_coeffs = (0.8, -0.2, 4.0 / 105.0, -1.0 / 280.0)
second_coeffs = (1.6, -0.2, 8.0 / 315.0, -1.0 / 560.0)
center_coeff = -205.0 / 72.0
VMEM_BYTES = 48 * 1024 * 1024
WIDE_BYTES = 60 * 1024 * 1024
EXACT = lax.Precision.HIGHEST
f32 = jnp.float32


def wall_matrices(points):
    final_row = points - 1
    j = np.arange(points)
    half = math.pi / (2.0 * final_row)
    spacing = -2.0 * np.sin(half * (j[:, None] + j[None, :])) * np.sin(half * (j[:, None] - j[None, :]))
    ends = np.where((j == 0) | (j == final_row), 2.0, 1.0) * np.where(j % 2 == 0, 1.0, -1.0)
    eye = np.eye(points, dtype=bool)
    entries = np.where(eye, 0.0, ends[:, None] / ends[None, :] / np.where(eye, 1.0, spacing))
    first = entries - np.diag(entries.sum(axis=1))
    second = first @ first
    return first.astype(np.float32), second.astype(np.float32)


def wall_profile(points):
    final_row = points - 1
    j = np.arange(points)
    weight = np.sin(j * (math.pi / final_row)) ** 4
    return np.repeat(weight[:, None], 128, 1).astype(np.float32)


def call(kernel, outs, args, flops, scratch=()):
    moved = sum(4 * math.prod(a.shape) for a in (*outs, *args))
    return pl.pallas_call(
        kernel,
        out_shape=outs,
        scratch_shapes=list(scratch),
        cost_estimate=pl.CostEstimate(flops=flops, bytes_accessed=moved, transcendentals=0),
        compiler_params=pltpu.CompilerParams(vmem_limit_bytes=VMEM_BYTES),
    )(*args)


def like(*shape):
    return jax.ShapeDtypeStruct(shape, f32)


def row_profile(at_ref, points, shape):
    row = at_ref[0] * shape[0] + lax.broadcasted_iota(jnp.int32, shape, 0)
    weight = jnp.sin(row.astype(f32) * (math.pi / (points - 1))) ** 4
    wall = jnp.where((row == 0) | (row == points - 1), 1.0, 0.0).astype(f32)
    return weight, wall


def load(pairs, sems):
    copies = [pltpu.make_async_copy(src, dst, sems.at[i]) for i, (src, dst) in enumerate(pairs)]
    for copy in copies:
        copy.start()
    for copy in copies:
        copy.wait()


def faces_kernel(fields_any, cot_any, _res, last_out, lead_out, sems):
    cells = fields_any.shape[1]
    load(
        [
            (fields_any.at[:, cells - 4 : cells], last_out.at[0:4]),
            (cot_any.at[:, cells - 4 : cells], last_out.at[4:8]),
            (fields_any.at[:, 0:4], lead_out.at[0:4]),
            (cot_any.at[:, 0:4], lead_out.at[4:8]),
        ],
        sems,
    )


def pack_faces(held, zed_out):
    def plane(x, _):
        lane = lax.broadcasted_iota(jnp.int32, zed_out.shape[1:], 1)
        total = jnp.zeros(zed_out.shape[1:], f32)
        for c in range(8):
            moved = pltpu.roll(held[c, x], 4 + 8 * c, 1)
            total = jnp.where((lane >= 8 * c) & (lane < 8 * c + 8), moved, total)
        zed_out[x] = total
        return 0

    lax.fori_loop(0, zed_out.shape[0], plane, 0, unroll=4)


def pack_kernel(fields_any, cot_any, sent_out, zed_out, held, in_sems, out_sems):
    ins, outs = [], []
    for c in range(4):
        for ref, slot in ((fields_any, c), (cot_any, 4 + c)):
            ins.append(pltpu.make_async_copy(ref.at[c], held.at[slot], in_sems.at[slot]))
            outs.append(pltpu.make_async_copy(held.at[slot], sent_out.at[:, slot], out_sems.at[slot]))
    for copy in ins:
        copy.start()
    for arrived, leaving in zip(ins, outs):
        arrived.wait()
        leaving.start()

    pack_faces(held, zed_out)
    for copy in outs:
        copy.wait()


def stencils(values, space, need_first, need_second):
    first = second = None
    if need_first:
        for k in range(4):
            term = (first_coeffs[k] / space) * (values[5 + k] - values[3 - k])
            first = term if first is None else first + term
    if need_second:
        second = (center_coeff / (space * space)) * values[4]
        for k in range(4):
            second = second + (second_coeffs[k] / (space * space)) * (values[5 + k] + values[3 - k])
    return first, second


def along_z_work(
    core, points, core_ref, at_ref, fields_any, prev_any, cot_any, zed_ref,
    res_ref, adj_ref, field_ref, cot_ref, prev_ref, sems,
):
    cells, rows, lanes = fields_any.shape[1:]

    @pl.when(core_ref[0] % 2 == core)
    def _():
        load([(fields_any, field_ref), (cot_any, cot_ref), (prev_any, prev_ref)], sems)
        weight, wall = row_profile(at_ref, points, (rows, lanes))

        def plane(x, _):
            lane = lax.broadcasted_iota(jnp.int32, (rows, lanes), 1)
            packed = zed_ref[x]
            u = [field_ref[c, x] for c in range(4)]
            w = [weight * cot_ref[c, x] for c in range(4)]
            far = [pltpu.roll(packed, (lanes - 4 - 8 * c) % lanes, 1) for c in range(8)]
            far_u = far[0:4]
            far_w = [weight * value for value in far[4:8]]

            def along(own, other, need_first, need_second):
                values = [None] * 9
                values[4] = own
                for k in range(1, 5):
                    values[4 + k] = pltpu.roll(jnp.where(lane < k, other, own), lanes - k, 1)
                    values[4 - k] = pltpu.roll(jnp.where(lane >= lanes - k, other, own), k, 1)
                return stencils(values, SPACE_Z, need_first, need_second)

            du = [along(u[c], far_u[c], True, c < 3) for c in range(4)]
            for c in range(3):
                moment = (u[c] - prev_ref[c, x]) * (1.0 / STEP_DT) + u[2] * du[c][0] - NU_VALUE * du[c][1]
                if c == 2:
                    moment = moment + du[3][0]
                res_ref[c, x] = weight * moment + wall * u[c]
            res_ref[3, x] = weight * du[2][0]
            dw = [along(w[c], far_w[c], c >= 2, c < 3) for c in range(4)]
            for c in range(3):
                flux = along(u[2] * w[c], far_u[2] * far_w[c], True, False)[0]
                total = w[c] * (1.0 / STEP_DT) - flux - NU_VALUE * dw[c][1] + wall * cot_ref[c, x]
                if c == 2:
                    stretch = w[0] * du[0][0] + w[1] * du[1][0] + w[2] * du[2][0]
                    total = total + stretch - dw[3][0]
                adj_ref[c, x] = total
            adj_ref[3, x] = -dw[2][0]
            return 0

        lax.fori_loop(0, cells, plane, 0)


def early_z_kernel(
    points, core_ref, at_ref, fields_any, prev_any, cot_any, zed_ref, _packed, _zed,
    _same, res_ref, adj_ref, _same_zed, *scratch,
):
    along_z_work(
        1, points, core_ref, at_ref, fields_any, prev_any, cot_any, zed_ref, res_ref, adj_ref, *scratch
    )


def late_z_kernel(
    points, core_ref, at_ref, fields_any, prev_any, cot_any, zed_ref, _res, _adj,
    res_ref, adj_ref, *scratch,
):
    along_z_work(
        0, points, core_ref, at_ref, fields_any, prev_any, cot_any, zed_ref, res_ref, adj_ref, *scratch
    )


def along_x_kernel(
    points, at_ref, fields_any, cot_any, before_any, after_any, _res, _adj,
    res_ref, adj_ref, ext, cot_ref, sems,
):
    cells, rows, lanes = fields_any.shape[1:]
    load(
        [
            (fields_any, ext.at[0:4, 4 : 4 + cells]),
            (before_any.at[0:4], ext.at[0:4, 0:4]),
            (after_any.at[0:4], ext.at[0:4, 4 + cells : 8 + cells]),
            (cot_any, cot_ref.at[:, 4 : 4 + cells]),
            (before_any.at[4:8], cot_ref.at[:, 0:4]),
            (after_any.at[4:8], cot_ref.at[:, 4 + cells : 8 + cells]),
        ],
        sems,
    )
    weight = row_profile(at_ref, points, (rows, lanes))[0]

    for c in range(4):
        for x in range(cells + 8):
            value = weight * cot_ref[c, x]
            ext[4 + c, x] = value
            if c < 3:
                ext[8 + c, x] = ext[0, x] * value

    def plane(x, _):
        def along(c, need_first, need_second):
            return stencils([ext[c, x + k] for k in range(9)], SPACE_X, need_first, need_second)

        u = ext[0, 4 + x]
        w = [ext[4 + c, 4 + x] for c in range(3)]
        du = [along(c, True, c < 3) for c in range(4)]
        for c in range(3):
            moment = u * du[c][0] - NU_VALUE * du[c][1]
            if c == 0:
                moment = moment + du[3][0]
            res_ref[c, x] += weight * moment
        res_ref[3, x] += weight * du[0][0]
        dw = [along(4 + c, c in (0, 3), c < 3) for c in range(4)]
        for c in range(3):
            total = -along(8 + c, True, False)[0] - NU_VALUE * dw[c][1]
            if c == 0:
                total = total + (w[0] * du[0][0] + w[1] * du[1][0] + w[2] * du[2][0]) - dw[3][0]
            adj_ref[c, x] += total
        adj_ref[3, x] += -dw[0][0]
        return 0

    lax.fori_loop(0, cells, plane, 0)


def lines(ref, c):
    groups, _, rows, lanes = ref.shape
    return ref[:, c].reshape(groups * rows, lanes)


def blocks(value, groups):
    return value.reshape(groups, value.shape[0] // groups, value.shape[1])


def product(matrix_ref, values):
    lanes = values[0].shape[1]
    wide = jnp.dot(
        matrix_ref[...], jnp.concatenate(values, axis=1), precision=EXACT, preferred_element_type=f32
    )
    return [wide[:, i * lanes : (i + 1) * lanes] for i in range(len(values))]


def lines_kernel(
    first_ref, second_ref, first_t_ref, second_t_ref, weight_ref, in_ref, _res, out_ref, held, sems
):
    groups = in_ref.shape[0]
    weight = weight_ref[...]
    copies = []

    def send(slot, value):
        held[slot] = blocks(value, groups)
        copies.append(pltpu.make_async_copy(held.at[slot], out_ref.at[:, slot], sems.at[slot]))
        copies[-1].start()

    u = [lines(in_ref, c) for c in range(4)]
    w = [weight * lines(in_ref, 4 + c) for c in range(4)]
    slope = product(first_ref, u)
    curve = product(second_ref, u[0:3])
    for c in range(3):
        total = u[1] * slope[c] - NU_VALUE * curve[c]
        if c == 1:
            total = total + slope[3]
        send(c, weight * total)
    send(3, weight * slope[1])
    stretch = w[0] * slope[0] + w[1] * slope[1] + w[2] * slope[2]
    lifted = product(first_t_ref, [u[1] * w[0], u[1] * w[1] + w[3], u[1] * w[2], w[1]])
    send(7, lifted[3])
    bent = product(second_t_ref, w[0:3])
    for c in range(3):
        total = lifted[c] - NU_VALUE * bent[c]
        if c == 1:
            total = total + stretch
        send(4 + c, total)
    for copy in copies:
        copy.wait()


def add_kernel(res_ref, adj_ref, back_ref, res_out, adj_out):
    for c in range(4):
        res_out[c] = res_ref[c] + back_ref[:, c]
        adj_out[c] = adj_ref[c] + back_ref[:, 4 + c]


def per_device(fields, previous, cotangent):
    cells, rows, lanes = fields.shape[1:]
    groups = lax.axis_size("gy")
    points = rows * groups
    first, second = wall_matrices(points)
    weight = wall_profile(points)
    sent = (cells, 8, rows, lanes)
    gx, gz = lax.axis_size("gx"), lax.axis_size("gz")
    at = lax.axis_index("gy").astype(jnp.int32).reshape(1)
    core_at = lax.axis_index("gx").astype(jnp.int32).reshape(1)
    exchange = functools.partial(lax.all_to_all, axis_name="gy", split_axis=0, concat_axis=0, tiled=True)
    far = pl.BlockSpec(memory_space=pltpu.HBM)
    near = pl.BlockSpec(memory_space=pltpu.VMEM)
    any_place = pl.BlockSpec(memory_space=pl.ANY)
    scalars = pl.BlockSpec(memory_space=pltpu.SMEM)
    plane = (rows, lanes)
    limit = pltpu.CompilerParams(vmem_limit_bytes=WIDE_BYTES)

    zed_shape = pltpu.VMEM((cells,) + plane, f32)
    held = pltpu.VMEM((8, cells) + plane, f32)

    def swap_zed(zed, core):
        pairs = [(x * gz + z, x * gz + (z + 1) % gz) for x in range(core, gx, 2) for z in range(gz)]
        return pltpu.with_memory_space_constraint(lax.ppermute(zed, ("gx", "gz"), pairs), pltpu.VMEM)

    packed, zed = pl.pallas_call(
        pack_kernel,
        out_shape=[like(*sent), zed_shape],
        in_specs=[far, far],
        out_specs=[far, near],
        scratch_shapes=[held, pltpu.SemaphoreType.DMA((8,)), pltpu.SemaphoreType.DMA((8,))],
        compiler_params=limit,
    )(fields, cotangent)

    z_scratch = [
        pltpu.VMEM((4, cells) + plane, f32),
        pltpu.VMEM((4, cells) + plane, f32),
        pltpu.VMEM((3, cells) + plane, f32),
        pltpu.SemaphoreType.DMA((3,)),
    ]
    part = pltpu.VMEM((4, cells) + plane, f32)
    cost = pl.CostEstimate(flops=2 * 10**7, bytes_accessed=6 * 10**6, transcendentals=0)

    packed, res, adj, zed_later = pl.pallas_call(
        functools.partial(early_z_kernel, points),
        out_shape=[like(*sent), part, part, zed_shape],
        in_specs=[scalars] * 2 + [far] * 3 + [near, far, near],
        out_specs=[far, near, near, near],
        scratch_shapes=z_scratch,
        input_output_aliases={6: 0, 7: 3},
        cost_estimate=cost,
        compiler_params=limit,
    )(core_at, at, fields, previous, cotangent, swap_zed(zed, 1), packed, zed)
    gathered = exchange(packed)

    res, adj = pl.pallas_call(
        functools.partial(late_z_kernel, points),
        out_shape=[part, part],
        in_specs=[scalars] * 2 + [far] * 3 + [near] * 3,
        scratch_shapes=z_scratch,
        input_output_aliases={6: 0, 7: 1},
        cost_estimate=cost,
        compiler_params=limit,
    )(core_at, at, fields, previous, cotangent, swap_zed(zed_later, 0), res, adj)

    matrices = [first, second, np.ascontiguousarray(first.T), np.ascontiguousarray(second.T), weight]
    resident = pl.BlockSpec(memory_space=pltpu.VMEM)
    lined = pl.pallas_call(
        lines_kernel,
        out_shape=like(groups, 8, rows, lanes),
        in_specs=[resident] * 7,
        out_specs=pl.BlockSpec(memory_space=pltpu.HBM),
        scratch_shapes=[pltpu.VMEM((8, groups, rows, lanes), f32), pltpu.SemaphoreType.DMA((8,))],
        cost_estimate=pl.CostEstimate(
            flops=2 * points * points * lanes * 14 * 6, bytes_accessed=4 * 10**6, transcendentals=0
        ),
        compiler_params=pltpu.CompilerParams(vmem_limit_bytes=VMEM_BYTES),
    )(*[jnp.asarray(m) for m in matrices], gathered, res)
    face = pltpu.VMEM((8, 4) + plane, f32)
    last, lead = pl.pallas_call(
        faces_kernel,
        out_shape=[face, face],
        in_specs=[far] * 2 + [any_place],
        out_specs=[near] * 2,
        scratch_shapes=[pltpu.SemaphoreType.DMA((4,))],
        compiler_params=limit,
    )(fields, cotangent, lined)
    before = lax.ppermute(last, "gx", [(i, (i + 1) % gx) for i in range(gx)])
    after = lax.ppermute(lead, "gx", [((i + 1) % gx, i) for i in range(gx)])
    res, adj = pl.pallas_call(
        functools.partial(along_x_kernel, points),
        out_shape=[part, part],
        in_specs=[scalars] + [far] * 2 + [near] * 4,
        scratch_shapes=[
            pltpu.VMEM((11, cells + 8) + plane, f32),
            pltpu.VMEM((4, cells + 8) + plane, f32),
            pltpu.SemaphoreType.DMA((6,)),
        ],
        input_output_aliases={5: 0, 6: 1},
        cost_estimate=cost,
        compiler_params=limit,
    )(at, fields, cotangent, before, after, res, adj)

    back = exchange(lined)
    block = like(4, cells, rows, lanes)
    residual, adjoint = call(add_kernel, [block, block], [res, adj, back], 10**6)
    return residual, adjoint


def solution(mesh):
    spec = P(None, "gx", "gy", "gz")
    return jax.shard_map(
        per_device, mesh=mesh, in_specs=(spec,) * 3, out_specs=(spec,) * 2, check_vma=False
    )
```

time: 73.2 us -> 70.5 us (0.963)
  the two profiles are of different devices: /device:TPU:32 before, /device:TPU:1 now
where the time goes in v4:
time: 70.5 us; the launch traced here: 70.1 us
  waiting for transfers between devices  30.6 us (43%)
  starting transfers between devices  20.6 us (29%)
  Pallas kernels  17.3 us (25%)
  between operations  0.79 us (1%)
  local copies, waits for them, and re-layouts  0.74 us (1%)
    all_to_all x1, waiting for transfers between devices, per_device(): gathered = exchange(packed)  15 us
    all_to_all x1, starting transfers between devices, per_device(): gathered = exchange(packed)  9.36 us
    all_to_all x1, waiting for transfers between devices, per_device(): back = exchange(lined)  7.65 us
    pallas_call x1, Pallas kernels, per_device(): pl.pallas_call(functools.partial(early_z_kernel, points), out_shape=[like...  6.67 us
    ppermute x2, starting transfers between devices, swap_zed(): lax.ppermute(zed, ('gx', 'gz'), pairs)  6.32 us
    all_to_all x1, starting transfers between devices, per_device(): back = exchange(lined)  4.44 us
    pallas_call x1, Pallas kernels, per_device(): pl.pallas_call(functools.partial(along_x_kernel, points), out_shape=[part...  3.48 us
    ppermute x1, waiting for transfers between devices, per_device(): before = lax.ppermute(last, 'gx', [(i, (i + 1) % gx) for i in range(gx)])  2.81 us
  transfers between devices with their start and end apart: 6, of which 5 were waited for; matrix products, arithmetic and copies ran while one was open for 0% of the time, Pallas kernels for 7%

profile of v4, /device:TPU:1, one launch (start us, length us, event | category | flops | bytes accessed | tf_op | source)
XLA Modules:
  0.0 70.1 jit_solution(17535018738754112248)
XLA Ops:
  0.6 2.1 %shard_map.95 = (f32[16,8,16,128]{3,2,1,0:T(8,128)}, f32[16,16,128]{2,1,0:T(8,128)S(1)}) custom-call(f32[4,16,16,128]{3,2,1,0:T(8,128)} %fields_any.9, f32[4,16,16,128]{3,2,1,0:T(8,128)} %cot_any.9), custom_call_target="tpu_custom_call" | custom-call | tf_op jit(solution)/shard_map/pallas_call | solution.py:331
  2.7 5.7 %collective-permute-start = (f32[16,16,128]{2,1,0:T(8,128)S(1)}, f32[16,16,128]{2,1,0:T(8,128)S(1)}, u32[]{:S(2)}, u32[]{:S(2)}) collective-permute-start(f32[16,16,128]{2,1,0:T(8,128)S(1)} %get-tuple-element.14._zed), channel_id=1, source_target_pairs={{2,3},{3,2},{6,7},{7,6},{10,11},{11,10},{14,15},{15,14},{18,19},{1... | collective-permute-start | bytes 393224 | tf_op jit(solution)/shard_map/ppermute | solution.py:329
  8.4 2.3 %collective-permute-done.zed_ref = f32[16,16,128]{2,1,0:T(8,128)S(1)} collective-permute-done((f32[16,16,128]{2,1,0:T(8,128)S(1)}, f32[16,16,128]{2,1,0:T(8,128)S(1)}, u32[]{:S(2)}, u32[]{:S(2)}) %collective-permute-start) | collective-permute-done | bytes 131104 | tf_op jit(solution)/shard_map/ppermute | solution.py:329
  10.7 6.7 %shard_map.96 = (f32[16,8,16,128]{3,2,1,0:T(8,128)}, f32[4,16,16,128]{3,2,1,0:T(8,128)S(1)}, f32[4,16,16,128]{3,2,1,0:T(8,128)S(1)}, f32[16,16,128]{2,1,0:T(8,128)S(1)}) custom-call(s32[1]{0:T(128)} %bitcast.1.core_ref, s32[1]{0:T(128)} %bitcast.at_ref, f32[4,16,16,128]{3,2,1,0:T(8,128)} %fields_any.9, ...), custom_call_target="tpu_custom_call", output_to_operand_aliasing={{0}: (6, {}), {3}: (7, {})} | custom-call | flops 20000000 | bytes 6000000 | tf_op jit(solution)/shard_map/pallas_call | solution.py:349
  17.4 9.4 %all-to-all-start = ((f32[16,8,16,128]{3,2,1,0:T(8,128)}), f32[16,8,16,128]{3,2,1,0:T(8,128)S(1)}, u32[]{:S(2)}, u32[]{:S(2)}) async-start(f32[16,8,16,128]{3,2,1,0:T(8,128)} %get-tuple-element.16), calls=%async_computation | async-start | bytes 2097152 | tf_op jit(solution)/shard_map/all_to_all | solution.py:359
  26.8 0.7 collective-permute-start.1
  27.5 0.0 collective-permute-done.1.zed_ref
  27.5 0.0 copy-start
  27.5 0.0 copy-start.1
  27.5 0.0 copy-start.2
  27.5 0.0 copy-start.3
  27.5 0.0 copy-start.4
  27.6 15.0 %all-to-all-done.in_ref = f32[16,8,16,128]{3,2,1,0:T(8,128)S(1)} async-done(((f32[16,8,16,128]{3,2,1,0:T(8,128)}), f32[16,8,16,128]{3,2,1,0:T(8,128)S(1)}, u32[]{:S(2)}, u32[]{:S(2)}) %all-to-all-start) | async-done | bytes 1048608 | tf_op jit(solution)/shard_map/all_to_all | solution.py:359
  42.6 0.0 copy-done
  42.6 0.0 copy-done.1
  42.6 0.0 copy-done.2
  42.6 0.0 copy-done.3
  42.6 0.0 copy-done.4
  42.6 2.8 %shard_map.98._res = f32[16,8,16,128]{3,2,1,0:T(8,128)} custom-call(f32[256,256]{1,0:T(8,128)S(1)} %copy-done.3, f32[256,256]{1,0:T(8,128)S(1)} %copy-done.2, f32[256,256]{1,0:T(8,128)S(1)} %copy-done.1, f32[256,256]{1,0:T(8,128)S(1)} %copy-done, f32[256,128]{1,0:T(8,128)S(1)} %copy-done.4, f32[16,8,16,128]{3,2,1,0:T(8,128)S(1)} %all-to-all-done.in_ref, ...), custom_call_target="tpu_custom_call" | custom-call | flops 1409286144 | bytes 4000000 | tf_op jit(solution)/shard_map/pallas_call | solution.py:373
  45.4 4.4 %all-to-all-start.1 = ((f32[16,8,16,128]{3,2,1,0:T(8,128)}), f32[16,8,16,128]{3,2,1,0:T(8,128)S(1)}, u32[]{:S(2)}, u32[]{:S(2)}) async-start(f32[16,8,16,128]{3,2,1,0:T(8,128)} %shard_map.98._res), calls=%async_computation.1 | async-start | bytes 2097152 | tf_op jit(solution)/shard_map/all_to_all | solution.py:409
  49.9 1.1 %shard_map.99 = (f32[8,4,16,128]{3,2,1,0:T(8,128)S(1)}, f32[8,4,16,128]{3,2,1,0:T(8,128)S(1)}) custom-call(f32[4,16,16,128]{3,2,1,0:T(8,128)} %fields_any.9, f32[4,16,16,128]{3,2,1,0:T(8,128)} %cot_any.9, f32[16,8,16,128]{3,2,1,0:T(8,128)} %shard_map.98._res), custom_call_target="tpu_custom_call" | custom-call | tf_op jit(solution)/shard_map/pallas_call | solution.py:385
  51.0 0.0 collective-permute-start.2
  51.0 0.5 collective-permute-start.3
  51.5 2.8 %collective-permute-done.2.before_any = f32[8,4,16,128]{3,2,1,0:T(8,128)S(1)} collective-permute-done((f32[8,4,16,128]{3,2,1,0:T(8,128)S(1)}, f32[8,4,16,128]{3,2,1,0:T(8,128)S(1)}, u32[]{:S(2)}, u32[]{:S(2)}) %collective-permute-start.2) | collective-permute-done | bytes 262176 | tf_op jit(solution)/shard_map/ppermute | solution.py:393
  54.4 0.0 copy-start.5
  54.4 2.8 %collective-permute-done.3.after_any = f32[8,4,16,128]{3,2,1,0:T(8,128)S(1)} collective-permute-done((f32[8,4,16,128]{3,2,1,0:T(8,128)S(1)}, f32[8,4,16,128]{3,2,1,0:T(8,128)S(1)}, u32[]{:S(2)}, u32[]{:S(2)}) %collective-permute-start.3) | collective-permute-done | bytes 262176 | tf_op jit(solution)/shard_map/ppermute | solution.py:394
  57.2 0.0 copy-start.6
  57.2 0.0 copy-done.5
  57.2 0.7 copy-done.6
  57.9 3.5 %shard_map.100 = (f32[4,16,16,128]{3,2,1,0:T(8,128)S(1)}, f32[4,16,16,128]{3,2,1,0:T(8,128)S(1)}) custom-call(s32[1]{0:T(128)} %bitcast.at_ref, f32[4,16,16,128]{3,2,1,0:T(8,128)} %fields_any.9, f32[4,16,16,128]{3,2,1,0:T(8,128)} %cot_any.9, f32[8,4,16,128]{3,2,1,0:T(8,128)} %copy-done.5, ...), custom_call_target="tpu_custom_call", output_to_operand_aliasing={{0}: (5, {}), {1}: (6, {})} | custom-call | flops 20000000 | bytes 6000000 | tf_op jit(solution)/shard_map/pallas_call | solution.py:395
  61.3 7.7 %all-to-all-done.1.back_ref = f32[16,8,16,128]{3,2,1,0:T(8,128)S(1)} async-done(((f32[16,8,16,128]{3,2,1,0:T(8,128)}), f32[16,8,16,128]{3,2,1,0:T(8,128)S(1)}, u32[]{:S(2)}, u32[]{:S(2)}) %all-to-all-start.1) | async-done | bytes 1048608 | tf_op jit(solution)/shard_map/all_to_all | solution.py:409
  69.0 1.1 %shard_map.101 = (f32[4,16,16,128]{3,2,1,0:T(8,128)}, f32[4,16,16,128]{3,2,1,0:T(8,128)}) custom-call(f32[4,16,16,128]{3,2,1,0:T(8,128)S(1)} %get-tuple-element.24.res_ref, f32[4,16,16,128]{3,2,1,0:T(8,128)S(1)} %get-tuple-element.25.adj_ref, f32[16,8,16,128]{3,2,1,0:T(8,128)S(1)} %all-to-all-done.1.back_ref), custom_call_target="tpu_custom_call" | custom-call | flops 1000000 | bytes 3145728 | tf_op jit(solution)/shard_map/pallas_call | solution.py:47
  (1 shorter events, 0.0 us)
Async XLA Ops:
  2.7 8.0 %collective-permute-start = (f32[16,16,128]{2,1,0:T(8,128)S(1)}, f32[16,16,128]{2,1,0:T(8,128)S(1)}, u32[]{:S(2)}, u32[]{:S(2)}) collective-permute-start(f32[16,16,128]{2,1,0:T(8,128)S(1)} %get-tuple-element.14._zed), channel_id=1, source_target_pairs={{2,3},{3,2},{6,7},{7,6},{10,11},{11,10},{14,15},{15,14},{18,19},{1... | collective-permute-start | bytes 393224 | tf_op jit(solution)/shard_map/ppermute | solution.py:329
  17.4 25.2 %all-to-all-start = ((f32[16,8,16,128]{3,2,1,0:T(8,128)}), f32[16,8,16,128]{3,2,1,0:T(8,128)S(1)}, u32[]{:S(2)}, u32[]{:S(2)}) async-start(f32[16,8,16,128]{3,2,1,0:T(8,128)} %get-tuple-element.16), calls=%async_computation | async-start | bytes 2097152 | tf_op jit(solution)/shard_map/all_to_all | solution.py:359
  26.8 0.7 collective-permute-start.1
  27.5 15.1 %copy-start = (f32[256,256]{1,0:T(8,128)S(1)}, f32[256,256]{1,0:T(8,128)}, u32[]{:S(2)}) copy-start(f32[256,256]{1,0:T(8,128)} %constant.24.clone.second_t_ref) | copy-start | bytes 786436
  27.5 15.1 %copy-start.1 = (f32[256,256]{1,0:T(8,128)S(1)}, f32[256,256]{1,0:T(8,128)}, u32[]{:S(2)}) copy-start(f32[256,256]{1,0:T(8,128)} %constant.23.clone.first_t_ref) | copy-start | bytes 786436
  27.5 15.1 %copy-start.2 = (f32[256,256]{1,0:T(8,128)S(1)}, f32[256,256]{1,0:T(8,128)}, u32[]{:S(2)}) copy-start(f32[256,256]{1,0:T(8,128)} %constant.22.clone.second_ref) | copy-start | bytes 786436
  27.5 15.1 %copy-start.3 = (f32[256,256]{1,0:T(8,128)S(1)}, f32[256,256]{1,0:T(8,128)}, u32[]{:S(2)}) copy-start(f32[256,256]{1,0:T(8,128)} %constant.21.clone.first_ref) | copy-start | bytes 786436
  27.5 15.1 %copy-start.4 = (f32[256,128]{1,0:T(8,128)S(1)}, f32[256,128]{1,0:T(8,128)}, u32[]{:S(2)}) copy-start(f32[256,128]{1,0:T(8,128)} %constant.25.clone.weight_ref) | copy-start | bytes 393220
  45.4 23.6 %all-to-all-start.1 = ((f32[16,8,16,128]{3,2,1,0:T(8,128)}), f32[16,8,16,128]{3,2,1,0:T(8,128)S(1)}, u32[]{:S(2)}, u32[]{:S(2)}) async-start(f32[16,8,16,128]{3,2,1,0:T(8,128)} %shard_map.98._res), calls=%async_computation.1 | async-start | bytes 2097152 | tf_op jit(solution)/shard_map/all_to_all | solution.py:409
  51.0 3.3 %collective-permute-start.2 = (f32[8,4,16,128]{3,2,1,0:T(8,128)S(1)}, f32[8,4,16,128]{3,2,1,0:T(8,128)S(1)}, u32[]{:S(2)}, u32[]{:S(2)}) collective-permute-start(f32[8,4,16,128]{3,2,1,0:T(8,128)S(1)} %get-tuple-element.21), channel_id=1, source_target_pairs={{0,2},{2,4},{4,6},{6,8},{8,10},{10,12},{12,14},{14,0},{1,3},{3,5},... | collective-permute-start | bytes 786440 | tf_op jit(solution)/shard_map/ppermute | solution.py:393
  51.0 6.1 %collective-permute-start.3 = (f32[8,4,16,128]{3,2,1,0:T(8,128)S(1)}, f32[8,4,16,128]{3,2,1,0:T(8,128)S(1)}, u32[]{:S(2)}, u32[]{:S(2)}) collective-permute-start(f32[8,4,16,128]{3,2,1,0:T(8,128)S(1)} %get-tuple-element.22), channel_id=1, source_target_pairs={{2,0},{4,2},{6,4},{8,6},{10,8},{12,10},{14,12},{0,14},{3,1},{5,3},... | collective-permute-start | bytes 786440 | tf_op jit(solution)/shard_map/ppermute | solution.py:394
  54.4 2.8 %copy-start.5 = (f32[8,4,16,128]{3,2,1,0:T(8,128)}, f32[8,4,16,128]{3,2,1,0:T(8,128)S(1)}, u32[]{:S(2)}) copy-start(f32[8,4,16,128]{3,2,1,0:T(8,128)S(1)} %collective-permute-done.2.before_any) | copy-start | bytes 786436
  57.2 0.7 %copy-start.6 = (f32[8,4,16,128]{3,2,1,0:T(8,128)}, f32[8,4,16,128]{3,2,1,0:T(8,128)S(1)}, u32[]{:S(2)}) copy-start(f32[8,4,16,128]{3,2,1,0:T(8,128)S(1)} %collective-permute-done.3.after_any) | copy-start | bytes 786436

commit v5 on v4

--- a/solution.py
+++ b/solution.py
@@ -72,7 +72,7 @@
         copy.wait()
 
 
-def faces_kernel(fields_any, cot_any, _res, last_out, lead_out, sems):
+def faces_kernel(fields_any, cot_any, _token, last_out, lead_out, sems):
     cells = fields_any.shape[1]
     load(
         [
@@ -174,7 +174,7 @@
             adj_ref[3, x] = -dw[2][0]
             return 0
 
-        lax.fori_loop(0, cells, plane, 0)
+        lax.fori_loop(0, cells, plane, 0, unroll=2)
 
 
 def early_z_kernel(
@@ -187,9 +187,10 @@
 
 
 def late_z_kernel(
-    points, core_ref, at_ref, fields_any, prev_any, cot_any, zed_ref, _res, _adj,
-    res_ref, adj_ref, *scratch,
+    points, core_ref, at_ref, fields_any, prev_any, cot_any, zed_ref, _res, _adj, _lined,
+    res_ref, adj_ref, token_ref, *scratch,
 ):
+    token_ref[...] = jnp.zeros_like(token_ref)
     along_z_work(
         0, points, core_ref, at_ref, fields_any, prev_any, cot_any, zed_ref, res_ref, adj_ref, *scratch
     )
@@ -263,7 +264,7 @@
 
 
 def lines_kernel(
-    first_ref, second_ref, first_t_ref, second_t_ref, weight_ref, in_ref, _res, out_ref, held, sems
+    first_ref, second_ref, first_t_ref, second_t_ref, weight_ref, in_ref, _zed, out_ref, held, sems
 ):
     groups = in_ref.shape[0]
     weight = weight_ref[...]
@@ -358,16 +359,7 @@
     )(core_at, at, fields, previous, cotangent, swap_zed(zed, 1), packed, zed)
     gathered = exchange(packed)
 
-    res, adj = pl.pallas_call(
-        functools.partial(late_z_kernel, points),
-        out_shape=[part, part],
-        in_specs=[scalars] * 2 + [far] * 3 + [near] * 3,
-        scratch_shapes=z_scratch,
-        input_output_aliases={6: 0, 7: 1},
-        cost_estimate=cost,
-        compiler_params=limit,
-    )(core_at, at, fields, previous, cotangent, swap_zed(zed_later, 0), res, adj)
-
+    even_zed = swap_zed(zed_later, 0)
     matrices = [first, second, np.ascontiguousarray(first.T), np.ascontiguousarray(second.T), weight]
     resident = pl.BlockSpec(memory_space=pltpu.VMEM)
     lined = pl.pallas_call(
@@ -380,16 +372,26 @@
             flops=2 * points * points * lanes * 14 * 6, bytes_accessed=4 * 10**6, transcendentals=0
         ),
         compiler_params=pltpu.CompilerParams(vmem_limit_bytes=VMEM_BYTES),
-    )(*[jnp.asarray(m) for m in matrices], gathered, res)
+    )(*[jnp.asarray(m) for m in matrices], gathered, even_zed)
+    res, adj, token = pl.pallas_call(
+        functools.partial(late_z_kernel, points),
+        out_shape=[part, part, pltpu.VMEM((8, lanes), f32)],
+        in_specs=[scalars] * 2 + [far] * 3 + [near] * 3 + [far],
+        scratch_shapes=z_scratch,
+        input_output_aliases={6: 0, 7: 1},
+        cost_estimate=cost,
+        compiler_params=limit,
+    )(core_at, at, fields, previous, cotangent, even_zed, res, adj, lined)
+
     face = pltpu.VMEM((8, 4) + plane, f32)
     last, lead = pl.pallas_call(
         faces_kernel,
         out_shape=[face, face],
-        in_specs=[far] * 2 + [any_place],
+        in_specs=[far] * 2 + [near],
         out_specs=[near] * 2,
         scratch_shapes=[pltpu.SemaphoreType.DMA((4,))],
         compiler_params=limit,
-    )(fields, cotangent, lined)
+    )(fields, cotangent, token)
     before = lax.ppermute(last, "gx", [(i, (i + 1) % gx) for i in range(gx)])
     after = lax.ppermute(lead, "gx", [((i + 1) % gx, i) for i in range(gx)])
     res, adj = pl.pallas_call(
@@ -404,7 +406,7 @@
         input_output_aliases={5: 0, 6: 1},
         cost_estimate=cost,
         compiler_params=limit,
-    )(at, fields, cotangent, before, after, res, adj)
+    )(at, fields, cotangent, *(pltpu.with_memory_space_constraint(v, pltpu.VMEM) for v in (before, after)), res, adj)
 
     back = exchange(lined)
     block = like(4, cells, rows, lanes)

time: 70.5 us -> 68.6 us (0.973)
  Pallas kernels: 17.3 us -> 16.4 us
  waiting for transfers between devices: 30.6 us -> 29.8 us
    all_to_all x1, waiting for transfers between devices: 7.65 us -> 6.46 us  [per_device(): back = exchange(lined)]
    pallas_call x1, Pallas kernels: 3.48 us -> 2.45 us  [per_device(): pl.pallas_call(functools.partial(along_x_kernel, points), out_shape=[part...]
  transfers between devices with their start and end apart: 6 -> 6, of which waited for: 5 -> 5; matrix products, arithmetic and copies ran while one was open for 0% -> 0% of each run, Pallas kernels for 7% -> 6%
where the time goes in v5:
time: 68.6 us; the launch traced here: 68.2 us
  waiting for transfers between devices  29.8 us (43%)
  starting transfers between devices  20.6 us (30%)
  Pallas kernels  16.4 us (24%)
  between operations  0.8 us (1%)
    all_to_all x1, waiting for transfers between devices, per_device(): gathered = exchange(packed)  15.4 us
    all_to_all x1, starting transfers between devices, per_device(): gathered = exchange(packed)  9.49 us
    all_to_all x1, waiting for transfers between devices, per_device(): back = exchange(lined)  6.46 us
    ppermute x2, starting transfers between devices, swap_zed(): lax.ppermute(zed, ('gx', 'gz'), pairs)  6.32 us
    pallas_call x1, Pallas kernels, per_device(): pl.pallas_call(functools.partial(early_z_kernel, points), out_shape=[like...  6.06 us
    all_to_all x1, starting transfers between devices, per_device(): back = exchange(lined)  4.24 us
    pallas_call x1, Pallas kernels, per_device(): pl.pallas_call(lines_kernel, out_shape=like(groups, 8, rows, lanes), in_s...  2.82 us
    ppermute x1, waiting for transfers between devices, per_device(): before = lax.ppermute(last, 'gx', [(i, (i + 1) % gx) for i in range(gx)])  2.81 us
  transfers between devices with their start and end apart: 6, of which 5 were waited for; matrix products, arithmetic and copies ran while one was open for 0% of the time, Pallas kernels for 6%

profile of v5, /device:TPU:1, one launch (start us, length us, event | category | flops | bytes accessed | tf_op | source)
XLA Modules:
  0.0 68.2 jit_solution(12421101971587680555)
XLA Ops:
  0.6 2.1 %shard_map.95 = (f32[16,8,16,128]{3,2,1,0:T(8,128)}, f32[16,16,128]{2,1,0:T(8,128)S(1)}) custom-call(f32[4,16,16,128]{3,2,1,0:T(8,128)} %fields_any.9, f32[4,16,16,128]{3,2,1,0:T(8,128)} %cot_any.9), custom_call_target="tpu_custom_call" | custom-call | tf_op jit(solution)/shard_map/pallas_call | solution.py:332
  2.8 5.7 %collective-permute-start = (f32[16,16,128]{2,1,0:T(8,128)S(1)}, f32[16,16,128]{2,1,0:T(8,128)S(1)}, u32[]{:S(2)}, u32[]{:S(2)}) collective-permute-start(f32[16,16,128]{2,1,0:T(8,128)S(1)} %get-tuple-element.15._zed), channel_id=1, source_target_pairs={{2,3},{3,2},{6,7},{7,6},{10,11},{11,10},{14,15},{15,14},{18,19},{1... | collective-permute-start | bytes 393224 | tf_op jit(solution)/shard_map/ppermute | solution.py:330
  8.4 2.3 %collective-permute-done.zed_ref = f32[16,16,128]{2,1,0:T(8,128)S(1)} collective-permute-done((f32[16,16,128]{2,1,0:T(8,128)S(1)}, f32[16,16,128]{2,1,0:T(8,128)S(1)}, u32[]{:S(2)}, u32[]{:S(2)}) %collective-permute-start) | collective-permute-done | bytes 131104 | tf_op jit(solution)/shard_map/ppermute | solution.py:330
  10.8 6.1 %shard_map.96 = (f32[16,8,16,128]{3,2,1,0:T(8,128)}, f32[4,16,16,128]{3,2,1,0:T(8,128)S(1)}, f32[4,16,16,128]{3,2,1,0:T(8,128)S(1)}, f32[16,16,128]{2,1,0:T(8,128)S(1)}) custom-call(s32[1]{0:T(128)} %bitcast.1.core_ref, s32[1]{0:T(128)} %bitcast.at_ref, f32[4,16,16,128]{3,2,1,0:T(8,128)} %fields_any.9, ...), custom_call_target="tpu_custom_call", output_to_operand_aliasing={{0}: (6, {}), {3}: (7, {})} | custom-call | flops 20000000 | bytes 6000000 | tf_op jit(solution)/shard_map/pallas_call | solution.py:350
  16.8 0.0 copy-start.1
  16.9 0.0 copy-start.2
  16.9 0.0 copy-start.3
  16.9 0.0 copy-start.4
  16.9 0.0 copy-start.5
  16.9 9.5 %all-to-all-start = ((f32[16,8,16,128]{3,2,1,0:T(8,128)}), f32[16,8,16,128]{3,2,1,0:T(8,128)S(1)}, u32[]{:S(2)}, u32[]{:S(2)}) async-start(f32[16,8,16,128]{3,2,1,0:T(8,128)} %get-tuple-element.20), calls=%async_computation | async-start | bytes 2097152 | tf_op jit(solution)/shard_map/all_to_all | solution.py:360
  26.4 0.7 collective-permute-start.1
  27.1 0.0 collective-permute-done.1._zed.zed_ref
  27.1 15.4 %all-to-all-done.in_ref = f32[16,8,16,128]{3,2,1,0:T(8,128)S(1)} async-done(((f32[16,8,16,128]{3,2,1,0:T(8,128)}), f32[16,8,16,128]{3,2,1,0:T(8,128)S(1)}, u32[]{:S(2)}, u32[]{:S(2)}) %all-to-all-start) | async-done | bytes 1048608 | tf_op jit(solution)/shard_map/all_to_all | solution.py:360
  42.5 0.0 copy-done.1
  42.5 0.0 copy-done.2
  42.5 0.0 copy-done.3
  42.5 0.0 copy-done.4
  42.5 0.0 copy-done.5
  42.5 2.8 %shard_map.97._lined = f32[16,8,16,128]{3,2,1,0:T(8,128)} custom-call(f32[256,256]{1,0:T(8,128)S(1)} %copy-done.4, f32[256,256]{1,0:T(8,128)S(1)} %copy-done.3, f32[256,256]{1,0:T(8,128)S(1)} %copy-done.2, f32[256,256]{1,0:T(8,128)S(1)} %copy-done.1, f32[256,128]{1,0:T(8,128)S(1)} %copy-done.5, f32[16,8,16,128]{3,2,1,0:T(8,128)S(1)} %all-to-all-done.in_ref, ...), custom_call_target="tpu_custom_call" | custom-call | flops 1409286144 | bytes 4000000 | tf_op jit(solution)/shard_map/pallas_call | solution.py:365
  45.4 4.2 %all-to-all-start.1 = ((f32[16,8,16,128]{3,2,1,0:T(8,128)}), f32[16,8,16,128]{3,2,1,0:T(8,128)S(1)}, u32[]{:S(2)}, u32[]{:S(2)}) async-start(f32[16,8,16,128]{3,2,1,0:T(8,128)} %shard_map.97._lined), calls=%async_computation.1 | async-start | bytes 2097152 | tf_op jit(solution)/shard_map/all_to_all | solution.py:411
  49.7 0.0 copy-start
  49.7 0.6 copy-done
  50.3 1.8 %shard_map.99 = (f32[8,4,16,128]{3,2,1,0:T(8,128)S(1)}, f32[8,4,16,128]{3,2,1,0:T(8,128)S(1)}) custom-call(f32[4,16,16,128]{3,2,1,0:T(8,128)} %fields_any.9, f32[4,16,16,128]{3,2,1,0:T(8,128)} %cot_any.9, f32[8,128]{1,0:T(8,128)} %copy-done), custom_call_target="tpu_custom_call" | custom-call | tf_op jit(solution)/shard_map/pallas_call | solution.py:387
  52.1 0.0 collective-permute-start.2
  52.1 0.5 collective-permute-start.3
  52.6 2.8 %collective-permute-done.2.before_any = f32[8,4,16,128]{3,2,1,0:T(8,128)S(1)} collective-permute-done((f32[8,4,16,128]{3,2,1,0:T(8,128)S(1)}, f32[8,4,16,128]{3,2,1,0:T(8,128)S(1)}, u32[]{:S(2)}, u32[]{:S(2)}) %collective-permute-start.2) | collective-permute-done | bytes 262176 | tf_op jit(solution)/shard_map/ppermute | solution.py:395
  55.4 2.8 %collective-permute-done.3.after_any = f32[8,4,16,128]{3,2,1,0:T(8,128)S(1)} collective-permute-done((f32[8,4,16,128]{3,2,1,0:T(8,128)S(1)}, f32[8,4,16,128]{3,2,1,0:T(8,128)S(1)}, u32[]{:S(2)}, u32[]{:S(2)}) %collective-permute-start.3) | collective-permute-done | bytes 262176 | tf_op jit(solution)/shard_map/ppermute | solution.py:396
  58.2 2.5 %shard_map.100 = (f32[4,16,16,128]{3,2,1,0:T(8,128)S(1)}, f32[4,16,16,128]{3,2,1,0:T(8,128)S(1)}) custom-call(s32[1]{0:T(128)} %bitcast.at_ref, f32[4,16,16,128]{3,2,1,0:T(8,128)} %fields_any.9, f32[4,16,16,128]{3,2,1,0:T(8,128)} %cot_any.9, f32[8,4,16,128]{3,2,1,0:T(8,128)S(1)} %collective-permute-done.2.before_any, ...), custom_call_target="tpu_custom_call", output_to_operand_aliasing={{0}: (5, {}), {1}: (6, {})} | custom-call | flops 20000000 | bytes 6000000 | tf_op jit(solution)/shard_map/pallas_call | solution.py:397
  60.7 6.5 %all-to-all-done.1.back_ref = f32[16,8,16,128]{3,2,1,0:T(8,128)S(1)} async-done(((f32[16,8,16,128]{3,2,1,0:T(8,128)}), f32[16,8,16,128]{3,2,1,0:T(8,128)S(1)}, u32[]{:S(2)}, u32[]{:S(2)}) %all-to-all-start.1) | async-done | bytes 1048608 | tf_op jit(solution)/shard_map/all_to_all | solution.py:411
  67.1 1.1 %shard_map.101 = (f32[4,16,16,128]{3,2,1,0:T(8,128)}, f32[4,16,16,128]{3,2,1,0:T(8,128)}) custom-call(f32[4,16,16,128]{3,2,1,0:T(8,128)S(1)} %get-tuple-element.26.res_ref, f32[4,16,16,128]{3,2,1,0:T(8,128)S(1)} %get-tuple-element.27.adj_ref, f32[16,8,16,128]{3,2,1,0:T(8,128)S(1)} %all-to-all-done.1.back_ref), custom_call_target="tpu_custom_call" | custom-call | flops 1000000 | bytes 3145728 | tf_op jit(solution)/shard_map/pallas_call | solution.py:47
  (1 shorter events, 0.0 us)
Async XLA Ops:
  2.8 8.0 %collective-permute-start = (f32[16,16,128]{2,1,0:T(8,128)S(1)}, f32[16,16,128]{2,1,0:T(8,128)S(1)}, u32[]{:S(2)}, u32[]{:S(2)}) collective-permute-start(f32[16,16,128]{2,1,0:T(8,128)S(1)} %get-tuple-element.15._zed), channel_id=1, source_target_pairs={{2,3},{3,2},{6,7},{7,6},{10,11},{11,10},{14,15},{15,14},{18,19},{1... | collective-permute-start | bytes 393224 | tf_op jit(solution)/shard_map/ppermute | solution.py:330
  16.8 25.7 %copy-start.1 = (f32[256,256]{1,0:T(8,128)S(1)}, f32[256,256]{1,0:T(8,128)}, u32[]{:S(2)}) copy-start(f32[256,256]{1,0:T(8,128)} %constant.24.clone.second_t_ref) | copy-start | bytes 786436
  16.9 25.7 %copy-start.2 = (f32[256,256]{1,0:T(8,128)S(1)}, f32[256,256]{1,0:T(8,128)}, u32[]{:S(2)}) copy-start(f32[256,256]{1,0:T(8,128)} %constant.23.clone.first_t_ref) | copy-start | bytes 786436
  16.9 25.7 %copy-start.3 = (f32[256,256]{1,0:T(8,128)S(1)}, f32[256,256]{1,0:T(8,128)}, u32[]{:S(2)}) copy-start(f32[256,256]{1,0:T(8,128)} %constant.22.clone.second_ref) | copy-start | bytes 786436
  16.9 25.6 %copy-start.4 = (f32[256,256]{1,0:T(8,128)S(1)}, f32[256,256]{1,0:T(8,128)}, u32[]{:S(2)}) copy-start(f32[256,256]{1,0:T(8,128)} %constant.21.clone.first_ref) | copy-start | bytes 786436
  16.9 25.6 %copy-start.5 = (f32[256,128]{1,0:T(8,128)S(1)}, f32[256,128]{1,0:T(8,128)}, u32[]{:S(2)}) copy-start(f32[256,128]{1,0:T(8,128)} %constant.25.clone.weight_ref) | copy-start | bytes 393220
  16.9 25.6 %all-to-all-start = ((f32[16,8,16,128]{3,2,1,0:T(8,128)}), f32[16,8,16,128]{3,2,1,0:T(8,128)S(1)}, u32[]{:S(2)}, u32[]{:S(2)}) async-start(f32[16,8,16,128]{3,2,1,0:T(8,128)} %get-tuple-element.20), calls=%async_computation | async-start | bytes 2097152 | tf_op jit(solution)/shard_map/all_to_all | solution.py:360
  26.4 0.7 collective-permute-start.1
  45.4 21.8 %all-to-all-start.1 = ((f32[16,8,16,128]{3,2,1,0:T(8,128)}), f32[16,8,16,128]{3,2,1,0:T(8,128)S(1)}, u32[]{:S(2)}, u32[]{:S(2)}) async-start(f32[16,8,16,128]{3,2,1,0:T(8,128)} %shard_map.97._lined), calls=%async_computation.1 | async-start | bytes 2097152 | tf_op jit(solution)/shard_map/all_to_all | solution.py:411
  49.7 0.6 copy-start
  52.1 3.3 %collective-permute-start.2 = (f32[8,4,16,128]{3,2,1,0:T(8,128)S(1)}, f32[8,4,16,128]{3,2,1,0:T(8,128)S(1)}, u32[]{:S(2)}, u32[]{:S(2)}) collective-permute-start(f32[8,4,16,128]{3,2,1,0:T(8,128)S(1)} %get-tuple-element.22), channel_id=1, source_target_pairs={{0,2},{2,4},{4,6},{6,8},{8,10},{10,12},{12,14},{14,0},{1,3},{3,5},... | collective-permute-start | bytes 786440 | tf_op jit(solution)/shard_map/ppermute | solution.py:395
  52.1 6.1 %collective-permute-start.3 = (f32[8,4,16,128]{3,2,1,0:T(8,128)S(1)}, f32[8,4,16,128]{3,2,1,0:T(8,128)S(1)}, u32[]{:S(2)}, u32[]{:S(2)}) collective-permute-start(f32[8,4,16,128]{3,2,1,0:T(8,128)S(1)} %get-tuple-element.23), channel_id=1, source_target_pairs={{2,0},{4,2},{6,4},{8,6},{10,8},{12,10},{14,12},{0,14},{3,1},{5,3},... | collective-permute-start | bytes 786440 | tf_op jit(solution)/shard_map/ppermute | solution.py:396

commit v6 on v5

--- a/solution.py
+++ b/solution.py
@@ -72,47 +72,52 @@
         copy.wait()
 
 
-def faces_kernel(fields_any, cot_any, _token, last_out, lead_out, sems):
-    cells = fields_any.shape[1]
-    load(
-        [
-            (fields_any.at[:, cells - 4 : cells], last_out.at[0:4]),
-            (cot_any.at[:, cells - 4 : cells], last_out.at[4:8]),
-            (fields_any.at[:, 0:4], lead_out.at[0:4]),
-            (cot_any.at[:, 0:4], lead_out.at[4:8]),
-        ],
-        sems,
-    )
-
-
-def pack_faces(held, zed_out):
+def z_faces(held, zed_out):
+    half = zed_out.shape[0]
+
     def plane(x, _):
         lane = lax.broadcasted_iota(jnp.int32, zed_out.shape[1:], 1)
         total = jnp.zeros(zed_out.shape[1:], f32)
         for c in range(8):
-            moved = pltpu.roll(held[c, x], 4 + 8 * c, 1)
-            total = jnp.where((lane >= 8 * c) & (lane < 8 * c + 8), moved, total)
+            for side in range(2):
+                at = 8 * c + 64 * side
+                moved = pltpu.roll(held[c, x + half * side], 4 + at, 1)
+                total = jnp.where((lane >= at) & (lane < at + 8), moved, total)
         zed_out[x] = total
         return 0
 
-    lax.fori_loop(0, zed_out.shape[0], plane, 0, unroll=4)
-
-
-def pack_kernel(fields_any, cot_any, sent_out, zed_out, held, in_sems, out_sems):
-    ins, outs = [], []
-    for c in range(4):
-        for ref, slot in ((fields_any, c), (cot_any, 4 + c)):
-            ins.append(pltpu.make_async_copy(ref.at[c], held.at[slot], in_sems.at[slot]))
-            outs.append(pltpu.make_async_copy(held.at[slot], sent_out.at[:, slot], out_sems.at[slot]))
-    for copy in ins:
+    lax.fori_loop(0, half, plane, 0, unroll=2)
+
+
+def pack_kernel(core_ref, fields_any, cot_any, sent_out, zed_out, last_out, lead_out, held, sems):
+    cells = fields_any.shape[1]
+    copies = [
+        pltpu.make_async_copy(fields_any, held.at[0:4], sems.at[0]),
+        pltpu.make_async_copy(cot_any, held.at[4:8], sems.at[1]),
+    ]
+    for copy in copies:
         copy.start()
-    for arrived, leaving in zip(ins, outs):
-        arrived.wait()
-        leaving.start()
-
-    pack_faces(held, zed_out)
-    for copy in outs:
+    for part, copy in enumerate(copies):
         copy.wait()
+        for c in range(4 * part, 4 * part + 4):
+            sent_out[:, c] = held[c]
+            last_out[c] = held[c, cells - 4 : cells]
+            lead_out[c] = held[c, 0:4]
+
+    @pl.when(core_ref[0] % 2 == 1)
+    def _():
+        z_faces(held, zed_out)
+
+
+def late_faces_kernel(core_ref, fields_any, cot_any, _lined, zed_out, held, sems):
+    @pl.when(core_ref[0] % 2 == 0)
+    def _():
+        load([(fields_any, held.at[0:4]), (cot_any, held.at[4:8])], sems)
+        z_faces(held, zed_out)
+
+
+def order_kernel(_zed, _last, _lead, _same_last, _same_lead):
+    pass
 
 
 def stencils(values, space, need_first, need_second):
@@ -133,18 +138,20 @@
     res_ref, adj_ref, field_ref, cot_ref, prev_ref, sems,
 ):
     cells, rows, lanes = fields_any.shape[1:]
+    half = cells // 2
 
     @pl.when(core_ref[0] % 2 == core)
     def _():
         load([(fields_any, field_ref), (cot_any, cot_ref), (prev_any, prev_ref)], sems)
         weight, wall = row_profile(at_ref, points, (rows, lanes))
 
-        def plane(x, _):
+        def plane(side, step, _):
+            x = step + half * side
             lane = lax.broadcasted_iota(jnp.int32, (rows, lanes), 1)
-            packed = zed_ref[x]
+            packed = zed_ref[step]
             u = [field_ref[c, x] for c in range(4)]
             w = [weight * cot_ref[c, x] for c in range(4)]
-            far = [pltpu.roll(packed, (lanes - 4 - 8 * c) % lanes, 1) for c in range(8)]
+            far = [pltpu.roll(packed, (lanes - 4 - 8 * c - 64 * side) % lanes, 1) for c in range(8)]
             far_u = far[0:4]
             far_w = [weight * value for value in far[4:8]]
 
@@ -174,12 +181,13 @@
             adj_ref[3, x] = -dw[2][0]
             return 0
 
-        lax.fori_loop(0, cells, plane, 0, unroll=2)
+        for side in range(2):
+            lax.fori_loop(0, half, functools.partial(plane, side), 0, unroll=1 + (core == 0))
 
 
 def early_z_kernel(
-    points, core_ref, at_ref, fields_any, prev_any, cot_any, zed_ref, _packed, _zed,
-    _same, res_ref, adj_ref, _same_zed, *scratch,
+    points, core_ref, at_ref, fields_any, prev_any, cot_any, zed_ref, _packed,
+    _same, res_ref, adj_ref, *scratch,
 ):
     along_z_work(
         1, points, core_ref, at_ref, fields_any, prev_any, cot_any, zed_ref, res_ref, adj_ref, *scratch
@@ -187,10 +195,9 @@
 
 
 def late_z_kernel(
-    points, core_ref, at_ref, fields_any, prev_any, cot_any, zed_ref, _res, _adj, _lined,
-    res_ref, adj_ref, token_ref, *scratch,
+    points, core_ref, at_ref, fields_any, prev_any, cot_any, zed_ref, _res, _adj,
+    res_ref, adj_ref, *scratch,
 ):
-    token_ref[...] = jnp.zeros_like(token_ref)
     along_z_work(
         0, points, core_ref, at_ref, fields_any, prev_any, cot_any, zed_ref, res_ref, adj_ref, *scratch
     )
@@ -264,7 +271,7 @@
 
 
 def lines_kernel(
-    first_ref, second_ref, first_t_ref, second_t_ref, weight_ref, in_ref, _zed, out_ref, held, sems
+    first_ref, second_ref, first_t_ref, second_t_ref, weight_ref, in_ref, out_ref, held, sems
 ):
     groups = in_ref.shape[0]
     weight = weight_ref[...]
@@ -322,21 +329,21 @@
     plane = (rows, lanes)
     limit = pltpu.CompilerParams(vmem_limit_bytes=WIDE_BYTES)
 
-    zed_shape = pltpu.VMEM((cells,) + plane, f32)
-    held = pltpu.VMEM((8, cells) + plane, f32)
+    zed_shape = pltpu.VMEM((cells // 2,) + plane, f32)
+    face = pltpu.VMEM((8, 4) + plane, f32)
 
     def swap_zed(zed, core):
         pairs = [(x * gz + z, x * gz + (z + 1) % gz) for x in range(core, gx, 2) for z in range(gz)]
         return pltpu.with_memory_space_constraint(lax.ppermute(zed, ("gx", "gz"), pairs), pltpu.VMEM)
 
-    packed, zed = pl.pallas_call(
+    packed, zed, last, lead = pl.pallas_call(
         pack_kernel,
-        out_shape=[like(*sent), zed_shape],
-        in_specs=[far, far],
-        out_specs=[far, near],
-        scratch_shapes=[held, pltpu.SemaphoreType.DMA((8,)), pltpu.SemaphoreType.DMA((8,))],
-        compiler_params=limit,
-    )(fields, cotangent)
+        out_shape=[pltpu.VMEM(sent, f32), zed_shape, face, face],
+        in_specs=[scalars, far, far],
+        out_specs=[near] * 4,
+        scratch_shapes=[pltpu.VMEM((8, cells) + plane, f32), pltpu.SemaphoreType.DMA((2,))],
+        compiler_params=limit,
+    )(core_at, fields, cotangent)
 
     z_scratch = [
         pltpu.VMEM((4, cells) + plane, f32),
@@ -347,51 +354,58 @@
     part = pltpu.VMEM((4, cells) + plane, f32)
     cost = pl.CostEstimate(flops=2 * 10**7, bytes_accessed=6 * 10**6, transcendentals=0)
 
-    packed, res, adj, zed_later = pl.pallas_call(
+    packed, res, adj = pl.pallas_call(
         functools.partial(early_z_kernel, points),
-        out_shape=[like(*sent), part, part, zed_shape],
-        in_specs=[scalars] * 2 + [far] * 3 + [near, far, near],
-        out_specs=[far, near, near, near],
+        out_shape=[pltpu.VMEM(sent, f32), part, part],
+        in_specs=[scalars] * 2 + [far] * 3 + [near] * 2,
+        out_specs=[near] * 3,
         scratch_shapes=z_scratch,
-        input_output_aliases={6: 0, 7: 3},
+        input_output_aliases={6: 0},
         cost_estimate=cost,
         compiler_params=limit,
-    )(core_at, at, fields, previous, cotangent, swap_zed(zed, 1), packed, zed)
+    )(core_at, at, fields, previous, cotangent, swap_zed(zed, 1), packed)
     gathered = exchange(packed)
 
-    even_zed = swap_zed(zed_later, 0)
     matrices = [first, second, np.ascontiguousarray(first.T), np.ascontiguousarray(second.T), weight]
     resident = pl.BlockSpec(memory_space=pltpu.VMEM)
     lined = pl.pallas_call(
         lines_kernel,
         out_shape=like(groups, 8, rows, lanes),
-        in_specs=[resident] * 7,
-        out_specs=pl.BlockSpec(memory_space=pltpu.HBM),
+        in_specs=[resident] * 6,
+        out_specs=far,
         scratch_shapes=[pltpu.VMEM((8, groups, rows, lanes), f32), pltpu.SemaphoreType.DMA((8,))],
         cost_estimate=pl.CostEstimate(
             flops=2 * points * points * lanes * 14 * 6, bytes_accessed=4 * 10**6, transcendentals=0
         ),
         compiler_params=pltpu.CompilerParams(vmem_limit_bytes=VMEM_BYTES),
-    )(*[jnp.asarray(m) for m in matrices], gathered, even_zed)
-    res, adj, token = pl.pallas_call(
+    )(*[jnp.asarray(m) for m in matrices], gathered)
+
+    zed_later = pl.pallas_call(
+        late_faces_kernel,
+        out_shape=zed_shape,
+        in_specs=[scalars] + [far] * 3,
+        scratch_shapes=[pltpu.VMEM((8, cells) + plane, f32), pltpu.SemaphoreType.DMA((2,))],
+        cost_estimate=cost,
+        compiler_params=limit,
+    )(core_at, fields, cotangent, lined)
+    even_zed = swap_zed(zed_later, 0)
+    last, lead = pl.pallas_call(
+        order_kernel,
+        out_shape=[face, face],
+        in_specs=[near] * 3,
+        input_output_aliases={1: 0, 2: 1},
+        compiler_params=limit,
+    )(even_zed, last, lead)
+    res, adj = pl.pallas_call(
         functools.partial(late_z_kernel, points),
-        out_shape=[part, part, pltpu.VMEM((8, lanes), f32)],
-        in_specs=[scalars] * 2 + [far] * 3 + [near] * 3 + [far],
+        out_shape=[part, part],
+        in_specs=[scalars] * 2 + [far] * 3 + [near] * 3,
         scratch_shapes=z_scratch,
         input_output_aliases={6: 0, 7: 1},
         cost_estimate=cost,
         compiler_params=limit,
-    )(core_at, at, fields, previous, cotangent, even_zed, res, adj, lined)
-
-    face = pltpu.VMEM((8, 4) + plane, f32)
-    last, lead = pl.pallas_call(
-        faces_kernel,
-        out_shape=[face, face],
-        in_specs=[far] * 2 + [near],
-        out_specs=[near] * 2,
-        scratch_shapes=[pltpu.SemaphoreType.DMA((4,))],
-        compiler_params=limit,
-    )(fields, cotangent, token)
+    )(core_at, at, fields, previous, cotangent, even_zed, res, adj)
+
     before = lax.ppermute(last, "gx", [(i, (i + 1) % gx) for i in range(gx)])
     after = lax.ppermute(lead, "gx", [((i + 1) % gx, i) for i in range(gx)])
     res, adj = pl.pallas_call(

time: 68.6 us -> 67.7 us (0.987)
  blocking collectives: 0 us -> 25.9 us
  waiting for transfers between devices: 29.8 us -> 15 us
  starting transfers between devices: 20.6 us -> 10.8 us
  Pallas kernels: 16.4 us -> 14.9 us
    all_to_all x0 -> x1, blocking collectives: none -> 25.9 us  [per_device(): gathered = exchange(packed)]
    all_to_all x1 -> x0, waiting for transfers between devices: 15.4 us -> none  [per_device(): gathered = exchange(packed)]
    all_to_all x1 -> x0, starting transfers between devices: 9.49 us -> none  [per_device(): gathered = exchange(packed)]
    pallas_call x3 -> x4, Pallas kernels: 10 us -> 8.52 us  [the longest x1 6.67 us: per_device(): pl.pallas_call(functools.partial(early_z_kernel, points), out_shape=[pltp...]
    all_to_all x1, waiting for transfers between devices: 6.46 us -> 7.77 us  [per_device(): back = exchange(lined)]
    ppermute x2, waiting for transfers between devices: 2.34 us -> 1.64 us  [swap_zed(): lax.ppermute(zed, ('gx', 'gz'), pairs)]
  transfers between devices with their start and end apart: 6 -> 5, of which waited for: 5 -> 4; matrix products, arithmetic and copies ran while one was open for 0% -> 0% of each run, Pallas kernels for 6% -> 4%
where the time goes in v6:
time: 67.7 us; the launch traced here: 67.3 us
  blocking collectives  25.9 us (38%)
  waiting for transfers between devices  15 us (22%)
  Pallas kernels  14.9 us (22%)
  starting transfers between devices  10.8 us (16%)
  between operations  0.8 us (1%)
    all_to_all x1, blocking collectives, per_device(): gathered = exchange(packed)  25.9 us
    all_to_all x1, waiting for transfers between devices, per_device(): back = exchange(lined)  7.77 us
    pallas_call x1, Pallas kernels, per_device(): pl.pallas_call(functools.partial(early_z_kernel, points), out_shape=[pltp...  6.67 us
    ppermute x2, starting transfers between devices, swap_zed(): lax.ppermute(zed, ('gx', 'gz'), pairs)  6.32 us
    all_to_all x1, starting transfers between devices, per_device(): back = exchange(lined)  3.92 us
    pallas_call x1, Pallas kernels, per_device(): pl.pallas_call(lines_kernel, out_shape=like(groups, 8, rows, lanes), in_s...  2.81 us
    ppermute x1, waiting for transfers between devices, per_device(): after = lax.ppermute(lead, 'gx', [((i + 1) % gx, i) for i in range(gx)])  2.79 us
    ppermute x1, waiting for transfers between devices, per_device(): before = lax.ppermute(last, 'gx', [(i, (i + 1) % gx) for i in range(gx)])  2.78 us
  transfers between devices with their start and end apart: 5, of which 4 were waited for; matrix products, arithmetic and copies ran while one was open for 0% of the time, Pallas kernels for 4%

profile of v6, /device:TPU:1, one launch (start us, length us, event | category | flops | bytes accessed | tf_op | source)
XLA Modules:
  0.0 67.3 jit_solution(7193240381028353580)
XLA Ops:
  0.6 1.8 %shard_map.95 = (f32[16,8,16,128]{3,2,1,0:T(8,128)S(1)}, f32[8,16,128]{2,1,0:T(8,128)S(1)}, f32[8,4,16,128]{3,2,1,0:T(8,128)S(1)}, f32[8,4,16,128]{3,2,1,0:T(8,128)S(1)}) custom-call(s32[1]{0:T(128)} %bitcast.1.core_ref, f32[4,16,16,128]{3,2,1,0:T(8,128)} %fields_any.9, f32[4,16,16,128]{3,2,1,0:T(8,128)} %cot_any.9), custom_call_target="tpu_custom_call" | custom-call | tf_op jit(solution)/shard_map/pallas_call | solution.py:339
  2.5 5.7 %collective-permute-start = (f32[8,16,128]{2,1,0:T(8,128)S(1)}, f32[8,16,128]{2,1,0:T(8,128)S(1)}, u32[]{:S(2)}, u32[]{:S(2)}) collective-permute-start(f32[8,16,128]{2,1,0:T(8,128)S(1)} %get-tuple-element.15), channel_id=1, source_target_pairs={{2,3},{3,2},{6,7},{7,6},{10,11},{11,10},{14,15},{15,14},{18,19},{1... | collective-permute-start | bytes 196616 | tf_op jit(solution)/shard_map/ppermute | solution.py:337
  8.1 1.6 %collective-permute-done.zed_ref = f32[8,16,128]{2,1,0:T(8,128)S(1)} collective-permute-done((f32[8,16,128]{2,1,0:T(8,128)S(1)}, f32[8,16,128]{2,1,0:T(8,128)S(1)}, u32[]{:S(2)}, u32[]{:S(2)}) %collective-permute-start) | collective-permute-done | bytes 65568 | tf_op jit(solution)/shard_map/ppermute | solution.py:337
  9.8 6.7 %shard_map.96 = (f32[16,8,16,128]{3,2,1,0:T(8,128)S(1)}, f32[4,16,16,128]{3,2,1,0:T(8,128)S(1)}, f32[4,16,16,128]{3,2,1,0:T(8,128)S(1)}) custom-call(s32[1]{0:T(128)} %bitcast.1.core_ref, s32[1]{0:T(128)} %bitcast.at_ref, f32[4,16,16,128]{3,2,1,0:T(8,128)} %fields_any.9, f32[3,16,16,128]{3,2,1,0:T(8,128)} %prev_any.3, ...), custom_call_target="tpu_custom_call", output_to_operand_aliasing={{0}: (6, {})} | custom-call | flops 20000000 | bytes 6000000 | tf_op jit(solution)/shard_map/pallas_call | solution.py:357
  16.4 0.0 copy-start
  16.4 0.0 copy-start.1
  16.5 0.0 copy-start.2
  16.5 0.0 copy-start.3
  16.5 0.0 copy-start.4
  16.5 25.9 %all_to_all.10.in_ref = f32[16,8,16,128]{3,2,1,0:T(8,128)S(1)} all-to-all(f32[16,8,16,128]{3,2,1,0:T(8,128)S(1)} %get-tuple-element.17), channel_id=1, replica_groups=mesh['gy'=16,'gx'=8,'gz'=2] {'gy'}, dimensions={0} | all-to-all | bytes 2097152 | tf_op jit(solution)/shard_map/all_to_all | solution.py:367
  42.4 0.0 copy-done
  42.4 0.0 copy-done.1
  42.4 0.0 copy-done.2
  42.4 0.0 copy-done.3
  42.4 0.0 copy-done.4
  42.4 2.8 %shard_map.97._lined = f32[16,8,16,128]{3,2,1,0:T(8,128)} custom-call(f32[256,256]{1,0:T(8,128)S(1)} %copy-done.3, f32[256,256]{1,0:T(8,128)S(1)} %copy-done.2, f32[256,256]{1,0:T(8,128)S(1)} %copy-done.1, f32[256,256]{1,0:T(8,128)S(1)} %copy-done, f32[256,128]{1,0:T(8,128)S(1)} %copy-done.4, f32[16,8,16,128]{3,2,1,0:T(8,128)S(1)} %all_to_all.10.in_ref), custom_call_target="tpu_custom_call" | custom-call | flops 1409286144 | bytes 4000000 | tf_op jit(solution)/shard_map/pallas_call | solution.py:371
  45.2 3.9 %all-to-all-start.1 = ((f32[16,8,16,128]{3,2,1,0:T(8,128)}), f32[16,8,16,128]{3,2,1,0:T(8,128)S(1)}, u32[]{:S(2)}, u32[]{:S(2)}) async-start(f32[16,8,16,128]{3,2,1,0:T(8,128)} %shard_map.97._lined), calls=%async_computation.1 | async-start | bytes 2097152 | tf_op jit(solution)/shard_map/all_to_all | solution.py:425
  49.2 0.7 collective-permute-start.1
  49.9 0.0 collective-permute-done.1._zed.zed_ref
  49.9 0.0 collective-permute-start.2
  49.9 0.5 collective-permute-start.3
  50.5 2.8 %collective-permute-done.2.before_any = f32[8,4,16,128]{3,2,1,0:T(8,128)S(1)} collective-permute-done((f32[8,4,16,128]{3,2,1,0:T(8,128)S(1)}, f32[8,4,16,128]{3,2,1,0:T(8,128)S(1)}, u32[]{:S(2)}, u32[]{:S(2)}) %collective-permute-start.2) | collective-permute-done | bytes 262176 | tf_op jit(solution)/shard_map/ppermute | solution.py:409
  53.2 2.8 %collective-permute-done.3.after_any = f32[8,4,16,128]{3,2,1,0:T(8,128)S(1)} collective-permute-done((f32[8,4,16,128]{3,2,1,0:T(8,128)S(1)}, f32[8,4,16,128]{3,2,1,0:T(8,128)S(1)}, u32[]{:S(2)}, u32[]{:S(2)}) %collective-permute-start.3) | collective-permute-done | bytes 262176 | tf_op jit(solution)/shard_map/ppermute | solution.py:410
  56.0 2.5 %shard_map.101 = (f32[4,16,16,128]{3,2,1,0:T(8,128)S(1)}, f32[4,16,16,128]{3,2,1,0:T(8,128)S(1)}) custom-call(s32[1]{0:T(128)} %bitcast.at_ref, f32[4,16,16,128]{3,2,1,0:T(8,128)} %fields_any.9, f32[4,16,16,128]{3,2,1,0:T(8,128)} %cot_any.9, f32[8,4,16,128]{3,2,1,0:T(8,128)S(1)} %collective-permute-done.2.before_any, ...), custom_call_target="tpu_custom_call", output_to_operand_aliasing={{0}: (5, {}), {1}: (6, {})} | custom-call | flops 20000000 | bytes 6000000 | tf_op jit(solution)/shard_map/pallas_call | solution.py:411
  58.5 7.8 %all-to-all-done.1.back_ref = f32[16,8,16,128]{3,2,1,0:T(8,128)S(1)} async-done(((f32[16,8,16,128]{3,2,1,0:T(8,128)}), f32[16,8,16,128]{3,2,1,0:T(8,128)S(1)}, u32[]{:S(2)}, u32[]{:S(2)}) %all-to-all-start.1) | async-done | bytes 1048608 | tf_op jit(solution)/shard_map/all_to_all | solution.py:425
  66.3 1.1 %shard_map.102 = (f32[4,16,16,128]{3,2,1,0:T(8,128)}, f32[4,16,16,128]{3,2,1,0:T(8,128)}) custom-call(f32[4,16,16,128]{3,2,1,0:T(8,128)S(1)} %get-tuple-element.26.res_ref, f32[4,16,16,128]{3,2,1,0:T(8,128)S(1)} %get-tuple-element.27.adj_ref, f32[16,8,16,128]{3,2,1,0:T(8,128)S(1)} %all-to-all-done.1.back_ref), custom_call_target="tpu_custom_call" | custom-call | flops 1000000 | bytes 3145728 | tf_op jit(solution)/shard_map/pallas_call | solution.py:47
  (3 shorter events, 0.1 us)
Async XLA Ops:
  2.5 7.3 %collective-permute-start = (f32[8,16,128]{2,1,0:T(8,128)S(1)}, f32[8,16,128]{2,1,0:T(8,128)S(1)}, u32[]{:S(2)}, u32[]{:S(2)}) collective-permute-start(f32[8,16,128]{2,1,0:T(8,128)S(1)} %get-tuple-element.15), channel_id=1, source_target_pairs={{2,3},{3,2},{6,7},{7,6},{10,11},{11,10},{14,15},{15,14},{18,19},{1... | collective-permute-start | bytes 196616 | tf_op jit(solution)/shard_map/ppermute | solution.py:337
  16.4 26.0 %copy-start = (f32[256,256]{1,0:T(8,128)S(1)}, f32[256,256]{1,0:T(8,128)}, u32[]{:S(2)}) copy-start(f32[256,256]{1,0:T(8,128)} %constant.24.clone.second_t_ref) | copy-start | bytes 786436
  16.4 25.9 %copy-start.1 = (f32[256,256]{1,0:T(8,128)S(1)}, f32[256,256]{1,0:T(8,128)}, u32[]{:S(2)}) copy-start(f32[256,256]{1,0:T(8,128)} %constant.23.clone.first_t_ref) | copy-start | bytes 786436
  16.5 25.9 %copy-start.2 = (f32[256,256]{1,0:T(8,128)S(1)}, f32[256,256]{1,0:T(8,128)}, u32[]{:S(2)}) copy-start(f32[256,256]{1,0:T(8,128)} %constant.22.clone.second_ref) | copy-start | bytes 786436
  16.5 25.9 %copy-start.3 = (f32[256,256]{1,0:T(8,128)S(1)}, f32[256,256]{1,0:T(8,128)}, u32[]{:S(2)}) copy-start(f32[256,256]{1,0:T(8,128)} %constant.21.clone.first_ref) | copy-start | bytes 786436
  16.5 25.9 %copy-start.4 = (f32[256,128]{1,0:T(8,128)S(1)}, f32[256,128]{1,0:T(8,128)}, u32[]{:S(2)}) copy-start(f32[256,128]{1,0:T(8,128)} %constant.25.clone.weight_ref) | copy-start | bytes 393220
  45.2 21.0 %all-to-all-start.1 = ((f32[16,8,16,128]{3,2,1,0:T(8,128)}), f32[16,8,16,128]{3,2,1,0:T(8,128)S(1)}, u32[]{:S(2)}, u32[]{:S(2)}) async-start(f32[16,8,16,128]{3,2,1,0:T(8,128)} %shard_map.97._lined), calls=%async_computation.1 | async-start | bytes 2097152 | tf_op jit(solution)/shard_map/all_to_all | solution.py:425
  49.2 0.7 %collective-permute-start.1 = (f32[8,16,128]{2,1,0:T(8,128)S(1)}, f32[8,16,128]{2,1,0:T(8,128)S(1)}, u32[]{:S(2)}, u32[]{:S(2)}) collective-permute-start(f32[8,16,128]{2,1,0:T(8,128)S(1)} %shard_map.98), channel_id=1, source_target_pairs={{0,1},{1,0},{4,5},{5,4},{8,9},{9,8},{12,13},{13,12},{16,17},{17,16... | collective-permute-start | bytes 196616 | tf_op jit(solution)/shard_map/ppermute | solution.py:337
  49.9 3.3 %collective-permute-start.2 = (f32[8,4,16,128]{3,2,1,0:T(8,128)S(1)}, f32[8,4,16,128]{3,2,1,0:T(8,128)S(1)}, u32[]{:S(2)}, u32[]{:S(2)}) collective-permute-start(f32[8,4,16,128]{3,2,1,0:T(8,128)S(1)} %get-tuple-element.20), channel_id=1, source_target_pairs={{0,2},{2,4},{4,6},{6,8},{8,10},{10,12},{12,14},{14,0},{1,3},{3,5},... | collective-permute-start | bytes 786440 | tf_op jit(solution)/shard_map/ppermute | solution.py:409
  49.9 6.1 %collective-permute-start.3 = (f32[8,4,16,128]{3,2,1,0:T(8,128)S(1)}, f32[8,4,16,128]{3,2,1,0:T(8,128)S(1)}, u32[]{:S(2)}, u32[]{:S(2)}) collective-permute-start(f32[8,4,16,128]{3,2,1,0:T(8,128)S(1)} %get-tuple-element.21), channel_id=1, source_target_pairs={{2,0},{4,2},{6,4},{8,6},{10,8},{12,10},{14,12},{0,14},{3,1},{5,3},... | collective-permute-start | bytes 786440 | tf_op jit(solution)/shard_map/ppermute | solution.py:410

commit v7 on v6

--- a/solution.py
+++ b/solution.py
@@ -284,23 +284,21 @@
 
     u = [lines(in_ref, c) for c in range(4)]
     w = [weight * lines(in_ref, 4 + c) for c in range(4)]
-    slope = product(first_ref, u)
-    curve = product(second_ref, u[0:3])
-    for c in range(3):
-        total = u[1] * slope[c] - NU_VALUE * curve[c]
-        if c == 1:
-            total = total + slope[3]
-        send(c, weight * total)
-    send(3, weight * slope[1])
-    stretch = w[0] * slope[0] + w[1] * slope[1] + w[2] * slope[2]
-    lifted = product(first_t_ref, [u[1] * w[0], u[1] * w[1] + w[3], u[1] * w[2], w[1]])
-    send(7, lifted[3])
-    bent = product(second_t_ref, w[0:3])
-    for c in range(3):
-        total = lifted[c] - NU_VALUE * bent[c]
-        if c == 1:
-            total = total + stretch
-        send(4 + c, total)
+    slope_2, slope_1 = product(first_ref, [u[1], u[0]])
+    press, lifted_1 = product(first_t_ref, [w[1], u[1] * w[0]])
+    curve_1, curve_3 = product(second_ref, [u[0], u[2]])
+    send(0, weight * (u[1] * slope_1 - NU_VALUE * curve_1))
+    send(3, weight * slope_2)
+    send(7, press)
+    slope_3, joint = product(first_ref, [u[2], u[3] - NU_VALUE * slope_2])
+    send(1, weight * (u[1] * slope_2 + joint))
+    send(2, weight * (u[1] * slope_3 - NU_VALUE * curve_3))
+    stretch = w[0] * slope_1 + w[1] * slope_2 + w[2] * slope_3
+    bent_1, bent_3 = product(second_t_ref, [w[0], w[2]])
+    send(4, lifted_1 - NU_VALUE * bent_1)
+    lifted_2, lifted_3 = product(first_t_ref, [u[1] * w[1] + w[3] - NU_VALUE * press, u[1] * w[2]])
+    send(5, lifted_2 + stretch)
+    send(6, lifted_3 - NU_VALUE * bent_3)
     for copy in copies:
         copy.wait()
 

time: 67.7 us -> 67.4 us (level)
  no operation moved by 1% of the time
where the time goes in v7:
time: 67.4 us; the launch traced here: 67.1 us
  blocking collectives  25.9 us (38%)
  waiting for transfers between devices  15 us (22%)
  Pallas kernels  14.6 us (22%)
  starting transfers between devices  10.7 us (16%)
  between operations  0.8 us (1%)
    all_to_all x1, blocking collectives, per_device(): gathered = exchange(packed)  25.9 us
    all_to_all x1, waiting for transfers between devices, per_device(): back = exchange(lined)  7.82 us
    pallas_call x1, Pallas kernels, per_device(): pl.pallas_call(functools.partial(early_z_kernel, points), out_shape=[pltp...  6.67 us
    ppermute x2, starting transfers between devices, swap_zed(): lax.ppermute(zed, ('gx', 'gz'), pairs)  6.32 us
    all_to_all x1, starting transfers between devices, per_device(): back = exchange(lined)  3.91 us
    ppermute x1, waiting for transfers between devices, per_device(): after = lax.ppermute(lead, 'gx', [((i + 1) % gx, i) for i in range(gx)])  2.79 us
    ppermute x1, waiting for transfers between devices, per_device(): before = lax.ppermute(last, 'gx', [(i, (i + 1) % gx) for i in range(gx)])  2.78 us
    pallas_call x1, Pallas kernels, per_device(): pl.pallas_call(lines_kernel, out_shape=like(groups, 8, rows, lanes), in_s...  2.5 us
  transfers between devices with their start and end apart: 5, of which 4 were waited for; matrix products, arithmetic and copies ran while one was open for 0% of the time, Pallas kernels for 4%

profile of v7, /device:TPU:1, one launch (start us, length us, event | category | flops | bytes accessed | tf_op | source)
XLA Modules:
  0.0 67.1 jit_solution(17692696284257956979)
XLA Ops:
  0.6 1.8 %shard_map.95 = (f32[16,8,16,128]{3,2,1,0:T(8,128)S(1)}, f32[8,16,128]{2,1,0:T(8,128)S(1)}, f32[8,4,16,128]{3,2,1,0:T(8,128)S(1)}, f32[8,4,16,128]{3,2,1,0:T(8,128)S(1)}) custom-call(s32[1]{0:T(128)} %bitcast.1.core_ref, f32[4,16,16,128]{3,2,1,0:T(8,128)} %fields_any.9, f32[4,16,16,128]{3,2,1,0:T(8,128)} %cot_any.9), custom_call_target="tpu_custom_call" | custom-call | tf_op jit(solution)/shard_map/pallas_call | solution.py:337
  2.5 5.7 %collective-permute-start = (f32[8,16,128]{2,1,0:T(8,128)S(1)}, f32[8,16,128]{2,1,0:T(8,128)S(1)}, u32[]{:S(2)}, u32[]{:S(2)}) collective-permute-start(f32[8,16,128]{2,1,0:T(8,128)S(1)} %get-tuple-element.15), channel_id=1, source_target_pairs={{2,3},{3,2},{6,7},{7,6},{10,11},{11,10},{14,15},{15,14},{18,19},{1... | collective-permute-start | bytes 196616 | tf_op jit(solution)/shard_map/ppermute | solution.py:335
  8.1 1.6 %collective-permute-done.zed_ref = f32[8,16,128]{2,1,0:T(8,128)S(1)} collective-permute-done((f32[8,16,128]{2,1,0:T(8,128)S(1)}, f32[8,16,128]{2,1,0:T(8,128)S(1)}, u32[]{:S(2)}, u32[]{:S(2)}) %collective-permute-start) | collective-permute-done | bytes 65568 | tf_op jit(solution)/shard_map/ppermute | solution.py:335
  9.8 6.7 %shard_map.96 = (f32[16,8,16,128]{3,2,1,0:T(8,128)S(1)}, f32[4,16,16,128]{3,2,1,0:T(8,128)S(1)}, f32[4,16,16,128]{3,2,1,0:T(8,128)S(1)}) custom-call(s32[1]{0:T(128)} %bitcast.1.core_ref, s32[1]{0:T(128)} %bitcast.at_ref, f32[4,16,16,128]{3,2,1,0:T(8,128)} %fields_any.9, f32[3,16,16,128]{3,2,1,0:T(8,128)} %prev_any.3, ...), custom_call_target="tpu_custom_call", output_to_operand_aliasing={{0}: (6, {})} | custom-call | flops 20000000 | bytes 6000000 | tf_op jit(solution)/shard_map/pallas_call | solution.py:355
  16.4 0.0 copy-start
  16.4 0.0 copy-start.1
  16.5 0.0 copy-start.2
  16.5 0.0 copy-start.3
  16.5 0.0 copy-start.4
  16.5 25.9 %all_to_all.10.in_ref = f32[16,8,16,128]{3,2,1,0:T(8,128)S(1)} all-to-all(f32[16,8,16,128]{3,2,1,0:T(8,128)S(1)} %get-tuple-element.17), channel_id=1, replica_groups=mesh['gy'=16,'gx'=8,'gz'=2] {'gy'}, dimensions={0} | all-to-all | bytes 2097152 | tf_op jit(solution)/shard_map/all_to_all | solution.py:365
  42.4 0.0 copy-done
  42.4 0.0 copy-done.1
  42.4 0.0 copy-done.2
  42.4 0.0 copy-done.3
  42.4 0.0 copy-done.4
  42.4 2.5 %shard_map.97._lined = f32[16,8,16,128]{3,2,1,0:T(8,128)} custom-call(f32[256,256]{1,0:T(8,128)S(1)} %copy-done.3, f32[256,256]{1,0:T(8,128)S(1)} %copy-done.2, f32[256,256]{1,0:T(8,128)S(1)} %copy-done.1, f32[256,256]{1,0:T(8,128)S(1)} %copy-done, f32[256,128]{1,0:T(8,128)S(1)} %copy-done.4, f32[16,8,16,128]{3,2,1,0:T(8,128)S(1)} %all_to_all.10.in_ref), custom_call_target="tpu_custom_call" | custom-call | flops 1409286144 | bytes 4000000 | tf_op jit(solution)/shard_map/pallas_call | solution.py:369
  44.9 3.9 %all-to-all-start.1 = ((f32[16,8,16,128]{3,2,1,0:T(8,128)}), f32[16,8,16,128]{3,2,1,0:T(8,128)S(1)}, u32[]{:S(2)}, u32[]{:S(2)}) async-start(f32[16,8,16,128]{3,2,1,0:T(8,128)} %shard_map.97._lined), calls=%async_computation.1 | async-start | bytes 2097152 | tf_op jit(solution)/shard_map/all_to_all | solution.py:423
  48.9 0.7 collective-permute-start.1
  49.6 0.0 collective-permute-done.1._zed.zed_ref
  49.6 0.0 collective-permute-start.2
  49.6 0.5 collective-permute-start.3
  50.1 2.8 %collective-permute-done.2.before_any = f32[8,4,16,128]{3,2,1,0:T(8,128)S(1)} collective-permute-done((f32[8,4,16,128]{3,2,1,0:T(8,128)S(1)}, f32[8,4,16,128]{3,2,1,0:T(8,128)S(1)}, u32[]{:S(2)}, u32[]{:S(2)}) %collective-permute-start.2) | collective-permute-done | bytes 262176 | tf_op jit(solution)/shard_map/ppermute | solution.py:407
  52.9 2.8 %collective-permute-done.3.after_any = f32[8,4,16,128]{3,2,1,0:T(8,128)S(1)} collective-permute-done((f32[8,4,16,128]{3,2,1,0:T(8,128)S(1)}, f32[8,4,16,128]{3,2,1,0:T(8,128)S(1)}, u32[]{:S(2)}, u32[]{:S(2)}) %collective-permute-start.3) | collective-permute-done | bytes 262176 | tf_op jit(solution)/shard_map/ppermute | solution.py:408
  55.7 2.5 %shard_map.101 = (f32[4,16,16,128]{3,2,1,0:T(8,128)S(1)}, f32[4,16,16,128]{3,2,1,0:T(8,128)S(1)}) custom-call(s32[1]{0:T(128)} %bitcast.at_ref, f32[4,16,16,128]{3,2,1,0:T(8,128)} %fields_any.9, f32[4,16,16,128]{3,2,1,0:T(8,128)} %cot_any.9, f32[8,4,16,128]{3,2,1,0:T(8,128)S(1)} %collective-permute-done.2.before_any, ...), custom_call_target="tpu_custom_call", output_to_operand_aliasing={{0}: (5, {}), {1}: (6, {})} | custom-call | flops 20000000 | bytes 6000000 | tf_op jit(solution)/shard_map/pallas_call | solution.py:409
  58.2 7.8 %all-to-all-done.1.back_ref = f32[16,8,16,128]{3,2,1,0:T(8,128)S(1)} async-done(((f32[16,8,16,128]{3,2,1,0:T(8,128)}), f32[16,8,16,128]{3,2,1,0:T(8,128)S(1)}, u32[]{:S(2)}, u32[]{:S(2)}) %all-to-all-start.1) | async-done | bytes 1048608 | tf_op jit(solution)/shard_map/all_to_all | solution.py:423
  66.0 1.1 %shard_map.102 = (f32[4,16,16,128]{3,2,1,0:T(8,128)}, f32[4,16,16,128]{3,2,1,0:T(8,128)}) custom-call(f32[4,16,16,128]{3,2,1,0:T(8,128)S(1)} %get-tuple-element.26.res_ref, f32[4,16,16,128]{3,2,1,0:T(8,128)S(1)} %get-tuple-element.27.adj_ref, f32[16,8,16,128]{3,2,1,0:T(8,128)S(1)} %all-to-all-done.1.back_ref), custom_call_target="tpu_custom_call" | custom-call | flops 1000000 | bytes 3145728 | tf_op jit(solution)/shard_map/pallas_call | solution.py:47
  (3 shorter events, 0.1 us)
Async XLA Ops:
  2.5 7.3 %collective-permute-start = (f32[8,16,128]{2,1,0:T(8,128)S(1)}, f32[8,16,128]{2,1,0:T(8,128)S(1)}, u32[]{:S(2)}, u32[]{:S(2)}) collective-permute-start(f32[8,16,128]{2,1,0:T(8,128)S(1)} %get-tuple-element.15), channel_id=1, source_target_pairs={{2,3},{3,2},{6,7},{7,6},{10,11},{11,10},{14,15},{15,14},{18,19},{1... | collective-permute-start | bytes 196616 | tf_op jit(solution)/shard_map/ppermute | solution.py:335
  16.4 26.0 %copy-start = (f32[256,256]{1,0:T(8,128)S(1)}, f32[256,256]{1,0:T(8,128)}, u32[]{:S(2)}) copy-start(f32[256,256]{1,0:T(8,128)} %constant.24.clone.second_t_ref) | copy-start | bytes 786436
  16.4 26.0 %copy-start.1 = (f32[256,256]{1,0:T(8,128)S(1)}, f32[256,256]{1,0:T(8,128)}, u32[]{:S(2)}) copy-start(f32[256,256]{1,0:T(8,128)} %constant.23.clone.first_t_ref) | copy-start | bytes 786436
  16.5 25.9 %copy-start.2 = (f32[256,256]{1,0:T(8,128)S(1)}, f32[256,256]{1,0:T(8,128)}, u32[]{:S(2)}) copy-start(f32[256,256]{1,0:T(8,128)} %constant.22.clone.second_ref) | copy-start | bytes 786436
  16.5 25.9 %copy-start.3 = (f32[256,256]{1,0:T(8,128)S(1)}, f32[256,256]{1,0:T(8,128)}, u32[]{:S(2)}) copy-start(f32[256,256]{1,0:T(8,128)} %constant.21.clone.first_ref) | copy-start | bytes 786436
  16.5 25.9 %copy-start.4 = (f32[256,128]{1,0:T(8,128)S(1)}, f32[256,128]{1,0:T(8,128)}, u32[]{:S(2)}) copy-start(f32[256,128]{1,0:T(8,128)} %constant.25.clone.weight_ref) | copy-start | bytes 393220
  44.9 21.1 %all-to-all-start.1 = ((f32[16,8,16,128]{3,2,1,0:T(8,128)}), f32[16,8,16,128]{3,2,1,0:T(8,128)S(1)}, u32[]{:S(2)}, u32[]{:S(2)}) async-start(f32[16,8,16,128]{3,2,1,0:T(8,128)} %shard_map.97._lined), calls=%async_computation.1 | async-start | bytes 2097152 | tf_op jit(solution)/shard_map/all_to_all | solution.py:423
  48.9 0.7 %collective-permute-start.1 = (f32[8,16,128]{2,1,0:T(8,128)S(1)}, f32[8,16,128]{2,1,0:T(8,128)S(1)}, u32[]{:S(2)}, u32[]{:S(2)}) collective-permute-start(f32[8,16,128]{2,1,0:T(8,128)S(1)} %shard_map.98), channel_id=1, source_target_pairs={{0,1},{1,0},{4,5},{5,4},{8,9},{9,8},{12,13},{13,12},{16,17},{17,16... | collective-permute-start | bytes 196616 | tf_op jit(solution)/shard_map/ppermute | solution.py:335
  49.6 3.3 %collective-permute-start.2 = (f32[8,4,16,128]{3,2,1,0:T(8,128)S(1)}, f32[8,4,16,128]{3,2,1,0:T(8,128)S(1)}, u32[]{:S(2)}, u32[]{:S(2)}) collective-permute-start(f32[8,4,16,128]{3,2,1,0:T(8,128)S(1)} %get-tuple-element.20), channel_id=1, source_target_pairs={{0,2},{2,4},{4,6},{6,8},{8,10},{10,12},{12,14},{14,0},{1,3},{3,5},... | collective-permute-start | bytes 786440 | tf_op jit(solution)/shard_map/ppermute | solution.py:407
  49.6 6.1 %collective-permute-start.3 = (f32[8,4,16,128]{3,2,1,0:T(8,128)S(1)}, f32[8,4,16,128]{3,2,1,0:T(8,128)S(1)}, u32[]{:S(2)}, u32[]{:S(2)}) collective-permute-start(f32[8,4,16,128]{3,2,1,0:T(8,128)S(1)} %get-tuple-element.21), channel_id=1, source_target_pairs={{2,0},{4,2},{6,4},{8,6},{10,8},{12,10},{14,12},{0,14},{3,1},{5,3},... | collective-permute-start | bytes 786440 | tf_op jit(solution)/shard_map/ppermute | solution.py:408

commit v8 on v7

--- a/solution.py
+++ b/solution.py
@@ -40,17 +40,6 @@
     j = np.arange(points)
     weight = np.sin(j * (math.pi / final_row)) ** 4
     return np.repeat(weight[:, None], 128, 1).astype(np.float32)
-
-
-def call(kernel, outs, args, flops, scratch=()):
-    moved = sum(4 * math.prod(a.shape) for a in (*outs, *args))
-    return pl.pallas_call(
-        kernel,
-        out_shape=outs,
-        scratch_shapes=list(scratch),
-        cost_estimate=pl.CostEstimate(flops=flops, bytes_accessed=moved, transcendentals=0),
-        compiler_params=pltpu.CompilerParams(vmem_limit_bytes=VMEM_BYTES),
-    )(*args)
 
 
 def like(*shape):
@@ -303,10 +292,15 @@
         copy.wait()
 
 
-def add_kernel(res_ref, adj_ref, back_ref, res_out, adj_out):
-    for c in range(4):
-        res_out[c] = res_ref[c] + back_ref[:, c]
-        adj_out[c] = adj_ref[c] + back_ref[:, 4 + c]
+def add_kernel(res_ref, adj_ref, back_ref, res_out, adj_out, held, sems):
+    copies = []
+    for c in range(8):
+        part, out = (res_ref, res_out) if c < 4 else (adj_ref, adj_out)
+        held[c] = part[c % 4] + back_ref[:, c]
+        copies.append(pltpu.make_async_copy(held.at[c], out.at[c % 4], sems.at[c]))
+        copies[-1].start()
+    for copy in copies:
+        copy.wait()
 
 
 def per_device(fields, previous, cotangent):
@@ -422,7 +416,14 @@
 
     back = exchange(lined)
     block = like(4, cells, rows, lanes)
-    residual, adjoint = call(add_kernel, [block, block], [res, adj, back], 10**6)
+    residual, adjoint = pl.pallas_call(
+        add_kernel,
+        out_shape=[block, block],
+        in_specs=[near] * 3,
+        out_specs=[far] * 2,
+        scratch_shapes=[pltpu.VMEM((8, cells) + plane, f32), pltpu.SemaphoreType.DMA((8,))],
+        compiler_params=pltpu.CompilerParams(vmem_limit_bytes=VMEM_BYTES),
+    )(res, adj, back)
     return residual, adjoint
 
 

time: 67.4 us -> 67.4 us (level)
  no operation moved by 1% of the time
where the time goes in v8:
time: 67.4 us; the launch traced here: 67 us
  blocking collectives  25.9 us (38%)
  waiting for transfers between devices  15 us (22%)
  Pallas kernels  14.5 us (22%)
  starting transfers between devices  10.7 us (16%)
  between operations  0.8 us (1%)
    all_to_all x1, blocking collectives, per_device(): gathered = exchange(packed)  25.9 us
    all_to_all x1, waiting for transfers between devices, per_device(): back = exchange(lined)  7.82 us
    pallas_call x1, Pallas kernels, per_device(): pl.pallas_call(functools.partial(early_z_kernel, points), out_shape=[pltp...  6.67 us
    ppermute x2, starting transfers between devices, swap_zed(): lax.ppermute(zed, ('gx', 'gz'), pairs)  6.32 us
    all_to_all x1, starting transfers between devices, per_device(): back = exchange(lined)  3.91 us
    ppermute x1, waiting for transfers between devices, per_device(): after = lax.ppermute(lead, 'gx', [((i + 1) % gx, i) for i in range(gx)])  2.79 us
    ppermute x1, waiting for transfers between devices, per_device(): before = lax.ppermute(last, 'gx', [(i, (i + 1) % gx) for i in range(gx)])  2.78 us
    pallas_call x1, Pallas kernels, per_device(): pl.pallas_call(lines_kernel, out_shape=like(groups, 8, rows, lanes), in_s...  2.5 us
  transfers between devices with their start and end apart: 5, of which 4 were waited for; matrix products, arithmetic and copies ran while one was open for 0% of the time, Pallas kernels for 4%

profile of v8, /device:TPU:1, one launch (start us, length us, event | category | flops | bytes accessed | tf_op | source)
XLA Modules:
  0.0 67.0 jit_solution(9258339495214266534)
XLA Ops:
  0.6 1.8 %shard_map.95 = (f32[16,8,16,128]{3,2,1,0:T(8,128)S(1)}, f32[8,16,128]{2,1,0:T(8,128)S(1)}, f32[8,4,16,128]{3,2,1,0:T(8,128)S(1)}, f32[8,4,16,128]{3,2,1,0:T(8,128)S(1)}) custom-call(s32[1]{0:T(128)} %bitcast.1.core_ref, f32[4,16,16,128]{3,2,1,0:T(8,128)} %fields_any.9, f32[4,16,16,128]{3,2,1,0:T(8,128)} %cot_any.9), custom_call_target="tpu_custom_call" | custom-call | tf_op jit(solution)/shard_map/pallas_call | solution.py:331
  2.5 5.7 %collective-permute-start = (f32[8,16,128]{2,1,0:T(8,128)S(1)}, f32[8,16,128]{2,1,0:T(8,128)S(1)}, u32[]{:S(2)}, u32[]{:S(2)}) collective-permute-start(f32[8,16,128]{2,1,0:T(8,128)S(1)} %get-tuple-element.15), channel_id=1, source_target_pairs={{2,3},{3,2},{6,7},{7,6},{10,11},{11,10},{14,15},{15,14},{18,19},{1... | collective-permute-start | bytes 196616 | tf_op jit(solution)/shard_map/ppermute | solution.py:329
  8.1 1.6 %collective-permute-done.zed_ref = f32[8,16,128]{2,1,0:T(8,128)S(1)} collective-permute-done((f32[8,16,128]{2,1,0:T(8,128)S(1)}, f32[8,16,128]{2,1,0:T(8,128)S(1)}, u32[]{:S(2)}, u32[]{:S(2)}) %collective-permute-start) | collective-permute-done | bytes 65568 | tf_op jit(solution)/shard_map/ppermute | solution.py:329
  9.8 6.7 %shard_map.96 = (f32[16,8,16,128]{3,2,1,0:T(8,128)S(1)}, f32[4,16,16,128]{3,2,1,0:T(8,128)S(1)}, f32[4,16,16,128]{3,2,1,0:T(8,128)S(1)}) custom-call(s32[1]{0:T(128)} %bitcast.1.core_ref, s32[1]{0:T(128)} %bitcast.at_ref, f32[4,16,16,128]{3,2,1,0:T(8,128)} %fields_any.9, f32[3,16,16,128]{3,2,1,0:T(8,128)} %prev_any.3, ...), custom_call_target="tpu_custom_call", output_to_operand_aliasing={{0}: (6, {})} | custom-call | flops 20000000 | bytes 6000000 | tf_op jit(solution)/shard_map/pallas_call | solution.py:349
  16.4 0.0 copy-start
  16.4 0.0 copy-start.1
  16.5 0.0 copy-start.2
  16.5 0.0 copy-start.3
  16.5 0.0 copy-start.4
  16.5 25.9 %all_to_all.10.in_ref = f32[16,8,16,128]{3,2,1,0:T(8,128)S(1)} all-to-all(f32[16,8,16,128]{3,2,1,0:T(8,128)S(1)} %get-tuple-element.17), channel_id=1, replica_groups=mesh['gy'=16,'gx'=8,'gz'=2] {'gy'}, dimensions={0} | all-to-all | bytes 2097152 | tf_op jit(solution)/shard_map/all_to_all | solution.py:359
  42.4 0.0 copy-done
  42.4 0.0 copy-done.1
  42.4 0.0 copy-done.2
  42.4 0.0 copy-done.3
  42.4 0.0 copy-done.4
  42.4 2.5 %shard_map.97._lined = f32[16,8,16,128]{3,2,1,0:T(8,128)} custom-call(f32[256,256]{1,0:T(8,128)S(1)} %copy-done.3, f32[256,256]{1,0:T(8,128)S(1)} %copy-done.2, f32[256,256]{1,0:T(8,128)S(1)} %copy-done.1, f32[256,256]{1,0:T(8,128)S(1)} %copy-done, f32[256,128]{1,0:T(8,128)S(1)} %copy-done.4, f32[16,8,16,128]{3,2,1,0:T(8,128)S(1)} %all_to_all.10.in_ref), custom_call_target="tpu_custom_call" | custom-call | flops 1409286144 | bytes 4000000 | tf_op jit(solution)/shard_map/pallas_call | solution.py:363
  44.9 3.9 %all-to-all-start.1 = ((f32[16,8,16,128]{3,2,1,0:T(8,128)}), f32[16,8,16,128]{3,2,1,0:T(8,128)S(1)}, u32[]{:S(2)}, u32[]{:S(2)}) async-start(f32[16,8,16,128]{3,2,1,0:T(8,128)} %shard_map.97._lined), calls=%async_computation.1 | async-start | bytes 2097152 | tf_op jit(solution)/shard_map/all_to_all | solution.py:417
  48.9 0.7 collective-permute-start.1
  49.6 0.0 collective-permute-done.1._zed.zed_ref
  49.6 0.0 collective-permute-start.2
  49.6 0.5 collective-permute-start.3
  50.1 2.8 %collective-permute-done.2.before_any = f32[8,4,16,128]{3,2,1,0:T(8,128)S(1)} collective-permute-done((f32[8,4,16,128]{3,2,1,0:T(8,128)S(1)}, f32[8,4,16,128]{3,2,1,0:T(8,128)S(1)}, u32[]{:S(2)}, u32[]{:S(2)}) %collective-permute-start.2) | collective-permute-done | bytes 262176 | tf_op jit(solution)/shard_map/ppermute | solution.py:401
  52.9 2.8 %collective-permute-done.3.after_any = f32[8,4,16,128]{3,2,1,0:T(8,128)S(1)} collective-permute-done((f32[8,4,16,128]{3,2,1,0:T(8,128)S(1)}, f32[8,4,16,128]{3,2,1,0:T(8,128)S(1)}, u32[]{:S(2)}, u32[]{:S(2)}) %collective-permute-start.3) | collective-permute-done | bytes 262176 | tf_op jit(solution)/shard_map/ppermute | solution.py:402
  55.7 2.5 %shard_map.101 = (f32[4,16,16,128]{3,2,1,0:T(8,128)S(1)}, f32[4,16,16,128]{3,2,1,0:T(8,128)S(1)}) custom-call(s32[1]{0:T(128)} %bitcast.at_ref, f32[4,16,16,128]{3,2,1,0:T(8,128)} %fields_any.9, f32[4,16,16,128]{3,2,1,0:T(8,128)} %cot_any.9, f32[8,4,16,128]{3,2,1,0:T(8,128)S(1)} %collective-permute-done.2.before_any, ...), custom_call_target="tpu_custom_call", output_to_operand_aliasing={{0}: (5, {}), {1}: (6, {})} | custom-call | flops 20000000 | bytes 6000000 | tf_op jit(solution)/shard_map/pallas_call | solution.py:403
  58.2 7.8 %all-to-all-done.1.back_ref = f32[16,8,16,128]{3,2,1,0:T(8,128)S(1)} async-done(((f32[16,8,16,128]{3,2,1,0:T(8,128)}), f32[16,8,16,128]{3,2,1,0:T(8,128)S(1)}, u32[]{:S(2)}, u32[]{:S(2)}) %all-to-all-start.1) | async-done | bytes 1048608 | tf_op jit(solution)/shard_map/all_to_all | solution.py:417
  66.0 1.0 %shard_map.102 = (f32[4,16,16,128]{3,2,1,0:T(8,128)}, f32[4,16,16,128]{3,2,1,0:T(8,128)}) custom-call(f32[4,16,16,128]{3,2,1,0:T(8,128)S(1)} %get-tuple-element.26.res_ref, f32[4,16,16,128]{3,2,1,0:T(8,128)S(1)} %get-tuple-element.27.adj_ref, f32[16,8,16,128]{3,2,1,0:T(8,128)S(1)} %all-to-all-done.1.back_ref), custom_call_target="tpu_custom_call" | custom-call | tf_op jit(solution)/shard_map/pallas_call | solution.py:419
  (3 shorter events, 0.1 us)
Async XLA Ops:
  2.5 7.3 %collective-permute-start = (f32[8,16,128]{2,1,0:T(8,128)S(1)}, f32[8,16,128]{2,1,0:T(8,128)S(1)}, u32[]{:S(2)}, u32[]{:S(2)}) collective-permute-start(f32[8,16,128]{2,1,0:T(8,128)S(1)} %get-tuple-element.15), channel_id=1, source_target_pairs={{2,3},{3,2},{6,7},{7,6},{10,11},{11,10},{14,15},{15,14},{18,19},{1... | collective-permute-start | bytes 196616 | tf_op jit(solution)/shard_map/ppermute | solution.py:329
  16.4 26.0 %copy-start = (f32[256,256]{1,0:T(8,128)S(1)}, f32[256,256]{1,0:T(8,128)}, u32[]{:S(2)}) copy-start(f32[256,256]{1,0:T(8,128)} %constant.24.clone.second_t_ref) | copy-start | bytes 786436
  16.4 26.0 %copy-start.1 = (f32[256,256]{1,0:T(8,128)S(1)}, f32[256,256]{1,0:T(8,128)}, u32[]{:S(2)}) copy-start(f32[256,256]{1,0:T(8,128)} %constant.23.clone.first_t_ref) | copy-start | bytes 786436
  16.5 25.9 %copy-start.2 = (f32[256,256]{1,0:T(8,128)S(1)}, f32[256,256]{1,0:T(8,128)}, u32[]{:S(2)}) copy-start(f32[256,256]{1,0:T(8,128)} %constant.22.clone.second_ref) | copy-start | bytes 786436
  16.5 25.9 %copy-start.3 = (f32[256,256]{1,0:T(8,128)S(1)}, f32[256,256]{1,0:T(8,128)}, u32[]{:S(2)}) copy-start(f32[256,256]{1,0:T(8,128)} %constant.21.clone.first_ref) | copy-start | bytes 786436
  16.5 25.9 %copy-start.4 = (f32[256,128]{1,0:T(8,128)S(1)}, f32[256,128]{1,0:T(8,128)}, u32[]{:S(2)}) copy-start(f32[256,128]{1,0:T(8,128)} %constant.25.clone.weight_ref) | copy-start | bytes 393220
  44.9 21.1 %all-to-all-start.1 = ((f32[16,8,16,128]{3,2,1,0:T(8,128)}), f32[16,8,16,128]{3,2,1,0:T(8,128)S(1)}, u32[]{:S(2)}, u32[]{:S(2)}) async-start(f32[16,8,16,128]{3,2,1,0:T(8,128)} %shard_map.97._lined), calls=%async_computation.1 | async-start | bytes 2097152 | tf_op jit(solution)/shard_map/all_to_all | solution.py:417
  48.9 0.7 %collective-permute-start.1 = (f32[8,16,128]{2,1,0:T(8,128)S(1)}, f32[8,16,128]{2,1,0:T(8,128)S(1)}, u32[]{:S(2)}, u32[]{:S(2)}) collective-permute-start(f32[8,16,128]{2,1,0:T(8,128)S(1)} %shard_map.98), channel_id=1, source_target_pairs={{0,1},{1,0},{4,5},{5,4},{8,9},{9,8},{12,13},{13,12},{16,17},{17,16... | collective-permute-start | bytes 196616 | tf_op jit(solution)/shard_map/ppermute | solution.py:329
  49.6 3.3 %collective-permute-start.2 = (f32[8,4,16,128]{3,2,1,0:T(8,128)S(1)}, f32[8,4,16,128]{3,2,1,0:T(8,128)S(1)}, u32[]{:S(2)}, u32[]{:S(2)}) collective-permute-start(f32[8,4,16,128]{3,2,1,0:T(8,128)S(1)} %get-tuple-element.20), channel_id=1, source_target_pairs={{0,2},{2,4},{4,6},{6,8},{8,10},{10,12},{12,14},{14,0},{1,3},{3,5},... | collective-permute-start | bytes 786440 | tf_op jit(solution)/shard_map/ppermute | solution.py:401
  49.6 6.1 %collective-permute-start.3 = (f32[8,4,16,128]{3,2,1,0:T(8,128)S(1)}, f32[8,4,16,128]{3,2,1,0:T(8,128)S(1)}, u32[]{:S(2)}, u32[]{:S(2)}) collective-permute-start(f32[8,4,16,128]{3,2,1,0:T(8,128)S(1)} %get-tuple-element.21), channel_id=1, source_target_pairs={{2,0},{4,2},{6,4},{8,6},{10,8},{12,10},{14,12},{0,14},{3,1},{5,3},... | collective-permute-start | bytes 786440 | tf_op jit(solution)/shard_map/ppermute | solution.py:402
